TPU v7x, 128 devices: a whole 4x4x4 slice. The times are simulated.
128 devices in a mesh: pts: 32 (over z_hi, x, y), lm: 4 (over z_lo, core).
Axes of the slice: x: 4, y: 4, z: 4 (z_hi: 2, z_lo: 2; z = z_hi * 2 + z_lo), core: 2. Of those that a mesh axis runs over, the one named last changes fastest.
Arguments:
- kernel_features: float32 [32768, 2048], P('pts', 'lm'), may hold values from -6 to 6
- factor: float32 [2048, 2048], P(None, 'lm'), may hold values from -0.125 to 0.125
- diag_inverse: float32 [4, 512, 512], P('lm'), as said below
- block_order: int32 [16], replicated, may hold values from 0 to 15, each once
Outputs:
- gram: float32 [2048, 2048], P('pts', 'lm')
Inputs may be any that keep to these rules, and one draw needn't show every extreme that they name: `block_order`: a permutation of the 16 cluster blocks. `diag_inverse`: each block is upper triangular.
All inputs are finite; a program needn't handle non-finite values.
Results may differ from a plain program's by a relative error of at most 0.0001.
Values sent between devices are 32-bit elements; how exact they have to be, the bound alone decides.
No kernel may reach another device: no remote copies, remote signals or barrier semaphores. Data moves between devices by JAX's collectives and lax.ppermute only.
A program may use at most 128 MiB of HBM per device.

v0:
```python
import jax
import jax.numpy as jnp
from jax import lax
from jax.sharding import PartitionSpec as P

CLUSTER = 128


def broadcast(value, axis, root):
    mine = lax.axis_index(axis) == root
    return lax.psum(jnp.where(mine, value, jnp.zeros_like(value)), axis)


def per_device(kernel_features, factor, diag_inverse, block_order):
    precise = lax.Precision.HIGHEST
    rows = kernel_features.shape[0]
    panel = kernel_features.shape[1]
    lm_size = lax.axis_size("lm")
    lm_index = lax.axis_index("lm")
    blocks_here = panel // CLUSTER
    targets = lax.dynamic_slice_in_dim(block_order, lm_index * blocks_here, blocks_here)
    sources = (targets[:, None] * CLUSTER + jnp.arange(CLUSTER, dtype=jnp.int32)[None, :]).reshape(
        -1
    )
    piece = lax.all_gather(kernel_features, "lm", axis=1, tiled=True)
    width = piece.shape[1]
    inside = (sources >= 0) & (sources < width)
    taken = jnp.take(piece, jnp.clip(sources, 0, width - 1), axis=1)
    ordered = jnp.where(inside[None, :], taken, 0.0)
    inverse = diag_inverse[0]
    running = ordered
    mine = jnp.zeros((rows, panel), jnp.float32)
    received = []
    for step in range(lm_size):
        solved = jnp.dot(running, inverse, precision=precise)
        mine = jnp.where(lm_index == step, solved, mine)
        if step + 1 < lm_size:
            arrived = broadcast(solved, "lm", step)
            received.append(arrived)
            coupling = factor[step * panel : (step + 1) * panel]
            running = jnp.where(
                step < lm_index, running - jnp.dot(arrived, coupling, precision=precise), running
            )
    blocks = []
    zeros_block = jnp.zeros((rows, panel), jnp.float32)
    for step in range(lm_size):
        if step + 1 < lm_size:
            earlier = jnp.where(step < lm_index, received[step], zeros_block)
        else:
            earlier = zeros_block
        blocks.append(jnp.where(lm_index == step, mine, earlier))
    whole = jnp.concatenate(blocks, axis=1)
    pts_size = lax.axis_size("pts")
    out_rows = whole.shape[1] // pts_size
    total_points = float(rows * pts_size)
    term = lax.dot_general(whole, mine, (((0,), (0,)), ((), ())), precision=precise)
    summed = lax.psum(term, "pts")
    gram_part = lax.dynamic_slice_in_dim(summed, lax.axis_index("pts") * out_rows, out_rows, 0)
    return gram_part / total_points


def solution(mesh):
    placed = (P("pts", "lm"), P(None, "lm"), P("lm", None, None), P())
    return jax.shard_map(
        per_device, mesh=mesh, in_specs=placed, out_specs=P("pts", "lm"), check_vma=False
    )
```

profile of v0, /device:TPU:0, one launch (start us, length us, event | category | flops | bytes accessed | tf_op | source)
XLA Modules:
  0.0 705.2 jit_solution(3815630753032214253)
XLA Ops:
  6.5 0.0 copy-start
  6.5 0.0 all-gather.2.cloned.1.call-start
  6.5 3.0 copy.5
  9.6 0.0 copy-start.6
  9.6 0.0 all-gather.2.cloned.1.call-update
  9.6 0.0 all-reduce.5.cloned.1.call-start
  9.6 0.6 copy-done.6
  10.2 0.1 dynamic-slice_multiply_fusion.1
  10.3 0.1 fusion.26
  10.4 0.1 compare_and_fusion
  10.5 0.1 fusion.30
  10.5 81.9 %all-gather.2.cloned.1.call-done = f32[1024,2048]{0,1:T(8,128)} async-done(((f32[1024,512]{0,1:T(8,128)}), f32[1024,2048]{0,1:T(8,128)}) %all-gather.2.cloned.1.call-update) | async-done | bytes 8388624 | tf_op jit(solution)/shard_map/all_gather | solution.py:25
  92.5 6.2 gather_fusion
  98.7 0.0 copy-done
  98.7 5.2 fusion.10
  103.8 0.0 all-reduce.5.cloned.1.call-update
  103.9 0.0 all-reduce.7.cloned.1.call-start
  103.9 59.7 %all-reduce.5.cloned.1.call-done = f32[1024,512]{0,1:T(8,128)} async-done(((f32[1024,512]{0,1:T(8,128)}), f32[1024,512]{0,1:T(8,128)}) %all-reduce.5.cloned.1.call-update) | async-done | bytes 2097168 | tf_op jit(solution)/shard_map/psum | solution.py:11
  163.7 5.6 subtract_select_fusion.2
  169.3 0.0 copy-start.2
  169.3 5.2 broadcast_select_fusion.1
  174.4 0.0 copy-done.2
  174.4 0.0 copy-start.3
  174.4 0.0 all-reduce.7.cloned.1.call-update
  174.5 0.2 all-reduce.9.cloned.1.call-start
  174.7 58.4 %all-reduce.7.cloned.1.call-done = f32[1024,512]{0,1:T(8,128)} async-done(((f32[1024,512]{0,1:T(8,128)}), f32[1024,512]{0,1:T(8,128)}) %all-reduce.7.cloned.1.call-update) | async-done | bytes 2097168 | tf_op jit(solution)/shard_map/psum | solution.py:11
  233.1 0.0 copy-done.3
  233.1 5.5 subtract_select_fusion.1
  238.6 0.0 copy-start.4
  238.6 5.2 broadcast_select_fusion
  243.8 0.0 copy-done.4
  243.8 0.0 all-reduce.9.cloned.1.call-update
  243.8 0.0 all-reduce.11.cloned.1.call-start
  243.9 0.0 copy-start.1
  243.9 58.6 %all-reduce.9.cloned.1.call-done = f32[1024,512]{0,1:T(8,128)} async-done(((f32[1024,512]{0,1:T(8,128)}), f32[1024,512]{0,1:T(8,128)}) %all-reduce.9.cloned.1.call-update) | async-done | bytes 2097168 | tf_op jit(solution)/shard_map/psum | solution.py:11
  302.5 0.0 copy-start.5
  302.5 5.5 fusion.19
  308.0 0.0 copy-done.1
  308.0 0.0 copy-done.5
  308.0 5.2 select_select_fusion.3
  313.3 16.6 %fusion = f32[2048,512]{1,0:T(8,128)} fusion(f32[1024,512]{0,1:T(8,128)S(1)} %get-tuple-element.13, f32[1024,512]{0,1:T(8,128)S(1)} %get-tuple-element.6, f32[1024,512]{0,1:T(8,128)S(1)} %get-tuple-element.7, f32[1024,512]{0,1:T(8,128)S(1)} %get-tuple-element.8, f32[1024,512]{0,1:T(8,128)S(1)} %get-tuple-element.5), kind=kOutput, calls=%fused_computation.1 | convolution fusion | flops 12891193344 | bytes 14680064 | tf_op jit(solution)/shard_map/dot_general | solution.py:56
  329.9 0.0 all-reduce.11.cloned.1.call-update
  330.0 367.2 %all-reduce.11.cloned.1.call-done = f32[2048,512]{1,0:T(8,128)} async-done(((f32[2048,512]{1,0:T(8,128)}), f32[2048,512]{1,0:T(8,128)}) %all-reduce.11.cloned.1.call-update) | async-done | bytes 4194320 | tf_op jit(solution)/shard_map/psum | solution.py:57
  697.1 1.6 dynamic-slice_multiply_fusion
  (2 shorter events, 0.0 us)
Async XLA Ops:
  6.5 92.1 %copy-start = (f32[1,512,512]{2,1,0:T(8,128)S(1)}, f32[1,512,512]{2,1,0:T(8,128)}, u32[]{:S(2)}) copy-start(f32[1,512,512]{2,1,0:T(8,128)} %param.6) | copy-start | bytes 3145732
  6.5 85.9 %all-gather.2.cloned.1.call-start = ((), (), s32[]{:S(2)}) async-start(), calls=%async_computation | async-start | bytes 10485760 | tf_op jit(solution)/shard_map/all_gather | solution.py:25
  9.6 0.7 copy-start.6
  9.6 154.1 %all-reduce.5.cloned.1.call-start = ((), (), s32[]{:S(2)}) async-start(), calls=%async_computation.1 | async-start | bytes 4194304 | tf_op jit(solution)/shard_map/psum | solution.py:11
  103.9 129.3 %all-reduce.7.cloned.1.call-start = ((), (), s32[]{:S(2)}) async-start(), calls=%async_computation.2 | async-start | bytes 4194304 | tf_op jit(solution)/shard_map/psum | solution.py:11
  169.3 5.2 copy-start.2
  174.4 58.7 %copy-start.3 = (f32[1024,512]{0,1:T(8,128)S(1)}, f32[1024,512]{0,1:T(8,128)}, u32[]{:S(2)}) copy-start(f32[1024,512]{0,1:T(8,128)} %copy-done.2) | copy-start | bytes 6291460
  174.5 128.0 %all-reduce.9.cloned.1.call-start = ((), (), s32[]{:S(2)}) async-start(), calls=%async_computation.3 | async-start | bytes 4194304 | tf_op jit(solution)/shard_map/psum | solution.py:11
  238.6 5.2 copy-start.4
  243.8 453.3 %all-reduce.11.cloned.1.call-start = ((), (), s32[]{:S(2)}) async-start(), calls=%async_computation.4 | async-start | bytes 8388608 | tf_op jit(solution)/shard_map/psum | solution.py:57
  243.9 64.1 %copy-start.1 = (f32[1024,512]{0,1:T(8,128)S(1)}, f32[1024,512]{0,1:T(8,128)}, u32[]{:S(2)}) copy-start(f32[1024,512]{0,1:T(8,128)} %fusion.10) | copy-start | bytes 6291460
  302.5 5.6 copy-start.5
Sparse Core Ops, SparseCore 0:
  9.7 82.7 all-gather.1
  104.0 59.6 all-reduce.4
  174.6 58.5 all-reduce.6
  243.9 58.4 all-reduce.8
  330.1 367.0 all-reduce.10
where the time goes:
time: 705 us
  waiting for transfers between devices  626 us (89%)
  matrix products  54 us (8%)
  between operations  13.3 us (2%)
  local copies, waits for them, and re-layouts  9.81 us (1%)
    psum x1, waiting for transfers between devices, per_device(): summed = lax.psum(term, 'pts')  367 us
    psum x3, waiting for transfers between devices, broadcast(): return lax.psum(jnp.where(mine, value, jnp.zeros_like(value)), axis)  177 us
    all_gather x1, waiting for transfers between devices, per_device(): piece = lax.all_gather(kernel_features, 'lm', axis=1, tiled=True)  81.9 us
    dot_general x4, matrix products, per_device(): solved = jnp.dot(running, inverse, precision=precise)  20.7 us
    dot_general x1, matrix products, per_device(): lax.dot_general(whole, mine, (((0,), (0,)), ((), ())), precision=precise)  16.6 us
    dot_general x3, matrix products, per_device(): jnp.dot(arrived, coupling, precision=precise)  16.6 us
  transfers between devices with their start and end apart: 5, of which 5 were waited for; matrix products, arithmetic and copies ran while one was open for 0% of the time, Pallas kernels for 0%

commit v1 on v0

v1 whole, which is shorter than its diff:
```python
import jax
import jax.numpy as jnp
from jax import lax
from jax.sharding import PartitionSpec as P

PANEL = 512
CLUSTER = 128
ROWS = 64
HIGH = lax.Precision.HIGH

CELLS = [(zh, x, y) for zh in range(2) for x in range(4) for y in range(4)]


def pts_index(zh, x, y):
    return (zh * 4 + x) * 4 + y


def along_x(step):
    return [(pts_index(z, x, y), pts_index(z, (x + step) % 4, y)) for z, x, y in CELLS]


def along_y(step):
    return [(pts_index(z, x, y), pts_index(z, x, (y + step) % 4)) for z, x, y in CELLS]


OTHER_HIGH = [(pts_index(z, x, y), pts_index(1 - z, x, y)) for z, x, y in CELLS]
OTHER_CHIP = [(k, k ^ 2) for k in range(4)]
OTHER_CORE = [(k, k ^ 1) for k in range(4)]


def flip(k):
    return [
        ((8 * a + b) * 4 + j, (8 * j + (b ^ k)) * 4 + a)
        for a in range(4)
        for b in range(8)
        for j in range(4)
    ]


def mm(a, b):
    return jnp.dot(a, b, precision=HIGH)


def tmm(a, b):
    return lax.dot_general(a, b, (((0,), (0,)), ((), ())), precision=HIGH)


def index_of(stack, k):
    return lax.dynamic_index_in_dim(stack, k, 0, keepdims=False)


def scatter_plane(first, second, x, y):
    a, b = index_of(first, x), lax.dynamic_index_in_dim(second, y, 1, keepdims=False)
    for step in (1, 3, 2):
        a += lax.ppermute(index_of(first, (x + step) % 4), "pts", along_x(step))
        b += lax.ppermute(
            lax.dynamic_index_in_dim(second, (y + step) % 4, 1, keepdims=False), "pts", along_y(step)
        )
    c, d = index_of(a, y), index_of(b, x)
    for step in (1, 3, 2):
        c += lax.ppermute(index_of(a, (y + step) % 4), "pts", along_y(step))
        d += lax.ppermute(index_of(b, (x + step) % 4), "pts", along_x(step))
    return c, d


def per_device(kernel_features, factor, diag_inverse, block_order):
    own = kernel_features
    points, panel = own.shape
    half = points // 2
    total = points * lax.axis_size("pts")
    i, j = lax.axis_index("pts"), lax.axis_index("lm")
    chip, core = j // 2, j % 2
    high, x, y = i // 16, (i // 4) % 4, i % 4
    group, member = i // 8, i % 8
    first_core, first_chip = core == 0, chip == 0

    sent = lax.dynamic_slice_in_dim(own, (1 - chip) * half, half)
    across = lax.ppermute(sent, "lm", OTHER_CHIP)
    pair = lax.ppermute(own, "lm", OTHER_CORE)

    inverse = diag_inverse[0]
    pair_inverse = lax.ppermute(inverse, "lm", OTHER_CORE)
    above = factor[: 2 * panel]
    pair_above = lax.ppermute(above, "lm", OTHER_CORE)
    link = lax.dynamic_slice_in_dim(factor, chip * 2 * panel, panel)
    corner = -mm(pair_inverse, mm(link, inverse))
    local = jnp.where(
        first_core,
        jnp.concatenate([inverse, jnp.zeros_like(inverse)], 0),
        jnp.concatenate([corner, inverse], 0),
    )
    far = mm(above, inverse) + jnp.where(first_core, 0.0, mm(pair_above, corner))

    diagonal = tmm(own, own) * 0.5
    beside = tmm(
        jnp.where(first_core, own, pair),
        jnp.where(first_core, pair[:, : panel // 2], own[:, panel // 2 :]),
    )
    own_half = lax.dynamic_slice_in_dim(own, chip * half, half)
    pair_half = lax.dynamic_slice_in_dim(pair, chip * half, half)
    cross_own = tmm(jnp.where(first_chip, own_half, across), jnp.where(first_chip, across, own_half))
    cross_pair = tmm(
        jnp.where(first_chip, pair_half, across), jnp.where(first_chip, across, pair_half)
    )

    def plane(a):
        return a.reshape(4, 4, panel // 16, a.shape[1])

    diagonal, beside, cross_own, cross_pair = map(plane, (diagonal, beside, cross_own, cross_pair))
    cut = 384
    d1, d2 = scatter_plane(
        diagonal[..., :cut], jnp.concatenate([diagonal[..., cut:], beside], -1), x, y
    )
    c1, c2 = scatter_plane(cross_own, cross_pair, x, y)
    mine = jnp.concatenate([d1, d2, c1, c2], -1)
    part = panel // 32
    mine = lax.dynamic_slice_in_dim(mine, high * part, part) + lax.ppermute(
        lax.dynamic_slice_in_dim(mine, (1 - high) * part, part), "pts", OTHER_HIGH
    )

    def spread(value):
        far_value = lax.ppermute(value, "lm", OTHER_CHIP)
        both = jnp.stack([value, far_value])
        other = lax.ppermute(both, "lm", OTHER_CORE)
        stack = jnp.stack([both[0], other[0], both[1], other[1]])
        return [index_of(stack, q ^ j) for q in range(4)]

    s0, s1, s2, s3 = spread(mine)
    wide, thin = panel, panel // 2

    def pick(s, at):
        edges = (0, wide, wide + thin, 2 * wide + thin, 3 * wide + thin)
        return s[:, edges[at] : edges[at + 1]]

    nothing = jnp.zeros((part, panel), jnp.float32)
    upper = jnp.concatenate(
        [
            jnp.concatenate(
                [
                    pick(s0, 0),
                    pick(s0, 1),
                    pick(s1, 1),
                    pick(s0, 2) + pick(s2, 2),
                    pick(s1, 3) + pick(s2, 3),
                ],
                1,
            ),
            jnp.concatenate(
                [nothing, pick(s1, 0), pick(s0, 3) + pick(s3, 3), pick(s1, 2) + pick(s3, 2)], 1
            ),
            jnp.concatenate([nothing, nothing, pick(s2, 0), pick(s2, 1), pick(s3, 1)], 1),
            jnp.concatenate([nothing, nothing, nothing, pick(s3, 0)], 1),
        ],
        0,
    )
    ordered = jnp.take(upper.reshape(ROWS, 16, CLUSTER), block_order, axis=1).reshape(ROWS, -1)

    def finish(near):
        got = lax.ppermute(near, "lm", OTHER_CHIP)
        got_pair = lax.ppermute(got, "lm", OTHER_CORE)
        before = jnp.where(
            first_core,
            jnp.concatenate([got, got_pair], 1),
            jnp.concatenate([got_pair, got], 1),
        )
        return near - jnp.where(first_chip, 0.0, mm(before, far))

    solved = finish(mm(lax.dynamic_slice_in_dim(ordered, chip * 2 * panel, 2 * panel, 1), local))

    def flipped(rows):
        blocks = rows.reshape(ROWS, 8, ROWS).transpose(1, 0, 2)
        got = jnp.stack(
            [lax.ppermute(index_of(blocks, member ^ k), ("pts", "lm"), flip(k)) for k in range(8)]
        )
        return jnp.take(got, jnp.arange(8) ^ member, axis=0)

    columns = jnp.concatenate(spread(flipped(solved)), 0)
    columns = columns.reshape(2, 16, 4, part, ROWS).transpose(2, 1, 0, 3, 4).reshape(16, CLUSTER, ROWS)
    columns = jnp.take(columns, block_order, axis=0).reshape(-1, ROWS)
    result = finish(tmm(lax.dynamic_slice_in_dim(columns, chip * 2 * panel, 2 * panel, 0), local))
    turned = flipped(result).transpose(2, 0, 1).reshape(ROWS, panel)
    return jnp.where(group <= j, (result + turned) / total, 0.0)


def solution(mesh):
    placed = (P("pts", "lm"), P(None, "lm"), P("lm", None, None), P())
    return jax.shard_map(
        per_device, mesh=mesh, in_specs=placed, out_specs=P("pts", "lm"), check_vma=False
    )
```

time: 705 us -> 211 us (0.30)
  the two profiles are of different devices: /device:TPU:0 before, /device:TPU:1 now
where the time goes in v1:
time: 211 us; the launch traced here: 208 us
  starting transfers between devices  111 us (53%)
  waiting for transfers between devices  46.2 us (22%)
  matrix products  32.2 us (15%)
  local copies, waits for them, and re-layouts  15.1 us (7%)
  other arithmetic  3 us (1%)
    ppermute x16, starting transfers between devices, flipped(): lax.ppermute(index_of(blocks, member ^ k), ('pts', 'lm'), flip(k))  42.1 us
    dot_general x7, matrix products, mm(): return jnp.dot(a, b, precision=HIGH)  18.9 us
    dot_general x5, matrix products, tmm(): return lax.dot_general(a, b, (((0,), (0,)), ((), ())), precision=HIGH)  13.4 us
    ppermute x2, starting transfers between devices, spread(): other = lax.ppermute(both, 'lm', OTHER_CORE)  12.4 us
    ppermute x6, starting transfers between devices, scatter_plane(): c += lax.ppermute(index_of(a, (y + step) % 4), 'pts', along_y(step))  10.1 us
    ppermute x6, starting transfers between devices, scatter_plane(): d += lax.ppermute(index_of(b, (x + step) % 4), 'pts', along_x(step))  9.88 us
    ppermute x16, waiting for transfers between devices, flipped(): lax.ppermute(index_of(blocks, member ^ k), ('pts', 'lm'), flip(k))  8.14 us
    ppermute x2, waiting for transfers between devices, finish(): got = lax.ppermute(near, 'lm', OTHER_CHIP)  8.11 us
  transfers between devices with their start and end apart: 53, of which 20 were waited for; matrix products, arithmetic and copies ran while one was open for 20% of the time, Pallas kernels for 0%

profile of v1, /device:TPU:1, one launch (start us, length us, event | category | flops | bytes accessed | tf_op | source)
XLA Modules:
  0.0 208.5 jit_solution(7428904555425384426)
XLA Ops:
  1.4 2.2 %constant_dynamic-slice_fusion.17 = f32[512,512]{1,0:T(8,128)} fusion(f32[1024,512]{1,0:T(8,128)} %param.6, s32[]{:T(128)S(6)} %select_n.350), kind=kLoop, calls=%fused_computation.179 | loop fusion | bytes 2097156 | tf_op jit(solution)/shard_map/dynamic_slice | solution.py:77
  3.7 1.7 collective-permute-start.13
  5.4 2.9 %convolution_multiply_fusion = f32[512,512]{1,0:T(8,128)} fusion(f32[1024,512]{1,0:T(8,128)S(1)} %copy-done), kind=kOutput, calls=%fused_computation.15 | convolution fusion | flops 1610874880 | bytes 3145728 | tf_op jit(solution)/shard_map/dot_general | solution.py:45
  8.3 2.1 slice.104
  10.4 1.9 dynamic-slice_bitcast_fusion.12
  17.5 3.1 %slice.93 = f32[1024,512]{1,0:T(8,128)} slice(f32[2048,512]{1,0:T(8,128)} %param.7), slice={[0:1024], [0:512]} | slice | bytes 4194304 | tf_op jit(solution)/shard_map/slice | solution.py:83
  20.6 3.6 %fusion.6 = f32[512,512]{1,0:T(8,128)} fusion(f32[2048,512]{1,0:T(8,128)} %param.7, s32[]{:T(128)S(6)} %select_n.363, f32[1,512,512]{2,1,0:T(8,128)} %param.8), kind=kOutput, calls=%fused_computation.23 | convolution fusion | flops 805306368 | bytes 3145732 | tf_op jit(solution)/shard_map/dot_general | solution.py:41
  24.2 5.0 %fusion.75 = f32[1024,512]{1,0:T(8,128)} fusion(f32[1,512,512]{2,1,0:T(8,128)} %param.8, f32[2048,512]{1,0:T(8,128)} %param.7), kind=kOutput, calls=%fused_computation.193 | convolution fusion | flops 1610612736 | bytes 5242880 | tf_op jit(solution)/shard_map/dot_general | solution.py:41
  32.2 2.3 %collective-permute-start.15 = (f32[4,32,512]{2,1,0:T(8,128)S(1)}, f32[4,32,512]{2,1,0:T(8,128)S(1)}, u32[]{:S(2)}, u32[]{:S(2)}) collective-permute-start(f32[4,32,512]{2,1,0:T(8,128)S(1)} %get-tuple-element.12), channel_id=1, source_target_pairs={{0,48},{4,52},{8,56},{12,60},{16,0},{20,4},{24,8},{28,12},{32,16},... | collective-permute-start | bytes 786440 | tf_op jit(solution)/shard_map/ppermute | solution.py:55
  36.5 4.5 %collective-permute-done.14 = f32[4,32,512]{2,1,0:T(8,128)S(1)} collective-permute-done((f32[4,32,512]{2,1,0:T(8,128)S(1)}, f32[4,32,512]{2,1,0:T(8,128)S(1)}, u32[]{:S(2)}, u32[]{:S(2)}) %collective-permute-start.14) | collective-permute-done | bytes 262176 | tf_op jit(solution)/shard_map/ppermute | solution.py:55
  43.7 3.0 %collective-permute-done.16 = f32[4,32,512]{2,1,0:T(8,128)S(1)} collective-permute-done((f32[4,32,512]{2,1,0:T(8,128)S(1)}, f32[4,32,512]{2,1,0:T(8,128)S(1)}, u32[]{:S(2)}, u32[]{:S(2)}) %collective-permute-start.16) | collective-permute-done | bytes 262176 | tf_op jit(solution)/shard_map/ppermute | solution.py:55
  46.7 2.9 %collective-permute-start.5 = (f32[32,384]{1,0:T(8,128)S(1)}, f32[32,384]{1,0:T(8,128)S(1)}, u32[]{:S(2)}, u32[]{:S(2)}) collective-permute-start(f32[32,384]{1,0:T(8,128)S(1)} %get-tuple-element.53), channel_id=1, source_target_pairs={{0,8},{4,12},{8,0},{12,4},{16,24},{20,28},{24,16},{28,20},{32,40},... | collective-permute-start | bytes 147464 | tf_op jit(solution)/shard_map/ppermute | solution.py:61
  50.2 2.3 %collective-permute-start.18 = (f32[32,512]{1,0:T(8,128)S(1)}, f32[32,512]{1,0:T(8,128)S(1)}, u32[]{:S(2)}, u32[]{:S(2)}) collective-permute-start(f32[32,512]{1,0:T(8,128)S(1)} %get-tuple-element.46), channel_id=1, source_target_pairs={{0,12},{4,0},{8,4},{12,8},{16,28},{20,16},{24,20},{28,24},{32,44},... | collective-permute-start | bytes 196616 | tf_op jit(solution)/shard_map/ppermute | solution.py:61
  52.5 1.7 collective-permute-start.19
  54.4 2.2 %collective-permute-start.32 = (f32[1024,512]{1,0:T(8,128)}, f32[1024,512]{1,0:T(8,128)}, u32[]{:S(2)}, u32[]{:S(2)}) collective-permute-start(f32[1024,512]{1,0:T(8,128)} %slice.93), channel_id=1, source_target_pairs={{0,1},{1,0},{2,3},{3,2},{4,5},{5,4},{6,7},{7,6},{8,9},{9,8},{10,11... | collective-permute-start | bytes 6291464 | tf_op jit(solution)/shard_map/ppermute | solution.py:84
  57.1 3.8 %fusion = f32[512,256]{1,0:T(8,128)S(1)} fusion(f32[1024,512]{1,0:T(8,128)S(1)} %copy-done, f32[1024,512]{1,0:T(8,128)} %collective-permute-done.6, pred[]{:T(512)S(6)} %eq.35), kind=kOutput, calls=%fused_computation.6 | convolution fusion | flops 806092800 | bytes 6816768 | tf_op jit(solution)/shard_map/dot_general | solution.py:45
  64.3 2.7 %fusion.8 = f32[512,512]{1,0:T(8,128)S(1)} fusion(f32[512,512]{1,0:T(8,128)S(1)} %collective-permute-done.13, f32[1024,512]{1,0:T(8,128)} %collective-permute-done.6, s32[]{:T(128)S(6)} %select_n.349, pred[]{:T(512)S(6)} %eq.36), kind=kOutput, calls=%fused_computation.25 | convolution fusion | flops 805830656 | bytes 5244928 | tf_op jit(solution)/shard_map/dot_general | solution.py:45
  67.4 3.2 %collective-permute-start.21 = (f32[4,32,512]{2,1,0:T(8,128)S(1)}, f32[4,32,512]{2,1,0:T(8,128)S(1)}, u32[]{:S(2)}, u32[]{:S(2)}) collective-permute-start(f32[4,32,512]{2,1,0:T(8,128)S(1)} %get-tuple-element.15), channel_id=1, source_target_pairs={{0,12},{4,0},{8,4},{12,8},{16,28},{20,16},{24,20},{28,24},{32,44},... | collective-permute-start | bytes 786440 | tf_op jit(solution)/shard_map/ppermute | solution.py:56
  72.3 4.9 %collective-permute-done.20 = f32[4,32,512]{2,1,0:T(8,128)S(1)} collective-permute-done((f32[4,32,512]{2,1,0:T(8,128)S(1)}, f32[4,32,512]{2,1,0:T(8,128)S(1)}, u32[]{:S(2)}, u32[]{:S(2)}) %collective-permute-start.20) | collective-permute-done | bytes 262176 | tf_op jit(solution)/shard_map/ppermute | solution.py:56
  78.5 3.5 %collective-permute-start.11 = (f32[32,384]{1,0:T(8,128)S(1)}, f32[32,384]{1,0:T(8,128)S(1)}, u32[]{:S(2)}, u32[]{:S(2)}) collective-permute-start(f32[32,384]{1,0:T(8,128)S(1)} %get-tuple-element.57), channel_id=1, source_target_pairs={{0,48},{4,52},{8,56},{12,60},{16,0},{20,4},{24,8},{28,12},{32,16},... | collective-permute-start | bytes 147464 | tf_op jit(solution)/shard_map/ppermute | solution.py:62
  84.0 2.9 %collective-permute-start.23 = (f32[32,512]{1,0:T(8,128)S(1)}, f32[32,512]{1,0:T(8,128)S(1)}, u32[]{:S(2)}, u32[]{:S(2)}) collective-permute-start(f32[32,512]{1,0:T(8,128)S(1)} %get-tuple-element.47), channel_id=1, source_target_pairs={{0,16},{4,20},{8,24},{12,28},{16,32},{20,36},{24,40},{28,44},{32,4... | collective-permute-start | bytes 196616 | tf_op jit(solution)/shard_map/ppermute | solution.py:62
  86.9 1.9 collective-permute-start.25
  91.6 3.4 %collective-permute-start.26 = (f32[16,1792]{1,0:T(8,128)S(1)}, f32[16,1792]{1,0:T(8,128)S(1)}, u32[]{:S(2)}, u32[]{:S(2)}) collective-permute-start(f32[16,1792]{1,0:T(8,128)S(1)} %constant_dynamic-slice_fusion.16), channel_id=1, source_target_pairs={{0,64},{4,68},{8,72},{12,76},{16,80},{20,84},{24,88},{28,92},{32,9... | collective-permute-start | bytes 344072 | tf_op jit(solution)/shard_map/ppermute | solution.py:117
  95.1 2.1 %collective-permute-done.26 = f32[16,1792]{1,0:T(8,128)S(1)} collective-permute-done((f32[16,1792]{1,0:T(8,128)S(1)}, f32[16,1792]{1,0:T(8,128)S(1)}, u32[]{:S(2)}, u32[]{:S(2)}) %collective-permute-start.26) | collective-permute-done | bytes 114720 | tf_op jit(solution)/shard_map/ppermute | solution.py:117
  97.2 1.9 collective-permute-start.27
  99.2 2.5 %collective-permute-done.27 = f32[16,1792]{1,0:T(8,128)S(1)} collective-permute-done((f32[16,1792]{1,0:T(8,128)S(1)}, f32[16,1792]{1,0:T(8,128)S(1)}, u32[]{:S(2)}, u32[]{:S(2)}) %collective-permute-start.27) | collective-permute-done | bytes 114720 | tf_op jit(solution)/shard_map/ppermute | solution.py:122
  101.6 12.3 %collective-permute-start.28 = (f32[2,16,1792]{2,1,0:T(8,128)S(1)}, f32[2,16,1792]{2,1,0:T(8,128)S(1)}, u32[]{:S(2)}, u32[]{:S(2)}) collective-permute-start(f32[2,16,1792]{2,1,0:T(8,128)S(1)} %pad_maximum_fusion.5), channel_id=1, source_target_pairs={{0,1},{1,0},{2,3},{3,2},{4,5},{5,4},{6,7},{7,6},{8,9},{9,8},{10,11... | collective-permute-start | bytes 688136 | tf_op jit(solution)/shard_map/ppermute | solution.py:124
  114.0 2.2 %convolution_negate_fusion = f32[512,512]{0,1:T(8,128)S(1)} fusion(f32[512,512]{1,0:T(8,128)S(1)} %copy-done.1, f32[512,512]{1,0:T(8,128)} %collective-permute-done.29), kind=kOutput, calls=%fused_computation.14 | convolution fusion | flops 805568512 | bytes 3145728 | tf_op jit(solution)/shard_map/dot_general | solution.py:41
  117.1 2.4 %fusion.3 = f32[64,512]{1,0:T(8,128)S(1)} fusion(f32[512,512]{1,0:T(8,128)} %bitcast.44, f32[512,512]{1,0:T(8,128)S(1)} %bitcast.218, pred[]{:T(512)S(6)} %eq.35, f32[64,2048]{1,0:T(8,128)S(1)} %copy_bitcast_fusion, s32[]{:T(128)S(6)} %select_n.363, pred[1024]{0:T(1024)(128)(4,1)S(1)} %dynamic-slice.65), kind=kOutput, calls=%fused_computation.9 | convolution fusion | flops 202440704 | bytes 2491397 | tf_op jit(solution)/shard_map/dot_general | solution.py:41
  120.2 4.6 %collective-permute-done.30 = f32[64,512]{1,0:T(8,128)S(1)} collective-permute-done((f32[64,512]{1,0:T(8,128)S(1)}, f32[64,512]{1,0:T(8,128)S(1)}, u32[]{:S(2)}, u32[]{:S(2)}) %collective-permute-start.30) | collective-permute-done | bytes 131104 | tf_op jit(solution)/shard_map/ppermute | solution.py:159
  125.6 4.1 %bitcast_add_fusion = f32[1024,512]{1,0:T(8,128)S(1)} fusion(f32[1024,512]{1,0:T(8,128)} %fusion.75, f32[512,512]{0,1:T(8,128)S(1)} %convolution_negate_fusion, f32[1024,512]{1,0:T(8,128)} %collective-permute-done.32, pred[]{:T(512)S(6)} %eq.35), kind=kOutput, calls=%fused_computation.5 | convolution fusion | flops 1611661312 | bytes 7340033 | tf_op jit(solution)/shard_map/dot_general | solution.py:41
  130.7 3.1 %collective-permute-start.33 = (f32[64,64]{1,0:T(8,128)S(1)}, f32[64,64]{1,0:T(8,128)S(1)}, u32[]{:S(2)}, u32[]{:S(2)}) collective-permute-start(f32[64,64]{1,0:T(8,128)S(1)} %bitcast.243), channel_id=1, source_target_pairs={{0,0},{1,32},{2,64},{3,96},{4,4},{5,36},{6,68},{7,100},{8,8},{9,40... | collective-permute-start | bytes 49160 | tf_op jit(solution)/shard_map/ppermute | solution.py:173
  133.9 3.8 %collective-permute-start.35 = (f32[64,64]{1,0:T(8,128)S(1)}, f32[64,64]{1,0:T(8,128)S(1)}, u32[]{:S(2)}, u32[]{:S(2)}) collective-permute-start(f32[64,64]{1,0:T(8,128)S(1)} %bitcast.241), channel_id=1, source_target_pairs={{0,8},{1,40},{2,72},{3,104},{4,12},{5,44},{6,76},{7,108},{8,0},{9,... | collective-permute-start | bytes 49160 | tf_op jit(solution)/shard_map/ppermute | solution.py:173
  137.7 4.5 %collective-permute-start.36 = (f32[64,64]{1,0:T(8,128)S(1)}, f32[64,64]{1,0:T(8,128)S(1)}, u32[]{:S(2)}, u32[]{:S(2)}) collective-permute-start(f32[64,64]{1,0:T(8,128)S(1)} %bitcast.239), channel_id=1, source_target_pairs={{0,12},{1,44},{2,76},{3,108},{4,8},{5,40},{6,72},{7,104},{8,4},{9,... | collective-permute-start | bytes 49160 | tf_op jit(solution)/shard_map/ppermute | solution.py:173
  143.9 3.0 %collective-permute-start.39 = (f32[64,64]{1,0:T(8,128)S(1)}, f32[64,64]{1,0:T(8,128)S(1)}, u32[]{:S(2)}, u32[]{:S(2)}) collective-permute-start(f32[64,64]{1,0:T(8,128)S(1)} %bitcast.234), channel_id=1, source_target_pairs={{0,24},{1,56},{2,88},{3,120},{4,28},{5,60},{6,92},{7,124},{8,16},{... | collective-permute-start | bytes 49160 | tf_op jit(solution)/shard_map/ppermute | solution.py:173
  146.9 4.2 %collective-permute-start.40 = (f32[64,64]{1,0:T(8,128)S(1)}, f32[64,64]{1,0:T(8,128)S(1)}, u32[]{:S(2)}, u32[]{:S(2)}) collective-permute-start(f32[64,64]{1,0:T(8,128)S(1)} %bitcast.233), channel_id=1, source_target_pairs={{0,28},{1,60},{2,92},{3,124},{4,24},{5,56},{6,88},{7,120},{8,20},{... | collective-permute-start | bytes 49160 | tf_op jit(solution)/shard_map/ppermute | solution.py:173
  151.3 2.3 %collective-permute-done.40 = f32[64,64]{1,0:T(8,128)S(1)} collective-permute-done((f32[64,64]{1,0:T(8,128)S(1)}, f32[64,64]{1,0:T(8,128)S(1)}, u32[]{:S(2)}, u32[]{:S(2)}) %collective-permute-start.40) | collective-permute-done | bytes 16416 | tf_op jit(solution)/shard_map/ppermute | solution.py:173
  154.3 6.1 %collective-permute-start.41 = (f32[8,64,64]{2,1,0:T(8,128)S(1)}, f32[8,64,64]{2,1,0:T(8,128)S(1)}, u32[]{:S(2)}, u32[]{:S(2)}) collective-permute-start(f32[8,64,64]{2,1,0:T(8,128)S(1)} %broadcast_select_fusion.1), channel_id=1, source_target_pairs={{0,2},{1,3},{2,0},{3,1},{4,6},{5,7},{6,4},{7,5},{8,10},{9,11},{10,... | collective-permute-start | bytes 393224 | tf_op jit(solution)/shard_map/ppermute | solution.py:122
  160.5 3.7 %collective-permute-done.41 = f32[8,64,64]{2,1,0:T(8,128)S(1)} collective-permute-done((f32[8,64,64]{2,1,0:T(8,128)S(1)}, f32[8,64,64]{2,1,0:T(8,128)S(1)}, u32[]{:S(2)}, u32[]{:S(2)}) %collective-permute-start.41) | collective-permute-done | bytes 131104 | tf_op jit(solution)/shard_map/ppermute | solution.py:122
  164.3 1.9 collective-permute-done.42
  168.3 3.0 %fusion.2 = f32[64,512]{1,0:T(8,128)S(1)} fusion(f32[512,512]{1,0:T(8,128)} %bitcast.44, f32[512,512]{1,0:T(8,128)} %bitcast.219, pred[]{:T(512)S(6)} %eq.35, f32[2048,64]{1,0:T(8,128)} %bitcast.220, s32[]{:T(128)S(6)} %select_n.363, pred[1024]{0:T(1024)(128)(4,1)S(1)} %dynamic-slice.65), kind=kOutput, calls=%fused_computation.8 | convolution fusion | flops 202440704 | bytes 2753541 | tf_op jit(solution)/shard_map/dot_general | solution.py:45
  172.9 3.6 %collective-permute-done.43 = f32[64,512]{1,0:T(8,128)S(1)} collective-permute-done((f32[64,512]{1,0:T(8,128)S(1)}, f32[64,512]{1,0:T(8,128)S(1)}, u32[]{:S(2)}, u32[]{:S(2)}) %collective-permute-start.43) | collective-permute-done | bytes 131104 | tf_op jit(solution)/shard_map/ppermute | solution.py:159
  179.4 1.9 collective-permute-start.45
  182.2 6.5 %collective-permute-start.47 = (f32[64,64]{1,0:T(8,128)S(1)}, f32[64,64]{1,0:T(8,128)S(1)}, u32[]{:S(2)}, u32[]{:S(2)}) collective-permute-start(f32[64,64]{1,0:T(8,128)S(1)} %bitcast.235), channel_id=1, source_target_pairs={{0,8},{1,40},{2,72},{3,104},{4,12},{5,44},{6,76},{7,108},{8,0},{9,... | collective-permute-start | bytes 49160 | tf_op jit(solution)/shard_map/ppermute | solution.py:173
  188.7 2.3 %collective-permute-start.48 = (f32[64,64]{1,0:T(8,128)S(1)}, f32[64,64]{1,0:T(8,128)S(1)}, u32[]{:S(2)}, u32[]{:S(2)}) collective-permute-start(f32[64,64]{1,0:T(8,128)S(1)} %bitcast.232), channel_id=1, source_target_pairs={{0,12},{1,44},{2,76},{3,108},{4,8},{5,40},{6,72},{7,104},{8,4},{9,... | collective-permute-start | bytes 49160 | tf_op jit(solution)/shard_map/ppermute | solution.py:173
  190.9 4.3 %collective-permute-start.49 = (f32[64,64]{1,0:T(8,128)S(1)}, f32[64,64]{1,0:T(8,128)S(1)}, u32[]{:S(2)}, u32[]{:S(2)}) collective-permute-start(f32[64,64]{1,0:T(8,128)S(1)} %bitcast.231), channel_id=1, source_target_pairs={{0,16},{1,48},{2,80},{3,112},{4,20},{5,52},{6,84},{7,116},{8,24},{... | collective-permute-start | bytes 49160 | tf_op jit(solution)/shard_map/ppermute | solution.py:173
  195.2 5.1 %collective-permute-start.51 = (f32[64,64]{1,0:T(8,128)S(1)}, f32[64,64]{1,0:T(8,128)S(1)}, u32[]{:S(2)}, u32[]{:S(2)}) collective-permute-start(f32[64,64]{1,0:T(8,128)S(1)} %bitcast.229), channel_id=1, source_target_pairs={{0,24},{1,56},{2,88},{3,120},{4,28},{5,60},{6,92},{7,124},{8,16},{... | collective-permute-start | bytes 49160 | tf_op jit(solution)/shard_map/ppermute | solution.py:173
  202.3 4.7 %collective-permute-done.52 = f32[64,64]{1,0:T(8,128)S(1)} collective-permute-done((f32[64,64]{1,0:T(8,128)S(1)}, f32[64,64]{1,0:T(8,128)S(1)}, u32[]{:S(2)}, u32[]{:S(2)}) %collective-permute-start.52) | collective-permute-done | bytes 16416 | tf_op jit(solution)/shard_map/ppermute | solution.py:173
  (157 shorter events, 44.0 us)
Async XLA Ops:
  0.0 57.1 %collective-permute-start.6 = (f32[1024,512]{1,0:T(8,128)}, f32[1024,512]{1,0:T(8,128)}, u32[]{:S(2)}, u32[]{:S(2)}) collective-permute-start(f32[1024,512]{1,0:T(8,128)} %param.6), channel_id=1, source_target_pairs={{0,1},{1,0},{2,3},{3,2},{4,5},{5,4},{6,7},{7,6},{8,9},{9,8},{10,11... | collective-permute-start | bytes 6291464 | tf_op jit(solution)/shard_map/ppermute | solution.py:79
  3.7 25.6 %collective-permute-start.13 = (f32[512,512]{1,0:T(8,128)}, f32[512,512]{1,0:T(8,128)S(1)}, u32[]{:S(2)}, u32[]{:S(2)}) collective-permute-start(f32[512,512]{1,0:T(8,128)} %constant_dynamic-slice_fusion.17), channel_id=1, source_target_pairs={{0,2},{1,3},{2,0},{3,1},{4,6},{5,7},{6,4},{7,5},{8,10},{9,11},{10,... | collective-permute-start | bytes 3145736 | tf_op jit(solution)/shard_map/ppermute | solution.py:78
  12.3 19.4 %collective-permute-start = (f32[4,32,384]{2,1,0:T(8,128)}, f32[4,32,384]{2,1,0:T(8,128)}, u32[]{:S(2)}, u32[]{:S(2)}) collective-permute-start(f32[4,32,384]{2,1,0:T(8,128)} %get-tuple-element.16), channel_id=1, source_target_pairs={{0,16},{4,20},{8,24},{12,28},{16,32},{20,36},{24,40},{28,44},{32,4... | collective-permute-start | bytes 589832 | tf_op jit(solution)/shard_map/ppermute | solution.py:55
  13.5 18.6 %collective-permute-start.1 = (f32[4,32,384]{2,1,0:T(8,128)}, f32[4,32,384]{2,1,0:T(8,128)}, u32[]{:S(2)}, u32[]{:S(2)}) collective-permute-start(f32[4,32,384]{2,1,0:T(8,128)} %get-tuple-element.18), channel_id=1, source_target_pairs={{0,48},{4,52},{8,56},{12,60},{16,0},{20,4},{24,8},{28,12},{32,16},... | collective-permute-start | bytes 589832 | tf_op jit(solution)/shard_map/ppermute | solution.py:55
  15.0 19.5 %collective-permute-start.2 = (f32[4,32,384]{2,1,0:T(8,128)}, f32[4,32,384]{2,1,0:T(8,128)}, u32[]{:S(2)}, u32[]{:S(2)}) collective-permute-start(f32[4,32,384]{2,1,0:T(8,128)} %get-tuple-element.17), channel_id=1, source_target_pairs={{0,32},{4,36},{8,40},{12,44},{16,48},{20,52},{24,56},{28,60},{32,0... | collective-permute-start | bytes 589832 | tf_op jit(solution)/shard_map/ppermute | solution.py:55
  29.3 84.7 %collective-permute-start.29 = (f32[512,512]{1,0:T(8,128)}, f32[512,512]{1,0:T(8,128)}, u32[]{:S(2)}, u32[]{:S(2)}) collective-permute-start(f32[512,512]{1,0:T(8,128)} %bitcast.44), channel_id=1, source_target_pairs={{0,1},{1,0},{2,3},{3,2},{4,5},{5,4},{6,7},{7,6},{8,9},{9,8},{10,11... | collective-permute-start | bytes 3145736 | tf_op jit(solution)/shard_map/ppermute | solution.py:82
  31.7 9.2 %collective-permute-start.14 = (f32[4,32,512]{2,1,0:T(8,128)S(1)}, f32[4,32,512]{2,1,0:T(8,128)S(1)}, u32[]{:S(2)}, u32[]{:S(2)}) collective-permute-start(f32[4,32,512]{2,1,0:T(8,128)S(1)} %get-tuple-element.10), channel_id=1, source_target_pairs={{0,16},{4,20},{8,24},{12,28},{16,32},{20,36},{24,40},{28,44},{32,4... | collective-permute-start | bytes 786440 | tf_op jit(solution)/shard_map/ppermute | solution.py:55
  32.2 10.1 %collective-permute-start.15 = (f32[4,32,512]{2,1,0:T(8,128)S(1)}, f32[4,32,512]{2,1,0:T(8,128)S(1)}, u32[]{:S(2)}, u32[]{:S(2)}) collective-permute-start(f32[4,32,512]{2,1,0:T(8,128)S(1)} %get-tuple-element.12), channel_id=1, source_target_pairs={{0,48},{4,52},{8,56},{12,60},{16,0},{20,4},{24,8},{28,12},{32,16},... | collective-permute-start | bytes 786440 | tf_op jit(solution)/shard_map/ppermute | solution.py:55
  34.5 12.2 %collective-permute-start.16 = (f32[4,32,512]{2,1,0:T(8,128)S(1)}, f32[4,32,512]{2,1,0:T(8,128)S(1)}, u32[]{:S(2)}, u32[]{:S(2)}) collective-permute-start(f32[4,32,512]{2,1,0:T(8,128)S(1)} %get-tuple-element.11), channel_id=1, source_target_pairs={{0,32},{4,36},{8,40},{12,44},{16,48},{20,52},{24,56},{28,60},{32,0... | collective-permute-start | bytes 786440 | tf_op jit(solution)/shard_map/ppermute | solution.py:55
  40.9 8.8 %collective-permute-start.3 = (f32[32,384]{1,0:T(8,128)S(1)}, f32[32,384]{1,0:T(8,128)S(1)}, u32[]{:S(2)}, u32[]{:S(2)}) collective-permute-start(f32[32,384]{1,0:T(8,128)S(1)} %get-tuple-element.52), channel_id=1, source_target_pairs={{0,4},{4,8},{8,12},{12,0},{16,20},{20,24},{24,28},{28,16},{32,36},... | collective-permute-start | bytes 147464 | tf_op jit(solution)/shard_map/ppermute | solution.py:61
  42.2 8.0 %collective-permute-start.4 = (f32[32,384]{1,0:T(8,128)S(1)}, f32[32,384]{1,0:T(8,128)S(1)}, u32[]{:S(2)}, u32[]{:S(2)}) collective-permute-start(f32[32,384]{1,0:T(8,128)S(1)} %get-tuple-element.54), channel_id=1, source_target_pairs={{0,12},{4,0},{8,4},{12,8},{16,28},{20,16},{24,20},{28,24},{32,44},... | collective-permute-start | bytes 147464 | tf_op jit(solution)/shard_map/ppermute | solution.py:61
  46.7 5.8 %collective-permute-start.5 = (f32[32,384]{1,0:T(8,128)S(1)}, f32[32,384]{1,0:T(8,128)S(1)}, u32[]{:S(2)}, u32[]{:S(2)}) collective-permute-start(f32[32,384]{1,0:T(8,128)S(1)} %get-tuple-element.53), channel_id=1, source_target_pairs={{0,8},{4,12},{8,0},{12,4},{16,24},{20,28},{24,16},{28,20},{32,40},... | collective-permute-start | bytes 147464 | tf_op jit(solution)/shard_map/ppermute | solution.py:61
  49.7 4.7 %collective-permute-start.17 = (f32[32,512]{1,0:T(8,128)S(1)}, f32[32,512]{1,0:T(8,128)S(1)}, u32[]{:S(2)}, u32[]{:S(2)}) collective-permute-start(f32[32,512]{1,0:T(8,128)S(1)} %get-tuple-element.44), channel_id=1, source_target_pairs={{0,4},{4,8},{8,12},{12,0},{16,20},{20,24},{24,28},{28,16},{32,36},... | collective-permute-start | bytes 196616 | tf_op jit(solution)/shard_map/ppermute | solution.py:61
  50.2 6.4 %collective-permute-start.18 = (f32[32,512]{1,0:T(8,128)S(1)}, f32[32,512]{1,0:T(8,128)S(1)}, u32[]{:S(2)}, u32[]{:S(2)}) collective-permute-start(f32[32,512]{1,0:T(8,128)S(1)} %get-tuple-element.46), channel_id=1, source_target_pairs={{0,12},{4,0},{8,4},{12,8},{16,28},{20,16},{24,20},{28,24},{32,44},... | collective-permute-start | bytes 196616 | tf_op jit(solution)/shard_map/ppermute | solution.py:61
  52.5 4.6 %collective-permute-start.19 = (f32[32,512]{1,0:T(8,128)S(1)}, f32[32,512]{1,0:T(8,128)S(1)}, u32[]{:S(2)}, u32[]{:S(2)}) collective-permute-start(f32[32,512]{1,0:T(8,128)S(1)} %get-tuple-element.45), channel_id=1, source_target_pairs={{0,8},{4,12},{8,0},{12,4},{16,24},{20,28},{24,16},{28,20},{32,40},... | collective-permute-start | bytes 196616 | tf_op jit(solution)/shard_map/ppermute | solution.py:61
  54.4 71.1 %collective-permute-start.32 = (f32[1024,512]{1,0:T(8,128)}, f32[1024,512]{1,0:T(8,128)}, u32[]{:S(2)}, u32[]{:S(2)}) collective-permute-start(f32[1024,512]{1,0:T(8,128)} %slice.93), channel_id=1, source_target_pairs={{0,1},{1,0},{2,3},{3,2},{4,5},{5,4},{6,7},{7,6},{8,9},{9,8},{10,11... | collective-permute-start | bytes 6291464 | tf_op jit(solution)/shard_map/ppermute | solution.py:84
  61.0 6.1 %collective-permute-start.7 = (f32[4,32,384]{2,1,0:T(8,128)S(1)}, f32[4,32,384]{2,1,0:T(8,128)S(1)}, u32[]{:S(2)}, u32[]{:S(2)}) collective-permute-start(f32[4,32,384]{2,1,0:T(8,128)S(1)} %get-tuple-element.19), channel_id=1, source_target_pairs={{0,4},{4,8},{8,12},{12,0},{16,20},{20,24},{24,28},{28,16},{32,36},... | collective-permute-start | bytes 589832 | tf_op jit(solution)/shard_map/ppermute | solution.py:56
  62.1 5.2 %collective-permute-start.8 = (f32[4,32,384]{2,1,0:T(8,128)S(1)}, f32[4,32,384]{2,1,0:T(8,128)S(1)}, u32[]{:S(2)}, u32[]{:S(2)}) collective-permute-start(f32[4,32,384]{2,1,0:T(8,128)S(1)} %get-tuple-element.20), channel_id=1, source_target_pairs={{0,12},{4,0},{8,4},{12,8},{16,28},{20,16},{24,20},{28,24},{32,44},... | collective-permute-start | bytes 589832 | tf_op jit(solution)/shard_map/ppermute | solution.py:56
  63.7 8.2 %collective-permute-start.9 = (f32[4,32,384]{2,1,0:T(8,128)S(1)}, f32[4,32,384]{2,1,0:T(8,128)S(1)}, u32[]{:S(2)}, u32[]{:S(2)}) collective-permute-start(f32[4,32,384]{2,1,0:T(8,128)S(1)} %get-tuple-element.21), channel_id=1, source_target_pairs={{0,8},{4,12},{8,0},{12,4},{16,24},{20,28},{24,16},{28,20},{32,40},... | collective-permute-start | bytes 589832 | tf_op jit(solution)/shard_map/ppermute | solution.py:56
  67.1 10.1 %collective-permute-start.20 = (f32[4,32,512]{2,1,0:T(8,128)S(1)}, f32[4,32,512]{2,1,0:T(8,128)S(1)}, u32[]{:S(2)}, u32[]{:S(2)}) collective-permute-start(f32[4,32,512]{2,1,0:T(8,128)S(1)} %get-tuple-element.13), channel_id=1, source_target_pairs={{0,4},{4,8},{8,12},{12,0},{16,20},{20,24},{24,28},{28,16},{32,36},... | collective-permute-start | bytes 786440 | tf_op jit(solution)/shard_map/ppermute | solution.py:56
  67.4 11.2 %collective-permute-start.21 = (f32[4,32,512]{2,1,0:T(8,128)S(1)}, f32[4,32,512]{2,1,0:T(8,128)S(1)}, u32[]{:S(2)}, u32[]{:S(2)}) collective-permute-start(f32[4,32,512]{2,1,0:T(8,128)S(1)} %get-tuple-element.15), channel_id=1, source_target_pairs={{0,12},{4,0},{8,4},{12,8},{16,28},{20,16},{24,20},{28,24},{32,44},... | collective-permute-start | bytes 786440 | tf_op jit(solution)/shard_map/ppermute | solution.py:56
  71.9 10.5 %collective-permute-start.22 = (f32[4,32,512]{2,1,0:T(8,128)S(1)}, f32[4,32,512]{2,1,0:T(8,128)S(1)}, u32[]{:S(2)}, u32[]{:S(2)}) collective-permute-start(f32[4,32,512]{2,1,0:T(8,128)S(1)} %get-tuple-element.14), channel_id=1, source_target_pairs={{0,8},{4,12},{8,0},{12,4},{16,24},{20,28},{24,16},{28,20},{32,40},... | collective-permute-start | bytes 786440 | tf_op jit(solution)/shard_map/ppermute | solution.py:56
  77.2 6.8 %collective-permute-start.10 = (f32[32,384]{1,0:T(8,128)S(1)}, f32[32,384]{1,0:T(8,128)S(1)}, u32[]{:S(2)}, u32[]{:S(2)}) collective-permute-start(f32[32,384]{1,0:T(8,128)S(1)} %get-tuple-element.55), channel_id=1, source_target_pairs={{0,16},{4,20},{8,24},{12,28},{16,32},{20,36},{24,40},{28,44},{32,4... | collective-permute-start | bytes 147464 | tf_op jit(solution)/shard_map/ppermute | solution.py:62
  78.5 8.3 %collective-permute-start.11 = (f32[32,384]{1,0:T(8,128)S(1)}, f32[32,384]{1,0:T(8,128)S(1)}, u32[]{:S(2)}, u32[]{:S(2)}) collective-permute-start(f32[32,384]{1,0:T(8,128)S(1)} %get-tuple-element.57), channel_id=1, source_target_pairs={{0,48},{4,52},{8,56},{12,60},{16,0},{20,4},{24,8},{28,12},{32,16},... | collective-permute-start | bytes 147464 | tf_op jit(solution)/shard_map/ppermute | solution.py:62
  84.0 4.8 %collective-permute-start.23 = (f32[32,512]{1,0:T(8,128)S(1)}, f32[32,512]{1,0:T(8,128)S(1)}, u32[]{:S(2)}, u32[]{:S(2)}) collective-permute-start(f32[32,512]{1,0:T(8,128)S(1)} %get-tuple-element.47), channel_id=1, source_target_pairs={{0,16},{4,20},{8,24},{12,28},{16,32},{20,36},{24,40},{28,44},{32,4... | collective-permute-start | bytes 196616 | tf_op jit(solution)/shard_map/ppermute | solution.py:62
  86.9 4.7 %collective-permute-start.25 = (f32[32,512]{1,0:T(8,128)S(1)}, f32[32,512]{1,0:T(8,128)S(1)}, u32[]{:S(2)}, u32[]{:S(2)}) collective-permute-start(f32[32,512]{1,0:T(8,128)S(1)} %get-tuple-element.48), channel_id=1, source_target_pairs={{0,32},{4,36},{8,40},{12,44},{16,48},{20,52},{24,56},{28,60},{32,0... | collective-permute-start | bytes 196616 | tf_op jit(solution)/shard_map/ppermute | solution.py:62
  91.6 5.6 %collective-permute-start.26 = (f32[16,1792]{1,0:T(8,128)S(1)}, f32[16,1792]{1,0:T(8,128)S(1)}, u32[]{:S(2)}, u32[]{:S(2)}) collective-permute-start(f32[16,1792]{1,0:T(8,128)S(1)} %constant_dynamic-slice_fusion.16), channel_id=1, source_target_pairs={{0,64},{4,68},{8,72},{12,76},{16,80},{20,84},{24,88},{28,92},{32,9... | collective-permute-start | bytes 344072 | tf_op jit(solution)/shard_map/ppermute | solution.py:117
  101.6 14.6 %collective-permute-start.28 = (f32[2,16,1792]{2,1,0:T(8,128)S(1)}, f32[2,16,1792]{2,1,0:T(8,128)S(1)}, u32[]{:S(2)}, u32[]{:S(2)}) collective-permute-start(f32[2,16,1792]{2,1,0:T(8,128)S(1)} %pad_maximum_fusion.5), channel_id=1, source_target_pairs={{0,1},{1,0},{2,3},{3,2},{4,5},{5,4},{6,7},{7,6},{8,9},{9,8},{10,11... | collective-permute-start | bytes 688136 | tf_op jit(solution)/shard_map/ppermute | solution.py:124
  119.6 5.2 %collective-permute-start.30 = (f32[64,512]{1,0:T(8,128)S(1)}, f32[64,512]{1,0:T(8,128)S(1)}, u32[]{:S(2)}, u32[]{:S(2)}) collective-permute-start(f32[64,512]{1,0:T(8,128)S(1)} %fusion.3), channel_id=1, source_target_pairs={{0,2},{1,3},{2,0},{3,1},{4,6},{5,7},{6,4},{7,5},{8,10},{9,11},{10,... | collective-permute-start | bytes 393224 | tf_op jit(solution)/shard_map/ppermute | solution.py:159
  124.7 4.9 %collective-permute-start.31 = (f32[64,512]{1,0:T(8,128)S(1)}, f32[64,512]{1,0:T(8,128)S(1)}, u32[]{:S(2)}, u32[]{:S(2)}) collective-permute-start(f32[64,512]{1,0:T(8,128)S(1)} %collective-permute-done.30), channel_id=1, source_target_pairs={{0,1},{1,0},{2,3},{3,2},{4,5},{5,4},{6,7},{7,6},{8,9},{9,8},{10,11... | collective-permute-start | bytes 393224 | tf_op jit(solution)/shard_map/ppermute | solution.py:160
  130.7 13.2 %collective-permute-start.33 = (f32[64,64]{1,0:T(8,128)S(1)}, f32[64,64]{1,0:T(8,128)S(1)}, u32[]{:S(2)}, u32[]{:S(2)}) collective-permute-start(f32[64,64]{1,0:T(8,128)S(1)} %bitcast.243), channel_id=1, source_target_pairs={{0,0},{1,32},{2,64},{3,96},{4,4},{5,36},{6,68},{7,100},{8,8},{9,40... | collective-permute-start | bytes 49160 | tf_op jit(solution)/shard_map/ppermute | solution.py:173
  133.8 10.1 %collective-permute-start.34 = (f32[64,64]{1,0:T(8,128)S(1)}, f32[64,64]{1,0:T(8,128)S(1)}, u32[]{:S(2)}, u32[]{:S(2)}) collective-permute-start(f32[64,64]{1,0:T(8,128)S(1)} %bitcast.242), channel_id=1, source_target_pairs={{0,4},{1,36},{2,68},{3,100},{4,0},{5,32},{6,64},{7,96},{8,12},{9,4... | collective-permute-start | bytes 49160 | tf_op jit(solution)/shard_map/ppermute | solution.py:173
  133.9 13.0 %collective-permute-start.35 = (f32[64,64]{1,0:T(8,128)S(1)}, f32[64,64]{1,0:T(8,128)S(1)}, u32[]{:S(2)}, u32[]{:S(2)}) collective-permute-start(f32[64,64]{1,0:T(8,128)S(1)} %bitcast.241), channel_id=1, source_target_pairs={{0,8},{1,40},{2,72},{3,104},{4,12},{5,44},{6,76},{7,108},{8,0},{9,... | collective-permute-start | bytes 49160 | tf_op jit(solution)/shard_map/ppermute | solution.py:173
  137.7 13.5 %collective-permute-start.36 = (f32[64,64]{1,0:T(8,128)S(1)}, f32[64,64]{1,0:T(8,128)S(1)}, u32[]{:S(2)}, u32[]{:S(2)}) collective-permute-start(f32[64,64]{1,0:T(8,128)S(1)} %bitcast.239), channel_id=1, source_target_pairs={{0,12},{1,44},{2,76},{3,108},{4,8},{5,40},{6,72},{7,104},{8,4},{9,... | collective-permute-start | bytes 49160 | tf_op jit(solution)/shard_map/ppermute | solution.py:173
  142.2 9.0 %collective-permute-start.37 = (f32[64,64]{1,0:T(8,128)S(1)}, f32[64,64]{1,0:T(8,128)S(1)}, u32[]{:S(2)}, u32[]{:S(2)}) collective-permute-start(f32[64,64]{1,0:T(8,128)S(1)} %bitcast.237), channel_id=1, source_target_pairs={{0,16},{1,48},{2,80},{3,112},{4,20},{5,52},{6,84},{7,116},{8,24},{... | collective-permute-start | bytes 49160 | tf_op jit(solution)/shard_map/ppermute | solution.py:173
  143.9 7.3 %collective-permute-start.38 = (f32[64,64]{1,0:T(8,128)S(1)}, f32[64,64]{1,0:T(8,128)S(1)}, u32[]{:S(2)}, u32[]{:S(2)}) collective-permute-start(f32[64,64]{1,0:T(8,128)S(1)} %bitcast.236), channel_id=1, source_target_pairs={{0,20},{1,52},{2,84},{3,116},{4,16},{5,48},{6,80},{7,112},{8,28},{... | collective-permute-start | bytes 49160 | tf_op jit(solution)/shard_map/ppermute | solution.py:173
  143.9 7.3 %collective-permute-start.39 = (f32[64,64]{1,0:T(8,128)S(1)}, f32[64,64]{1,0:T(8,128)S(1)}, u32[]{:S(2)}, u32[]{:S(2)}) collective-permute-start(f32[64,64]{1,0:T(8,128)S(1)} %bitcast.234), channel_id=1, source_target_pairs={{0,24},{1,56},{2,88},{3,120},{4,28},{5,60},{6,92},{7,124},{8,16},{... | collective-permute-start | bytes 49160 | tf_op jit(solution)/shard_map/ppermute | solution.py:173
  146.9 6.7 %collective-permute-start.40 = (f32[64,64]{1,0:T(8,128)S(1)}, f32[64,64]{1,0:T(8,128)S(1)}, u32[]{:S(2)}, u32[]{:S(2)}) collective-permute-start(f32[64,64]{1,0:T(8,128)S(1)} %bitcast.233), channel_id=1, source_target_pairs={{0,28},{1,60},{2,92},{3,124},{4,24},{5,56},{6,88},{7,120},{8,20},{... | collective-permute-start | bytes 49160 | tf_op jit(solution)/shard_map/ppermute | solution.py:173
  154.3 9.9 %collective-permute-start.41 = (f32[8,64,64]{2,1,0:T(8,128)S(1)}, f32[8,64,64]{2,1,0:T(8,128)S(1)}, u32[]{:S(2)}, u32[]{:S(2)}) collective-permute-start(f32[8,64,64]{2,1,0:T(8,128)S(1)} %broadcast_select_fusion.1), channel_id=1, source_target_pairs={{0,2},{1,3},{2,0},{3,1},{4,6},{5,7},{6,4},{7,5},{8,10},{9,11},{10,... | collective-permute-start | bytes 393224 | tf_op jit(solution)/shard_map/ppermute | solution.py:122
  171.3 5.1 %collective-permute-start.43 = (f32[64,512]{1,0:T(8,128)S(1)}, f32[64,512]{1,0:T(8,128)S(1)}, u32[]{:S(2)}, u32[]{:S(2)}) collective-permute-start(f32[64,512]{1,0:T(8,128)S(1)} %fusion.2), channel_id=1, source_target_pairs={{0,2},{1,3},{2,0},{3,1},{4,6},{5,7},{6,4},{7,5},{8,10},{9,11},{10,... | collective-permute-start | bytes 393224 | tf_op jit(solution)/shard_map/ppermute | solution.py:159
  179.4 15.8 %collective-permute-start.45 = (f32[64,64]{1,0:T(8,128)S(1)}, f32[64,64]{1,0:T(8,128)S(1)}, u32[]{:S(2)}, u32[]{:S(2)}) collective-permute-start(f32[64,64]{1,0:T(8,128)S(1)} %bitcast.240), channel_id=1, source_target_pairs={{0,0},{1,32},{2,64},{3,96},{4,4},{5,36},{6,68},{7,100},{8,8},{9,40... | collective-permute-start | bytes 49160 | tf_op jit(solution)/shard_map/ppermute | solution.py:173
  181.4 13.9 %collective-permute-start.46 = (f32[64,64]{1,0:T(8,128)S(1)}, f32[64,64]{1,0:T(8,128)S(1)}, u32[]{:S(2)}, u32[]{:S(2)}) collective-permute-start(f32[64,64]{1,0:T(8,128)S(1)} %bitcast.238), channel_id=1, source_target_pairs={{0,4},{1,36},{2,68},{3,100},{4,0},{5,32},{6,64},{7,96},{8,12},{9,4... | collective-permute-start | bytes 49160 | tf_op jit(solution)/shard_map/ppermute | solution.py:173
  182.2 18.1 %collective-permute-start.47 = (f32[64,64]{1,0:T(8,128)S(1)}, f32[64,64]{1,0:T(8,128)S(1)}, u32[]{:S(2)}, u32[]{:S(2)}) collective-permute-start(f32[64,64]{1,0:T(8,128)S(1)} %bitcast.235), channel_id=1, source_target_pairs={{0,8},{1,40},{2,72},{3,104},{4,12},{5,44},{6,76},{7,108},{8,0},{9,... | collective-permute-start | bytes 49160 | tf_op jit(solution)/shard_map/ppermute | solution.py:173
  188.7 12.5 %collective-permute-start.48 = (f32[64,64]{1,0:T(8,128)S(1)}, f32[64,64]{1,0:T(8,128)S(1)}, u32[]{:S(2)}, u32[]{:S(2)}) collective-permute-start(f32[64,64]{1,0:T(8,128)S(1)} %bitcast.232), channel_id=1, source_target_pairs={{0,12},{1,44},{2,76},{3,108},{4,8},{5,40},{6,72},{7,104},{8,4},{9,... | collective-permute-start | bytes 49160 | tf_op jit(solution)/shard_map/ppermute | solution.py:173
  190.9 10.3 %collective-permute-start.49 = (f32[64,64]{1,0:T(8,128)S(1)}, f32[64,64]{1,0:T(8,128)S(1)}, u32[]{:S(2)}, u32[]{:S(2)}) collective-permute-start(f32[64,64]{1,0:T(8,128)S(1)} %bitcast.231), channel_id=1, source_target_pairs={{0,16},{1,48},{2,80},{3,112},{4,20},{5,52},{6,84},{7,116},{8,24},{... | collective-permute-start | bytes 49160 | tf_op jit(solution)/shard_map/ppermute | solution.py:173
  195.2 6.0 %collective-permute-start.50 = (f32[64,64]{1,0:T(8,128)S(1)}, f32[64,64]{1,0:T(8,128)S(1)}, u32[]{:S(2)}, u32[]{:S(2)}) collective-permute-start(f32[64,64]{1,0:T(8,128)S(1)} %bitcast.230), channel_id=1, source_target_pairs={{0,20},{1,52},{2,84},{3,116},{4,16},{5,48},{6,80},{7,112},{8,28},{... | collective-permute-start | bytes 49160 | tf_op jit(solution)/shard_map/ppermute | solution.py:173
  195.2 7.1 %collective-permute-start.51 = (f32[64,64]{1,0:T(8,128)S(1)}, f32[64,64]{1,0:T(8,128)S(1)}, u32[]{:S(2)}, u32[]{:S(2)}) collective-permute-start(f32[64,64]{1,0:T(8,128)S(1)} %bitcast.229), channel_id=1, source_target_pairs={{0,24},{1,56},{2,88},{3,120},{4,28},{5,60},{6,92},{7,124},{8,16},{... | collective-permute-start | bytes 49160 | tf_op jit(solution)/shard_map/ppermute | solution.py:173
  200.4 6.7 %collective-permute-start.52 = (f32[64,64]{1,0:T(8,128)S(1)}, f32[64,64]{1,0:T(8,128)S(1)}, u32[]{:S(2)}, u32[]{:S(2)}) collective-permute-start(f32[64,64]{1,0:T(8,128)S(1)} %bitcast.228), channel_id=1, source_target_pairs={{0,28},{1,60},{2,92},{3,124},{4,24},{5,56},{6,88},{7,120},{8,20},{... | collective-permute-start | bytes 49160 | tf_op jit(solution)/shard_map/ppermute | solution.py:173
  (9 other events, 75.9 us)

commit v2 on v0

v2 whole, which is shorter than its diff:
```python
import jax
import jax.numpy as jnp
from jax import lax
from jax.experimental import pallas as pl
from jax.experimental.pallas import tpu as pltpu
from jax.sharding import PartitionSpec as P

PANEL = 512
CLUSTER = 128
COSTS = (40, 6, 4, 4)
PIECES = ((0, 128), (128, 384))
ROWS = 64

CELLS = [(zh, x, y) for zh in range(2) for x in range(4) for y in range(4)]


def pts_index(zh, x, y):
    return (zh * 4 + x) * 4 + y


def plane_step(step, swapped):
    pairs = []
    for z, x, y in CELLS:
        for j in range(4):
            if (j % 2 == 0) != swapped:
                to = pts_index(z, (x + step) % 4, y)
            else:
                to = pts_index(z, x, (y + step) % 4)
            pairs.append((pts_index(z, x, y) * 4 + j, to * 4 + j))
    return pairs


def other_high(k):
    return [
        (pts_index(z, x, y) * 4 + j, pts_index(1 - z, x, y) * 4 + (j ^ k))
        for z, x, y in CELLS
        for j in range(4)
    ]


OTHER_CHIP = [(k, k ^ 2) for k in range(4)]
OTHER_CORE = [(k, k ^ 1) for k in range(4)]


def swap(k):
    return [
        ((8 * a + b) * 4 + j, (8 * j + b) * 4 + (a ^ k))
        for a in range(4)
        for b in range(8)
        for j in range(4)
    ]


EIGHTS = [[8 * a + b for b in range(8)] for a in range(4)]


def halves(value):
    first = value.astype(jnp.bfloat16)
    return first, (value - first.astype(jnp.float32)).astype(jnp.bfloat16)


def contract(a, b):
    def one(u, v):
        return lax.dot_general(u, v, (((0,), (0,)), ((), ())), preferred_element_type=jnp.float32)

    return one(a[0], b[0]) + (one(a[0], b[1]) + one(a[1], b[0]))


def multiply(a, b):
    def one(u, v):
        return jnp.dot(u, v, preferred_element_type=jnp.float32)

    return one(a[0], b[0]) + (one(a[0], b[1]) + one(a[1], b[0]))


def write_strips(place, product, outs):
    core, first, second = place[0], place[2], place[3]
    for k in range(4):
        for m in range(4):
            f, g = (first + k) % 4, (second + m) % 4
            strip = jnp.where(core == 0, 4 * f + g, 4 * g + f)
            outs[k][m] = product[pl.ds(pl.multiple_of(strip * 32, 32), 32), :]


def near_kernel(place, own, pair, product):
    panel = own.shape[1]
    thin = panel // 2
    a = halves(own[...])
    product[:, :panel] = contract(a, a) * 0.5

    @pl.when(place[0] == 0)
    def _():
        product[:, panel:] = contract(a, halves(pair[:, :thin]))

    @pl.when(place[0] != 0)
    def _():
        b = [part[:, thin:] for part in a]
        product[:, panel:] = contract(halves(pair[...]), b)


def across_kernel(place, own, pair, value, *refs):
    *others, out0, out1, out2, out3, product = refs
    half, width = value.shape
    rows = pl.ds(pl.multiple_of(place[1] * half, half), half)
    b = halves(value[...])
    start = product.shape[1] - 2 * width
    for other in others:
        product[:, :start] = other[...]
    product[:, start : start + width] = contract(halves(own[rows, :]), b)
    product[:, start + width :] = contract(halves(pair[rows, :]), b)
    write_strips(place, product, (out0, out1, out2, out3))


def inverse_kernel(
    place, inverse, pair_inverse, factor, pair_factor, near, near_low, far, far_low, above, pair_above, link, done
):
    panel = inverse.shape[0]
    start = pl.multiple_of(place[1] * 2 * panel, 2 * panel)
    copies = [
        pltpu.make_async_copy(factor.at[pl.ds(0, 2 * panel), :], above, done.at[0]),
        pltpu.make_async_copy(pair_factor.at[pl.ds(0, 2 * panel), :], pair_above, done.at[1]),
        pltpu.make_async_copy(factor.at[pl.ds(start, panel), :], link, done.at[2]),
    ]
    for copy in copies:
        copy.start()
    for copy in copies:
        copy.wait()
    d = halves(inverse[...])

    def put(high, low, rows, value):
        parts = halves(value)
        high[rows, :] = parts[0]
        low[rows, :] = parts[1]

    top, bottom = slice(0, panel), slice(panel, 2 * panel)

    @pl.when(place[0] == 0)
    def _():
        near[top, :], near_low[top, :] = d
        near[bottom, :] = jnp.zeros_like(d[0])
        near_low[bottom, :] = jnp.zeros_like(d[0])
        for rows in (top, bottom):
            put(far, far_low, rows, multiply(halves(above[rows, :]), d))

    @pl.when(place[0] != 0)
    def _():
        near[bottom, :], near_low[bottom, :] = d
        corner = -multiply(halves(pair_inverse[...]), halves(multiply(halves(link[...]), d)))
        put(near, near_low, top, corner)
        c = halves(corner)
        for rows in (top, bottom):
            value = multiply(halves(above[rows, :]), d) + multiply(halves(pair_above[rows, :]), c)
            put(far, far_low, rows, value)


def collect(place, held, value, far, other):
    j = place[4]
    held[j] = value[...]
    held[j ^ 2] = far[...]
    held[j ^ 1] = other[0]
    held[j ^ 3] = other[1]


def first_kernel(place, order, value, far, other, near, near_low, out, held, upper, ordered):
    part = value.shape[0]
    panel = near.shape[1]
    thin = panel // 2
    collect(place, held, value, far, other)

    def put(q, column, source, first, width):
        upper[part * q : part * (q + 1), column : column + width] = held[
            source, :, first : first + width
        ]

    for q in range(4):
        chip, core = divmod(q, 2)
        put(q, q * panel, q, 0, panel)
        if core == 0:
            put(q, (q + 1) * panel, q, panel, thin)
            put(q, (q + 1) * panel + thin, q + 1, panel, thin)
        else:
            upper[part * q : part * (q + 1), (q - 1) * panel : q * panel] = jnp.zeros(
                (part, panel), jnp.float32
            )
        for c in range(2):
            first = panel + thin
            for at, width in PIECES:
                column = (2 * (1 - chip) + c) * panel + at
                put(q, column, q if c == core else q ^ 1, first + width * (c != core), width)
                first += 2 * width
    for k in range(8):
        block = order[place[1] * 8 + k]
        ordered[:, k * CLUSTER : (k + 1) * CLUSTER] = upper[
            :, pl.ds(pl.multiple_of(block * CLUSTER, CLUSTER), CLUSTER)
        ]
    out[...] = multiply(halves(ordered[...]), (near[...], near_low[...]))


def less_far(place, value, got, got_pair, far, far_low, solved):
    panel = value.shape[1]
    solved[...] = value[...]

    @pl.when(place[1] != 0)
    def _():
        core = place[0]
        rows = [pl.ds(pl.multiple_of(c * panel, panel), panel) for c in (core, 1 - core)]
        total = value[...]
        for source, r in zip((got, got_pair), rows):
            total -= multiply(halves(source[...]), (far[r, :], far_low[r, :]))
        solved[...] = total


def pack(solved, out):
    left = lax.broadcasted_iota(jnp.int32, (32, 2 * ROWS), 1) < ROWS
    for g in range(4):
        low = solved[:32, g * 2 * ROWS : (g + 1) * 2 * ROWS]
        high = solved[32:, g * 2 * ROWS : (g + 1) * 2 * ROWS]
        out[2 * g] = jnp.where(left, low, pltpu.roll(high, ROWS, 1))
        out[2 * g + 1] = jnp.where(left, pltpu.roll(low, ROWS, 1), high)


def second_kernel(place, value, got, got_pair, far, far_low, solved, out):
    less_far(place, value, got, got_pair, far, far_low, solved)
    pack(solved, out)


def third_kernel(place, order, value, far, other, near, near_low, out, held, rows, ordered):
    part = value.shape[1] // 2
    collect(place, held, value, far, other)
    for a in range(4):
        for b in range(8):
            high, strip = a // 2, 8 * (a % 2) + b
            for q in range(2):
                start = 512 * q + 32 * strip + part * high
                rows[start : start + part, :] = held[a, b, part * q : part * (q + 1), :]
    for k in range(8):
        block = order[place[1] * 8 + k]
        taken = rows[pl.ds(pl.multiple_of((block % 8) * CLUSTER, CLUSTER), CLUSTER), :]
        ordered[k * CLUSTER : (k + 1) * CLUSTER, :] = jnp.where(
            block >= 8, pltpu.roll(taken, ROWS, 1), taken
        )
    out[...] = contract(halves(ordered[...]), (near[...], near_low[...]))[:ROWS]


def last_kernel(place, scale, result, turned, out, rows):
    for b in range(8):
        rows[64 * b : 64 * b + 32, :] = turned[b]
        rows[64 * b + 32 : 64 * b + 64, :] = pltpu.roll(turned[b], ROWS, 1)
    both = (result[...] + rows[...].T[:ROWS]) * scale[0]
    out[...] = jnp.where(place[5] <= place[4], both, 0.0)


def kernel_call(kernel, scalars, out_shape, scratch, cost, *arrays, after=(), large=(), large_outs=0):
    arrays = (*arrays, *large)
    inputs = len(scalars) + len(arrays)

    def body(*refs):
        kernel(*refs[:inputs], *refs[inputs + len(after) :])

    vmem = pl.BlockSpec(memory_space=pltpu.VMEM)
    smem = pl.BlockSpec(memory_space=pltpu.SMEM)
    several = isinstance(out_shape, list)
    return pl.pallas_call(
        body,
        out_shape=out_shape,
        in_specs=[smem] * len(scalars)
        + [vmem] * (len(arrays) - len(large))
        + [pl.BlockSpec(memory_space=pl.ANY)] * (len(large) + len(after)),
        out_specs=[vmem] * (len(out_shape) - large_outs)
        + [pl.BlockSpec(memory_space=pl.ANY)] * large_outs
        if several
        else vmem,
        scratch_shapes=[pltpu.VMEM(shape, jnp.float32) for shape in scratch]
        + [pltpu.SemaphoreType.DMA((len(scratch),))] * bool(large),
        compiler_params=pltpu.CompilerParams(vmem_limit_bytes=40 << 20),
        cost_estimate=pl.CostEstimate(flops=int(cost * 1e9), bytes_accessed=int(cost * 3e6), transcendentals=0),
    )(*scalars, *arrays, *after)


def shape(*dims, dtype=jnp.float32):
    return jax.ShapeDtypeStruct(dims, dtype)


def strips(kernel, width, place, cost, *arrays, extra=(), **options):
    panel = arrays[0].shape[1]
    outs = [shape(4, panel // 16, width)] * 4
    return kernel_call(kernel, [place], [*outs, *extra], [(panel, width)], cost, *arrays, **options)


def sum_along(values, swapped):
    total = values[0]
    for step in (1, 3, 2):
        total += lax.ppermute(values[step], ("pts", "lm"), plane_step(step, swapped))
    return total


def per_device(kernel_features, factor, diag_inverse, block_order):
    own = kernel_features
    points, panel = own.shape
    half, thin, part = points // 2, panel // 2, panel // 32
    i, j = lax.axis_index("pts"), lax.axis_index("lm")
    chip, core = j // 2, j % 2
    high, x, y = i // 16, (i // 4) % 4, i % 4
    first_core = core == 0
    place = jnp.stack(
        [core, chip, jnp.where(first_core, x, y), jnp.where(first_core, y, x), j, i // 8]
    ).astype(jnp.int32)
    order = block_order

    pair = lax.ppermute(own, "lm", OTHER_CORE)
    sent = lax.dynamic_slice_in_dim(own, (1 - chip) * half, half)
    across = [lax.ppermute(sent[:, at : at + w], "lm", OTHER_CHIP) for at, w in PIECES]

    product = kernel_call(
        near_kernel, [place], shape(panel, panel + thin), [], COSTS[0], own, pair
    )
    widths = [panel + thin + 2 * PIECES[0][1], 2 * PIECES[1][1]]
    early = strips(across_kernel, widths[0], place, COSTS[1], own, pair, across[0], product)
    early_sum = sum_along(early, False)
    late = strips(across_kernel, widths[1], place, COSTS[3], own, pair, across[1], after=(early_sum,))
    late_sum = sum_along(late, False)
    parts = [jnp.concatenate([a, b], -1) for a, b in zip(early_sum, late_sum)]
    inverse = diag_inverse[0]
    near, near_low, far, far_low = kernel_call(
        inverse_kernel,
        [place],
        [shape(2 * panel, panel, dtype=jnp.bfloat16)] * 4,
        [(2 * panel, panel), (2 * panel, panel), (panel, panel)],
        COSTS[2],
        inverse,
        lax.ppermute(inverse, "lm", OTHER_CORE),
        large=(factor, lax.ppermute(factor[: 2 * panel], "lm", OTHER_CORE)),
        after=(early[0],),
    )
    parts, far_low = lax.optimization_barrier((parts, far_low))
    mine = sum_along(parts, True)
    here, there = lax.optimization_barrier(
        tuple(lax.dynamic_slice_in_dim(mine, at * part, part) for at in (high, 1 - high))
    )
    far_here = lax.ppermute(here, "lm", OTHER_CHIP)
    far_there = lax.ppermute(there, ("pts", "lm"), other_high(2))
    here += lax.ppermute(there, ("pts", "lm"), other_high(0))
    away = far_here + far_there

    def spread(value, away):
        return value, away, lax.ppermute(jnp.stack([value, away]), "lm", OTHER_CORE)

    def hop(value):
        got = lax.ppermute(value, "lm", OTHER_CHIP)
        return value, got, lax.ppermute(got, "lm", OTHER_CORE), far, far_low

    def flipped(packed, *kinds):
        got = lax.all_to_all(packed, "pts", 0, 0, axis_index_groups=EIGHTS, tiled=True)
        return [lax.ppermute(got, ("pts", "lm"), swap(k)) for k in kinds]

    square, packed = shape(ROWS, panel), shape(8, 32, 2 * ROWS)
    flops = 2
    width = here.shape[1]
    value = kernel_call(
        first_kernel,
        [place, order],
        square,
        [(4, part, width), (ROWS, 4 * panel), (ROWS, 2 * panel)],
        flops,
        *spread(here, away),
        near,
        near_low,
    )
    _, value = kernel_call(second_kernel, [place], [square, packed], [], flops, *hop(value))
    value = kernel_call(
        third_kernel,
        [place, order],
        square,
        [(4, 8, 32, 2 * ROWS), (2 * panel, 2 * ROWS), (2 * panel, 2 * ROWS)],
        flops,
        *spread(*flipped(value, 0, 2)),
        near,
        near_low,
    )
    result, value = kernel_call(second_kernel, [place], [square, packed], [], flops, *hop(value))
    scale = jnp.full((1,), 1.0 / (points * lax.axis_size("pts")), jnp.float32)
    return kernel_call(
        last_kernel, [place, scale], square, [(panel, 2 * ROWS)], 0, result, *flipped(value, 0)
    )


def solution(mesh):
    placed = (P("pts", "lm"), P(None, "lm"), P("lm", None, None), P())
    return jax.shard_map(
        per_device, mesh=mesh, in_specs=placed, out_specs=P("pts", "lm"), check_vma=False
    )
```

time: 705 us -> 141 us (0.20)
  the two profiles are of different devices: /device:TPU:0 before, /device:TPU:1 now
where the time goes in v2:
time: 141 us
  waiting for transfers between devices  54.1 us (38%)
  starting transfers between devices  37 us (26%)
  Pallas kernels  25.8 us (18%)
  blocking collectives  16.5 us (12%)
  local copies, waits for them, and re-layouts  4.36 us (3%)
  other arithmetic  2.78 us (2%)
    pallas_call x9, Pallas kernels, kernel_call(): pl.pallas_call(body, out_shape=out_shape, in_specs=[smem] * len(scalars)...  25.8 us
    ppermute x9, waiting for transfers between devices, sum_along(): lax.ppermute(values[step], ('pts', 'lm'), plane_step(step, swapped))  19 us
    all_to_all x2, blocking collectives, flipped(): lax.all_to_all(packed, 'pts', 0, 0, axis_index_groups=EIGHTS, tiled=True)  16.5 us
    ppermute x3, starting transfers between devices, flipped(): return [lax.ppermute(got, ('pts', 'lm'), swap(k)) for k in kinds]  11.5 us
    ppermute x9, starting transfers between devices, sum_along(): lax.ppermute(values[step], ('pts', 'lm'), plane_step(step, swapped))  11.3 us
    ppermute x3, waiting for transfers between devices, flipped(): return [lax.ppermute(got, ('pts', 'lm'), swap(k)) for k in kinds]  10.7 us
    ppermute x2, waiting for transfers between devices, hop(): got = lax.ppermute(value, 'lm', OTHER_CHIP)  9.11 us
    ppermute x2, waiting for transfers between devices, per_device(): lax.ppermute(sent[:, at:at + w], 'lm', OTHER_CHIP)  5 us
  transfers between devices with their start and end apart: 26, of which 20 were waited for; matrix products, arithmetic and copies ran while one was open for 4% of the time, Pallas kernels for 14%

profile of v2, /device:TPU:1, one launch (start us, length us, event | category | flops | bytes accessed | tf_op | source)
XLA Modules:
  0.0 140.9 jit_solution(15991695061897421676)
XLA Ops:
  0.0 1.4 %collective-permute-start = (f32[1024,512]{1,0:T(8,128)}, f32[1024,512]{1,0:T(8,128)}, u32[]{:S(2)}, u32[]{:S(2)}) collective-permute-start(f32[1024,512]{1,0:T(8,128)} %refs_1_.7), channel_id=1, source_target_pairs={{0,1},{1,0},{2,3},{3,2},{4,5},{5,4},{6,7},{7,6},{8,9},{9,8},{10,11... | collective-permute-start | bytes 6291464 | tf_op jit(solution)/shard_map/ppermute | solution.py:310
  1.4 1.0 constant_dynamic-slice_fusion
  2.4 1.8 %collective-permute-start.1 = (f32[512,128]{1,0:T(8,128)S(1)}, f32[512,128]{1,0:T(8,128)S(1)}, u32[]{:S(2)}, u32[]{:S(2)}) collective-permute-start(f32[512,128]{1,0:T(8,128)S(1)} %constant_dynamic-slice_fusion), channel_id=1, source_target_pairs={{0,2},{1,3},{2,0},{3,1},{4,6},{5,7},{6,4},{7,5},{8,10},{9,11},{10,... | collective-permute-start | bytes 786440 | tf_op jit(solution)/shard_map/ppermute | solution.py:312
  4.2 3.1 %slice.11 = f32[1024,512]{1,0:T(8,128)} slice(f32[2048,512]{1,0:T(8,128)} %refs_3_.1), slice={[0:1024], [0:512]} | slice | bytes 4194304 | tf_op jit(solution)/shard_map/slice | solution.py:332
  7.7 4.5 %shard_map.46.refs_4_ = f32[512,768]{1,0:T(8,128)S(1)} custom-call(s32[6]{0:T(128)S(1)} %stack.45.refs_0_, f32[1024,512]{1,0:T(8,128)S(1)} %copy-done.1, f32[1024,512]{1,0:T(8,128)} %collective-permute-done.refs_2_), custom_call_target="tpu_custom_call" | custom-call | flops 40000000000 | bytes 120000000 | tf_op jit(solution)/shard_map/pallas_call | solution.py:263
  12.2 3.8 %shard_map.47 = (f32[4,32,1024]{2,1,0:T(8,128)S(1)}, f32[4,32,1024]{2,1,0:T(8,128)S(1)}, f32[4,32,1024]{2,1,0:T(8,128)}, f32[4,32,1024]{2,1,0:T(8,128)}) custom-call(s32[6]{0:T(128)S(1)} %stack.45.refs_0_, f32[1024,512]{1,0:T(8,128)S(1)} %copy-done.1, f32[1024,512]{1,0:T(8,128)} %collective-permute-done.refs_2_, ...), custom_call_target="tpu_custom_call" | custom-call | flops 6000000000 | bytes 18000000 | tf_op jit(solution)/shard_map/pallas_call | solution.py:263
  15.9 2.9 %collective-permute-start.4 = (f32[4,32,1024]{2,1,0:T(8,128)}, f32[4,32,1024]{2,1,0:T(8,128)}, u32[]{:S(2)}, u32[]{:S(2)}) collective-permute-start(f32[4,32,1024]{2,1,0:T(8,128)} %get-tuple-element.30), channel_id=1, source_target_pairs={{0,32},{1,9},{2,34},{3,11},{4,36},{5,13},{6,38},{7,15},{8,40},{9,1... | collective-permute-start | bytes 1572872 | tf_op jit(solution)/shard_map/ppermute | solution.py:293
  20.5 5.6 %collective-permute-done.4 = f32[4,32,1024]{2,1,0:T(8,128)} collective-permute-done((f32[4,32,1024]{2,1,0:T(8,128)}, f32[4,32,1024]{2,1,0:T(8,128)}, u32[]{:S(2)}, u32[]{:S(2)}) %collective-permute-start.4) | collective-permute-done | bytes 524320 | tf_op jit(solution)/shard_map/ppermute | solution.py:293
  26.1 1.1 collective-permute-start.9
  27.2 4.9 %collective-permute-done.3 = f32[4,32,1024]{2,1,0:T(8,128)} collective-permute-done((f32[4,32,1024]{2,1,0:T(8,128)}, f32[4,32,1024]{2,1,0:T(8,128)}, u32[]{:S(2)}, u32[]{:S(2)}) %collective-permute-start.3) | collective-permute-done | bytes 524320 | tf_op jit(solution)/shard_map/ppermute | solution.py:293
  32.1 1.6 %add_add_fusion.refs_4_ = f32[4,32,1024]{2,1,0:T(8,128)S(1)} fusion(f32[4,32,1024]{2,1,0:T(8,128)} %collective-permute-done.4, f32[4,32,1024]{2,1,0:T(8,128)} %collective-permute-done.3, f32[4,32,1024]{2,1,0:T(8,128)S(1)} %get-tuple-element.27.refs_5_, f32[4,32,1024]{2,1,0:T(8,128)} %collective-permute-done.2), kind=kLoop, calls=%fused_computation | loop fusion | flops 393216 | bytes 2621440 | tf_op jit(solution)/shard_map/add | solution.py:293
  33.7 5.0 %collective-permute-done.5.refs_3_ = f32[512,384]{1,0:T(8,128)S(1)} collective-permute-done((f32[512,384]{1,0:T(8,128)S(1)}, f32[512,384]{1,0:T(8,128)S(1)}, u32[]{:S(2)}, u32[]{:S(2)}) %collective-permute-start.5) | collective-permute-done | bytes 786464 | tf_op jit(solution)/shard_map/ppermute | solution.py:312
  38.7 3.5 %shard_map.48 = (f32[4,32,768]{2,1,0:T(8,128)S(1)}, f32[4,32,768]{2,1,0:T(8,128)S(1)}, f32[4,32,768]{2,1,0:T(8,128)S(1)}, f32[4,32,768]{2,1,0:T(8,128)S(1)}) custom-call(s32[6]{0:T(128)S(1)} %stack.45.refs_0_, f32[1024,512]{1,0:T(8,128)S(1)} %copy-done.1, f32[1024,512]{1,0:T(8,128)} %collective-permute-done.refs_2_, ...), custom_call_target="tpu_custom_call" | custom-call | flops 4000000000 | bytes 12000000 | tf_op jit(solution)/shard_map/pallas_call | solution.py:263
  42.3 1.9 %collective-permute-start.7 = (f32[4,32,768]{2,1,0:T(8,128)S(1)}, f32[4,32,768]{2,1,0:T(8,128)S(1)}, u32[]{:S(2)}, u32[]{:S(2)}) collective-permute-start(f32[4,32,768]{2,1,0:T(8,128)S(1)} %get-tuple-element.33), channel_id=1, source_target_pairs={{0,48},{1,13},{2,50},{3,15},{4,52},{5,1},{6,54},{7,3},{8,56},{9,5}... | collective-permute-start | bytes 1179656 | tf_op jit(solution)/shard_map/ppermute | solution.py:293
  44.2 8.0 %shard_map.49 = (bf16[1024,512]{1,0:T(8,128)(2,1)S(1)}, bf16[1024,512]{1,0:T(8,128)(2,1)S(1)}, bf16[1024,512]{1,0:T(8,128)(2,1)S(1)}, bf16[1024,512]{1,0:T(8,128)(2,1)S(1)}) custom-call(s32[6]{0:T(128)S(1)} %stack.45.refs_0_, f32[512,512]{1,0:T(8,128)S(1)} %bitcast.32, f32[512,512]{1,0:T(8,128)S(1)} %collective-permute-done.9.refs_2_, ...), custom_call_target="tpu_custom_call" | custom-call | flops 4000000000 | bytes 12000000 | tf_op jit(solution)/shard_map/pallas_call | solution.py:263
  52.3 1.5 %collective-permute-done.7 = f32[4,32,768]{2,1,0:T(8,128)S(1)} collective-permute-done((f32[4,32,768]{2,1,0:T(8,128)S(1)}, f32[4,32,768]{2,1,0:T(8,128)S(1)}, u32[]{:S(2)}, u32[]{:S(2)}) %collective-permute-start.7) | collective-permute-done | bytes 393248 | tf_op jit(solution)/shard_map/ppermute | solution.py:293
  53.8 1.1 collective-permute-done.6
  55.2 3.5 %collective-permute-start.13 = (f32[32,1792]{1,0:T(8,128)S(1)}, f32[32,1792]{1,0:T(8,128)S(1)}, u32[]{:S(2)}, u32[]{:S(2)}) collective-permute-start(f32[32,1792]{1,0:T(8,128)S(1)} %get-tuple-element.39), channel_id=1, source_target_pairs={{0,8},{1,33},{2,10},{3,35},{4,12},{5,37},{6,14},{7,39},{8,0},{9,41... | collective-permute-start | bytes 688136 | tf_op jit(solution)/shard_map/ppermute | solution.py:293
  58.7 0.9 collective-permute-start.12
  60.2 1.9 %collective-permute-done.13 = f32[32,1792]{1,0:T(8,128)S(1)} collective-permute-done((f32[32,1792]{1,0:T(8,128)S(1)}, f32[32,1792]{1,0:T(8,128)S(1)}, u32[]{:S(2)}, u32[]{:S(2)}) %collective-permute-start.13) | collective-permute-done | bytes 229408 | tf_op jit(solution)/shard_map/ppermute | solution.py:293
  62.1 2.8 %collective-permute-done.12 = f32[32,1792]{1,0:T(8,128)S(1)} collective-permute-done((f32[32,1792]{1,0:T(8,128)S(1)}, f32[32,1792]{1,0:T(8,128)S(1)}, u32[]{:S(2)}, u32[]{:S(2)}) %collective-permute-start.12) | collective-permute-done | bytes 229408 | tf_op jit(solution)/shard_map/ppermute | solution.py:293
  64.9 1.2 collective-permute-done.11
  66.1 1.0 add_add_fusion.2
  67.1 3.4 %collective-permute-start.14 = (f32[16,1792]{1,0:T(8,128)S(1)}, f32[16,1792]{1,0:T(8,128)S(1)}, u32[]{:S(2)}, u32[]{:S(2)}) collective-permute-start(f32[16,1792]{1,0:T(8,128)S(1)} %get-tuple-element.41), channel_id=1, source_target_pairs={{0,64},{1,65},{2,66},{3,67},{4,68},{5,69},{6,70},{7,71},{8,72},{9,... | collective-permute-start | bytes 344072 | tf_op jit(solution)/shard_map/ppermute | solution.py:342
  70.9 1.8 %collective-permute-done.14 = f32[16,1792]{1,0:T(8,128)S(1)} collective-permute-done((f32[16,1792]{1,0:T(8,128)S(1)}, f32[16,1792]{1,0:T(8,128)S(1)}, u32[]{:S(2)}, u32[]{:S(2)}) %collective-permute-start.14) | collective-permute-done | bytes 114720 | tf_op jit(solution)/shard_map/ppermute | solution.py:342
  72.7 1.4 %collective-permute-done.15 = f32[16,1792]{1,0:T(8,128)S(1)} collective-permute-done((f32[16,1792]{1,0:T(8,128)S(1)}, f32[16,1792]{1,0:T(8,128)S(1)}, u32[]{:S(2)}, u32[]{:S(2)}) %collective-permute-start.15) | collective-permute-done | bytes 114720 | tf_op jit(solution)/shard_map/ppermute | solution.py:340
  74.2 2.4 %collective-permute-done.16 = f32[16,1792]{1,0:T(8,128)S(1)} collective-permute-done((f32[16,1792]{1,0:T(8,128)S(1)}, f32[16,1792]{1,0:T(8,128)S(1)}, u32[]{:S(2)}, u32[]{:S(2)}) %collective-permute-start.16) | collective-permute-done | bytes 114720 | tf_op jit(solution)/shard_map/ppermute | solution.py:341
  76.6 2.9 %collective-permute-start.17 = (f32[2,16,1792]{2,1,0:T(8,128)S(1)}, f32[2,16,1792]{2,1,0:T(8,128)S(1)}, u32[]{:S(2)}, u32[]{:S(2)}) collective-permute-start(f32[2,16,1792]{2,1,0:T(8,128)S(1)} %pad_maximum_fusion.5), channel_id=1, source_target_pairs={{0,1},{1,0},{2,3},{3,2},{4,5},{5,4},{6,7},{7,6},{8,9},{9,8},{10,11... | collective-permute-start | bytes 688136 | tf_op jit(solution)/shard_map/ppermute | solution.py:346
  79.5 1.1 collective-permute-done.17.refs_4_
  80.7 1.2 shard_map.50.refs_1_
  82.5 4.2 %collective-permute-done.18.refs_2_ = f32[64,512]{1,0:T(8,128)S(1)} collective-permute-done((f32[64,512]{1,0:T(8,128)S(1)}, f32[64,512]{1,0:T(8,128)S(1)}, u32[]{:S(2)}, u32[]{:S(2)}) %collective-permute-start.18) | collective-permute-done | bytes 131104 | tf_op jit(solution)/shard_map/ppermute | solution.py:349
  86.7 1.2 collective-permute-start.19
  87.9 1.0 collective-permute-done.19.refs_3_
  88.9 1.2 shard_map.51
  90.1 8.6 %all_to_all.10 = f32[8,32,128]{2,1,0:T(8,128)S(1)} all-to-all(f32[8,32,128]{2,1,0:T(8,128)S(1)} %get-tuple-element.46), channel_id=1, replica_groups={{0,4,8,12,16,20,24,28},{32,36,40,44,48,52,56,60},{64,68,72,76,80,84,88,..., dimensions={0} | all-to-all | bytes 262144 | tf_op jit(solution)/shard_map/all_to_all | solution.py:353
  98.7 6.0 %collective-permute-start.20 = (f32[8,32,128]{2,1,0:T(8,128)S(1)}, f32[8,32,128]{2,1,0:T(8,128)S(1)}, u32[]{:S(2)}, u32[]{:S(2)}) collective-permute-start(f32[8,32,128]{2,1,0:T(8,128)S(1)} %all_to_all.10), channel_id=1, source_target_pairs={{0,0},{1,32},{2,64},{3,96},{4,4},{5,36},{6,68},{7,100},{8,8},{9,40... | collective-permute-start | bytes 393224 | tf_op jit(solution)/shard_map/ppermute | solution.py:354
  104.7 1.0 collective-permute-start.21
  105.7 1.9 %collective-permute-done.20.refs_2_ = f32[8,32,128]{2,1,0:T(8,128)S(1)} collective-permute-done((f32[8,32,128]{2,1,0:T(8,128)S(1)}, f32[8,32,128]{2,1,0:T(8,128)S(1)}, u32[]{:S(2)}, u32[]{:S(2)}) %collective-permute-start.20) | collective-permute-done | bytes 131104 | tf_op jit(solution)/shard_map/ppermute | solution.py:354
  107.6 5.4 %collective-permute-done.21.refs_3_ = f32[8,32,128]{2,1,0:T(8,128)S(1)} collective-permute-done((f32[8,32,128]{2,1,0:T(8,128)S(1)}, f32[8,32,128]{2,1,0:T(8,128)S(1)}, u32[]{:S(2)}, u32[]{:S(2)}) %collective-permute-start.21) | collective-permute-done | bytes 131104 | tf_op jit(solution)/shard_map/ppermute | solution.py:354
  113.2 1.5 %collective-permute-done.22.refs_4_ = f32[2,8,32,128]{3,2,1,0:T(8,128)S(1)} collective-permute-done((f32[2,8,32,128]{3,2,1,0:T(8,128)S(1)}, f32[2,8,32,128]{3,2,1,0:T(8,128)S(1)}, u32[]{:S(2)}, u32[]{:S(2)}) %collective-permute-start.22) | collective-permute-done | bytes 262176 | tf_op jit(solution)/shard_map/ppermute | solution.py:346
  114.7 1.5 %shard_map.52.refs_1_ = f32[64,512]{1,0:T(8,128)S(1)} custom-call(s32[6]{0:T(128)S(1)} %stack.45.refs_0_, s32[16]{0:T(128)S(1)} %copy-done.3, f32[8,32,128]{2,1,0:T(8,128)S(1)} %collective-permute-done.20.refs_2_, f32[8,32,128]{2,1,0:T(8,128)S(1)} %collective-permute-done.21.refs_3_, f32[2,8,32,128]{3,2,1,0:T(8,128)S(1)} %collective-permute-done.22.refs_4_, ...), custom_call_target="tpu_custom_call" | custom-call | flops 2000000000 | bytes 6000000 | tf_op jit(solution)/shard_map/pallas_call | solution.py:263
  116.3 4.9 %collective-permute-done.23.refs_2_ = f32[64,512]{1,0:T(8,128)S(1)} collective-permute-done((f32[64,512]{1,0:T(8,128)S(1)}, f32[64,512]{1,0:T(8,128)S(1)}, u32[]{:S(2)}, u32[]{:S(2)}) %collective-permute-start.23) | collective-permute-done | bytes 131104 | tf_op jit(solution)/shard_map/ppermute | solution.py:349
  121.3 1.0 collective-permute-start.24
  122.2 1.0 collective-permute-done.24.refs_3_
  123.9 7.8 %all_to_all.11 = f32[8,32,128]{2,1,0:T(8,128)S(1)} all-to-all(f32[8,32,128]{2,1,0:T(8,128)S(1)} %get-tuple-element.48), channel_id=1, replica_groups={{0,4,8,12,16,20,24,28},{32,36,40,44,48,52,56,60},{64,68,72,76,80,84,88,..., dimensions={0} | all-to-all | bytes 262144 | tf_op jit(solution)/shard_map/all_to_all | solution.py:353
  131.7 4.5 %collective-permute-start.25 = (f32[8,32,128]{2,1,0:T(8,128)S(1)}, f32[8,32,128]{2,1,0:T(8,128)S(1)}, u32[]{:S(2)}, u32[]{:S(2)}) collective-permute-start(f32[8,32,128]{2,1,0:T(8,128)S(1)} %all_to_all.11), channel_id=1, source_target_pairs={{0,0},{1,32},{2,64},{3,96},{4,4},{5,36},{6,68},{7,100},{8,8},{9,40... | collective-permute-start | bytes 393224 | tf_op jit(solution)/shard_map/ppermute | solution.py:354
  136.2 3.3 %collective-permute-done.25.refs_3_ = f32[8,32,128]{2,1,0:T(8,128)S(1)} collective-permute-done((f32[8,32,128]{2,1,0:T(8,128)S(1)}, f32[8,32,128]{2,1,0:T(8,128)S(1)}, u32[]{:S(2)}, u32[]{:S(2)}) %collective-permute-start.25) | collective-permute-done | bytes 131104 | tf_op jit(solution)/shard_map/ppermute | solution.py:354
  139.5 1.4 shard_map.54
  (51 shorter events, 4.8 us)
Async XLA Ops:
  0.0 7.7 %collective-permute-start = (f32[1024,512]{1,0:T(8,128)}, f32[1024,512]{1,0:T(8,128)}, u32[]{:S(2)}, u32[]{:S(2)}) collective-permute-start(f32[1024,512]{1,0:T(8,128)} %refs_1_.7), channel_id=1, source_target_pairs={{0,1},{1,0},{2,3},{3,2},{4,5},{5,4},{6,7},{7,6},{8,9},{9,8},{10,11... | collective-permute-start | bytes 6291464 | tf_op jit(solution)/shard_map/ppermute | solution.py:310
  2.4 5.3 %copy-start.1 = (f32[1024,512]{1,0:T(8,128)S(1)}, f32[1024,512]{1,0:T(8,128)}, u32[]{:S(2)}) copy-start(f32[1024,512]{1,0:T(8,128)} %refs_1_.7) | copy-start | bytes 6291460
  2.4 9.8 %collective-permute-start.1 = (f32[512,128]{1,0:T(8,128)S(1)}, f32[512,128]{1,0:T(8,128)S(1)}, u32[]{:S(2)}, u32[]{:S(2)}) collective-permute-start(f32[512,128]{1,0:T(8,128)S(1)} %constant_dynamic-slice_fusion), channel_id=1, source_target_pairs={{0,2},{1,3},{2,0},{3,1},{4,6},{5,7},{6,4},{7,5},{8,10},{9,11},{10,... | collective-permute-start | bytes 786440 | tf_op jit(solution)/shard_map/ppermute | solution.py:312
  7.3 36.9 %collective-permute-start.10 = (f32[1024,512]{1,0:T(8,128)}, f32[1024,512]{1,0:T(8,128)}, u32[]{:S(2)}, u32[]{:S(2)}) collective-permute-start(f32[1024,512]{1,0:T(8,128)} %slice.11), channel_id=1, source_target_pairs={{0,1},{1,0},{2,3},{3,2},{4,5},{5,4},{6,7},{7,6},{8,9},{9,8},{10,11... | collective-permute-start | bytes 6291464 | tf_op jit(solution)/shard_map/ppermute | solution.py:332
  15.9 10.2 %collective-permute-start.4 = (f32[4,32,1024]{2,1,0:T(8,128)}, f32[4,32,1024]{2,1,0:T(8,128)}, u32[]{:S(2)}, u32[]{:S(2)}) collective-permute-start(f32[4,32,1024]{2,1,0:T(8,128)} %get-tuple-element.30), channel_id=1, source_target_pairs={{0,32},{1,9},{2,34},{3,11},{4,36},{5,13},{6,38},{7,15},{8,40},{9,1... | collective-permute-start | bytes 1572872 | tf_op jit(solution)/shard_map/ppermute | solution.py:293
  18.9 13.2 %collective-permute-start.3 = (f32[4,32,1024]{2,1,0:T(8,128)}, f32[4,32,1024]{2,1,0:T(8,128)}, u32[]{:S(2)}, u32[]{:S(2)}) collective-permute-start(f32[4,32,1024]{2,1,0:T(8,128)} %get-tuple-element.29), channel_id=1, source_target_pairs={{0,48},{1,13},{2,50},{3,15},{4,52},{5,1},{6,54},{7,3},{8,56},{9,5}... | collective-permute-start | bytes 1572872 | tf_op jit(solution)/shard_map/ppermute | solution.py:293
  19.6 12.5 %collective-permute-start.2 = (f32[4,32,1024]{2,1,0:T(8,128)S(1)}, f32[4,32,1024]{2,1,0:T(8,128)}, u32[]{:S(2)}, u32[]{:S(2)}) collective-permute-start(f32[4,32,1024]{2,1,0:T(8,128)S(1)} %get-tuple-element.28), channel_id=1, source_target_pairs={{0,16},{1,5},{2,18},{3,7},{4,20},{5,9},{6,22},{7,11},{8,24},{9,13}... | collective-permute-start | bytes 1572872 | tf_op jit(solution)/shard_map/ppermute | solution.py:293
  20.4 18.3 %collective-permute-start.5 = (f32[512,384]{1,0:T(8,128)S(1)}, f32[512,384]{1,0:T(8,128)S(1)}, u32[]{:S(2)}, u32[]{:S(2)}) collective-permute-start(f32[512,384]{1,0:T(8,128)S(1)} %dynamic-slice.1), channel_id=1, source_target_pairs={{0,2},{1,3},{2,0},{3,1},{4,6},{5,7},{6,4},{7,5},{8,10},{9,11},{10,... | collective-permute-start | bytes 2359304 | tf_op jit(solution)/shard_map/ppermute | solution.py:312
  26.1 18.0 %collective-permute-start.9 = (f32[512,512]{1,0:T(8,128)}, f32[512,512]{1,0:T(8,128)S(1)}, u32[]{:S(2)}, u32[]{:S(2)}) collective-permute-start(f32[512,512]{1,0:T(8,128)} %bitcast.31), channel_id=1, source_target_pairs={{0,1},{1,0},{2,3},{3,2},{4,5},{5,4},{6,7},{7,6},{8,9},{9,8},{10,11... | collective-permute-start | bytes 3145736 | tf_op jit(solution)/shard_map/ppermute | solution.py:331
  33.6 10.5 %copy-start = (f32[2048,512]{1,0:T(8,128)S(1)}, f32[2048,512]{1,0:T(8,128)}, u32[]{:S(2)}) copy-start(f32[2048,512]{1,0:T(8,128)} %refs_3_.1) | copy-start | bytes 12582916
  33.7 10.5 %copy-start.2 = (f32[1,512,512]{2,1,0:T(8,128)S(1)}, f32[1,512,512]{2,1,0:T(8,128)}, u32[]{:S(2)}) copy-start(f32[1,512,512]{2,1,0:T(8,128)} %param.6) | copy-start | bytes 3145732
  42.2 10.1 %collective-permute-start.8 = (f32[4,32,768]{2,1,0:T(8,128)S(1)}, f32[4,32,768]{2,1,0:T(8,128)S(1)}, u32[]{:S(2)}, u32[]{:S(2)}) collective-permute-start(f32[4,32,768]{2,1,0:T(8,128)S(1)} %get-tuple-element.34), channel_id=1, source_target_pairs={{0,32},{1,9},{2,34},{3,11},{4,36},{5,13},{6,38},{7,15},{8,40},{9,1... | collective-permute-start | bytes 1179656 | tf_op jit(solution)/shard_map/ppermute | solution.py:293
  42.3 11.5 %collective-permute-start.7 = (f32[4,32,768]{2,1,0:T(8,128)S(1)}, f32[4,32,768]{2,1,0:T(8,128)S(1)}, u32[]{:S(2)}, u32[]{:S(2)}) collective-permute-start(f32[4,32,768]{2,1,0:T(8,128)S(1)} %get-tuple-element.33), channel_id=1, source_target_pairs={{0,48},{1,13},{2,50},{3,15},{4,52},{5,1},{6,54},{7,3},{8,56},{9,5}... | collective-permute-start | bytes 1179656 | tf_op jit(solution)/shard_map/ppermute | solution.py:293
  44.2 10.8 %collective-permute-start.6 = (f32[4,32,768]{2,1,0:T(8,128)S(1)}, f32[4,32,768]{2,1,0:T(8,128)S(1)}, u32[]{:S(2)}, u32[]{:S(2)}) collective-permute-start(f32[4,32,768]{2,1,0:T(8,128)S(1)} %get-tuple-element.32), channel_id=1, source_target_pairs={{0,16},{1,5},{2,18},{3,7},{4,20},{5,9},{6,22},{7,11},{8,24},{9,13}... | collective-permute-start | bytes 1179656 | tf_op jit(solution)/shard_map/ppermute | solution.py:293
  52.2 2.9 %copy-start.4 = (bf16[1024,512]{1,0:T(8,128)(2,1)}, bf16[1024,512]{1,0:T(8,128)(2,1)S(1)}, u32[]{:S(2)}) copy-start(bf16[1024,512]{1,0:T(8,128)(2,1)S(1)} %get-tuple-element.43.refs_6_) | copy-start | bytes 3145732
  52.3 2.9 %copy-start.6 = (bf16[1024,512]{1,0:T(8,128)(2,1)}, bf16[1024,512]{1,0:T(8,128)(2,1)S(1)}, u32[]{:S(2)}) copy-start(bf16[1024,512]{1,0:T(8,128)(2,1)S(1)} %get-tuple-element.44.refs_4_) | copy-start | bytes 3145732
  52.3 2.9 %copy-start.8 = (bf16[1024,512]{1,0:T(8,128)(2,1)}, bf16[1024,512]{1,0:T(8,128)(2,1)S(1)}, u32[]{:S(2)}) copy-start(bf16[1024,512]{1,0:T(8,128)(2,1)S(1)} %get-tuple-element.45.refs_5_) | copy-start | bytes 3145732
  55.1 25.5 %copy-start.3 = (s32[16]{0:T(128)S(1)}, s32[16]{0:T(128)}, u32[]{:S(2)}) copy-start(s32[16]{0:T(128)} %refs_1_.9) | copy-start | bytes 196
  55.2 25.5 %copy-start.5 = (bf16[1024,512]{1,0:T(8,128)(2,1)S(1)}, bf16[1024,512]{1,0:T(8,128)(2,1)}, u32[]{:S(2)}) copy-start(bf16[1024,512]{1,0:T(8,128)(2,1)} %copy-done.4) | copy-start | bytes 3145732
  55.2 6.9 %collective-permute-start.13 = (f32[32,1792]{1,0:T(8,128)S(1)}, f32[32,1792]{1,0:T(8,128)S(1)}, u32[]{:S(2)}, u32[]{:S(2)}) collective-permute-start(f32[32,1792]{1,0:T(8,128)S(1)} %get-tuple-element.39), channel_id=1, source_target_pairs={{0,8},{1,33},{2,10},{3,35},{4,12},{5,37},{6,14},{7,39},{8,0},{9,41... | collective-permute-start | bytes 688136 | tf_op jit(solution)/shard_map/ppermute | solution.py:293
  58.7 6.2 %collective-permute-start.12 = (f32[32,1792]{1,0:T(8,128)S(1)}, f32[32,1792]{1,0:T(8,128)S(1)}, u32[]{:S(2)}, u32[]{:S(2)}) collective-permute-start(f32[32,1792]{1,0:T(8,128)S(1)} %get-tuple-element.38), channel_id=1, source_target_pairs={{0,12},{1,49},{2,14},{3,51},{4,0},{5,53},{6,2},{7,55},{8,4},{9,57}... | collective-permute-start | bytes 688136 | tf_op jit(solution)/shard_map/ppermute | solution.py:293
  59.6 6.5 %collective-permute-start.11 = (f32[32,1792]{1,0:T(8,128)S(1)}, f32[32,1792]{1,0:T(8,128)}, u32[]{:S(2)}, u32[]{:S(2)}) collective-permute-start(f32[32,1792]{1,0:T(8,128)S(1)} %get-tuple-element.37), channel_id=1, source_target_pairs={{0,4},{1,17},{2,6},{3,19},{4,8},{5,21},{6,10},{7,23},{8,12},{9,25}... | collective-permute-start | bytes 688136 | tf_op jit(solution)/shard_map/ppermute | solution.py:293
  67.1 5.6 %collective-permute-start.14 = (f32[16,1792]{1,0:T(8,128)S(1)}, f32[16,1792]{1,0:T(8,128)S(1)}, u32[]{:S(2)}, u32[]{:S(2)}) collective-permute-start(f32[16,1792]{1,0:T(8,128)S(1)} %get-tuple-element.41), channel_id=1, source_target_pairs={{0,64},{1,65},{2,66},{3,67},{4,68},{5,69},{6,70},{7,71},{8,72},{9,... | collective-permute-start | bytes 344072 | tf_op jit(solution)/shard_map/ppermute | solution.py:342
  70.5 3.6 %collective-permute-start.15 = (f32[16,1792]{1,0:T(8,128)S(1)}, f32[16,1792]{1,0:T(8,128)S(1)}, u32[]{:S(2)}, u32[]{:S(2)}) collective-permute-start(f32[16,1792]{1,0:T(8,128)S(1)} %get-tuple-element.40), channel_id=1, source_target_pairs={{0,2},{1,3},{2,0},{3,1},{4,6},{5,7},{6,4},{7,5},{8,10},{9,11},{10,... | collective-permute-start | bytes 344072 | tf_op jit(solution)/shard_map/ppermute | solution.py:340
  70.5 6.1 %collective-permute-start.16 = (f32[16,1792]{1,0:T(8,128)S(1)}, f32[16,1792]{1,0:T(8,128)S(1)}, u32[]{:S(2)}, u32[]{:S(2)}) collective-permute-start(f32[16,1792]{1,0:T(8,128)S(1)} %get-tuple-element.41), channel_id=1, source_target_pairs={{0,66},{1,67},{2,64},{3,65},{4,70},{5,71},{6,68},{7,69},{8,74},{9,... | collective-permute-start | bytes 344072 | tf_op jit(solution)/shard_map/ppermute | solution.py:341
  76.6 4.0 %collective-permute-start.17 = (f32[2,16,1792]{2,1,0:T(8,128)S(1)}, f32[2,16,1792]{2,1,0:T(8,128)S(1)}, u32[]{:S(2)}, u32[]{:S(2)}) collective-permute-start(f32[2,16,1792]{2,1,0:T(8,128)S(1)} %pad_maximum_fusion.5), channel_id=1, source_target_pairs={{0,1},{1,0},{2,3},{3,2},{4,5},{5,4},{6,7},{7,6},{8,9},{9,8},{10,11... | collective-permute-start | bytes 688136 | tf_op jit(solution)/shard_map/ppermute | solution.py:346
  80.7 8.2 %copy-start.7 = (bf16[1024,512]{1,0:T(8,128)(2,1)S(1)}, bf16[1024,512]{1,0:T(8,128)(2,1)}, u32[]{:S(2)}) copy-start(bf16[1024,512]{1,0:T(8,128)(2,1)} %copy-done.6) | copy-start | bytes 3145732
  80.7 8.2 %copy-start.9 = (bf16[1024,512]{1,0:T(8,128)(2,1)S(1)}, bf16[1024,512]{1,0:T(8,128)(2,1)}, u32[]{:S(2)}) copy-start(bf16[1024,512]{1,0:T(8,128)(2,1)} %copy-done.8) | copy-start | bytes 3145732
  81.9 4.8 %collective-permute-start.18 = (f32[64,512]{1,0:T(8,128)S(1)}, f32[64,512]{1,0:T(8,128)S(1)}, u32[]{:S(2)}, u32[]{:S(2)}) collective-permute-start(f32[64,512]{1,0:T(8,128)S(1)} %shard_map.50.refs_1_), channel_id=1, source_target_pairs={{0,2},{1,3},{2,0},{3,1},{4,6},{5,7},{6,4},{7,5},{8,10},{9,11},{10,... | collective-permute-start | bytes 393224 | tf_op jit(solution)/shard_map/ppermute | solution.py:349
  86.7 2.2 %collective-permute-start.19 = (f32[64,512]{1,0:T(8,128)S(1)}, f32[64,512]{1,0:T(8,128)S(1)}, u32[]{:S(2)}, u32[]{:S(2)}) collective-permute-start(f32[64,512]{1,0:T(8,128)S(1)} %collective-permute-done.18.refs_2_), channel_id=1, source_target_pairs={{0,1},{1,0},{2,3},{3,2},{4,5},{5,4},{6,7},{7,6},{8,9},{9,8},{10,11... | collective-permute-start | bytes 393224 | tf_op jit(solution)/shard_map/ppermute | solution.py:350
  98.7 8.9 %collective-permute-start.20 = (f32[8,32,128]{2,1,0:T(8,128)S(1)}, f32[8,32,128]{2,1,0:T(8,128)S(1)}, u32[]{:S(2)}, u32[]{:S(2)}) collective-permute-start(f32[8,32,128]{2,1,0:T(8,128)S(1)} %all_to_all.10), channel_id=1, source_target_pairs={{0,0},{1,32},{2,64},{3,96},{4,4},{5,36},{6,68},{7,100},{8,8},{9,40... | collective-permute-start | bytes 393224 | tf_op jit(solution)/shard_map/ppermute | solution.py:354
  104.7 8.4 %collective-permute-start.21 = (f32[8,32,128]{2,1,0:T(8,128)S(1)}, f32[8,32,128]{2,1,0:T(8,128)S(1)}, u32[]{:S(2)}, u32[]{:S(2)}) collective-permute-start(f32[8,32,128]{2,1,0:T(8,128)S(1)} %all_to_all.10), channel_id=1, source_target_pairs={{0,2},{1,34},{2,66},{3,98},{4,6},{5,38},{6,70},{7,102},{8,10},{9,4... | collective-permute-start | bytes 393224 | tf_op jit(solution)/shard_map/ppermute | solution.py:354
  113.1 1.6 %collective-permute-start.22 = (f32[2,8,32,128]{3,2,1,0:T(8,128)S(1)}, f32[2,8,32,128]{3,2,1,0:T(8,128)S(1)}, u32[]{:S(2)}, u32[]{:S(2)}) collective-permute-start(f32[2,8,32,128]{3,2,1,0:T(8,128)S(1)} %pad_maximum_fusion), channel_id=1, source_target_pairs={{0,1},{1,0},{2,3},{3,2},{4,5},{5,4},{6,7},{7,6},{8,9},{9,8},{10,11... | collective-permute-start | bytes 786440 | tf_op jit(solution)/shard_map/ppermute | solution.py:346
  116.2 5.0 %collective-permute-start.23 = (f32[64,512]{1,0:T(8,128)S(1)}, f32[64,512]{1,0:T(8,128)S(1)}, u32[]{:S(2)}, u32[]{:S(2)}) collective-permute-start(f32[64,512]{1,0:T(8,128)S(1)} %shard_map.52.refs_1_), channel_id=1, source_target_pairs={{0,2},{1,3},{2,0},{3,1},{4,6},{5,7},{6,4},{7,5},{8,10},{9,11},{10,... | collective-permute-start | bytes 393224 | tf_op jit(solution)/shard_map/ppermute | solution.py:349
  121.3 1.9 %collective-permute-start.24 = (f32[64,512]{1,0:T(8,128)S(1)}, f32[64,512]{1,0:T(8,128)S(1)}, u32[]{:S(2)}, u32[]{:S(2)}) collective-permute-start(f32[64,512]{1,0:T(8,128)S(1)} %collective-permute-done.23.refs_2_), channel_id=1, source_target_pairs={{0,1},{1,0},{2,3},{3,2},{4,5},{5,4},{6,7},{7,6},{8,9},{9,8},{10,11... | collective-permute-start | bytes 393224 | tf_op jit(solution)/shard_map/ppermute | solution.py:350
  131.7 7.8 %collective-permute-start.25 = (f32[8,32,128]{2,1,0:T(8,128)S(1)}, f32[8,32,128]{2,1,0:T(8,128)S(1)}, u32[]{:S(2)}, u32[]{:S(2)}) collective-permute-start(f32[8,32,128]{2,1,0:T(8,128)S(1)} %all_to_all.11), channel_id=1, source_target_pairs={{0,0},{1,32},{2,64},{3,96},{4,4},{5,36},{6,68},{7,100},{8,8},{9,40... | collective-permute-start | bytes 393224 | tf_op jit(solution)/shard_map/ppermute | solution.py:354

commit v3 on v2

--- a/solution.py
+++ b/solution.py
@@ -42,16 +42,10 @@
 OTHER_CORE = [(k, k ^ 1) for k in range(4)]
 
 
-def swap(k):
-    return [
-        ((8 * a + b) * 4 + j, (8 * j + b) * 4 + (a ^ k))
-        for a in range(4)
-        for b in range(8)
-        for j in range(4)
-    ]
-
-
-EIGHTS = [[8 * a + b for b in range(8)] for a in range(4)]
+def turn_groups():
+    rows = [((a, j), (j, a)) for a in range(4) for j in range(a + 1, 4)]
+    rows += [((a, a), (a + 1, a + 1)) for a in (0, 2)]
+    return [[(8 * a + b) * 4 + j for a, j in pair for b in range(8)] for pair in rows]
 
 
 def halves(value):
@@ -186,7 +180,7 @@
             first = panel + thin
             for at, width in PIECES:
                 column = (2 * (1 - chip) + c) * panel + at
-                put(q, column, q if c == core else q ^ 1, first + width * (c != core), width)
+                put(q, column, q if c != core else q ^ 1, first + width * (c == core), width)
                 first += 2 * width
     for k in range(8):
         block = order[place[1] * 8 + k]
@@ -210,18 +204,19 @@
         solved[...] = total
 
 
-def pack(solved, out):
+def pack(row, solved, out):
+    out[...] = jnp.zeros(out.shape, out.dtype)
     left = lax.broadcasted_iota(jnp.int32, (32, 2 * ROWS), 1) < ROWS
     for g in range(4):
         low = solved[:32, g * 2 * ROWS : (g + 1) * 2 * ROWS]
         high = solved[32:, g * 2 * ROWS : (g + 1) * 2 * ROWS]
-        out[2 * g] = jnp.where(left, low, pltpu.roll(high, ROWS, 1))
-        out[2 * g + 1] = jnp.where(left, pltpu.roll(low, ROWS, 1), high)
+        out[8 * row + 2 * g] = jnp.where(left, low, pltpu.roll(high, ROWS, 1))
+        out[8 * row + 2 * g + 1] = jnp.where(left, pltpu.roll(low, ROWS, 1), high)
 
 
 def second_kernel(place, value, got, got_pair, far, far_low, solved, out):
     less_far(place, value, got, got_pair, far, far_low, solved)
-    pack(solved, out)
+    pack(place[6], solved, out)
 
 
 def third_kernel(place, order, value, far, other, near, near_low, out, held, rows, ordered):
@@ -244,8 +239,9 @@
 
 def last_kernel(place, scale, result, turned, out, rows):
     for b in range(8):
-        rows[64 * b : 64 * b + 32, :] = turned[b]
-        rows[64 * b + 32 : 64 * b + 64, :] = pltpu.roll(turned[b], ROWS, 1)
+        block = turned[8 * place[6] + b]
+        rows[64 * b : 64 * b + 32, :] = block
+        rows[64 * b + 32 : 64 * b + 64, :] = pltpu.roll(block, ROWS, 1)
     both = (result[...] + rows[...].T[:ROWS]) * scale[0]
     out[...] = jnp.where(place[5] <= place[4], both, 0.0)
 
@@ -302,14 +298,17 @@
     chip, core = j // 2, j % 2
     high, x, y = i // 16, (i // 4) % 4, i % 4
     first_core = core == 0
+    group = i // 8
+    row = jnp.where(group < j, 1, jnp.where(group > j, 0, j % 2))
     place = jnp.stack(
-        [core, chip, jnp.where(first_core, x, y), jnp.where(first_core, y, x), j, i // 8]
+        [core, chip, jnp.where(first_core, x, y), jnp.where(first_core, y, x), j, group, row]
     ).astype(jnp.int32)
     order = block_order
 
     pair = lax.ppermute(own, "lm", OTHER_CORE)
     sent = lax.dynamic_slice_in_dim(own, (1 - chip) * half, half)
     across = [lax.ppermute(sent[:, at : at + w], "lm", OTHER_CHIP) for at, w in PIECES]
+    across = [lax.ppermute(value, "lm", OTHER_CORE) for value in across]
 
     product = kernel_call(
         near_kernel, [place], shape(panel, panel + thin), [], COSTS[0], own, pair
@@ -349,11 +348,11 @@
         got = lax.ppermute(value, "lm", OTHER_CHIP)
         return value, got, lax.ppermute(got, "lm", OTHER_CORE), far, far_low
 
-    def flipped(packed, *kinds):
-        got = lax.all_to_all(packed, "pts", 0, 0, axis_index_groups=EIGHTS, tiled=True)
-        return [lax.ppermute(got, ("pts", "lm"), swap(k)) for k in kinds]
-
-    square, packed = shape(ROWS, panel), shape(8, 32, 2 * ROWS)
+    def turned(packed):
+        groups = turn_groups()
+        return lax.all_to_all(packed, ("pts", "lm"), 0, 0, axis_index_groups=groups, tiled=True)
+
+    square, packed = shape(ROWS, panel), shape(16, 32, 2 * ROWS)
     flops = 2
     width = here.shape[1]
     value = kernel_call(
@@ -367,20 +366,22 @@
         near_low,
     )
     _, value = kernel_call(second_kernel, [place], [square, packed], [], flops, *hop(value))
+    value = lax.dynamic_slice_in_dim(turned(value), 8 * row, 8)
+    away = lax.ppermute(value, "lm", OTHER_CHIP)
     value = kernel_call(
         third_kernel,
         [place, order],
         square,
         [(4, 8, 32, 2 * ROWS), (2 * panel, 2 * ROWS), (2 * panel, 2 * ROWS)],
         flops,
-        *spread(*flipped(value, 0, 2)),
+        *spread(value, away),
         near,
         near_low,
     )
     result, value = kernel_call(second_kernel, [place], [square, packed], [], flops, *hop(value))
     scale = jnp.full((1,), 1.0 / (points * lax.axis_size("pts")), jnp.float32)
     return kernel_call(
-        last_kernel, [place, scale], square, [(panel, 2 * ROWS)], 0, result, *flipped(value, 0)
+        last_kernel, [place, scale], square, [(panel, 2 * ROWS)], 0, result, turned(value)
     )
 
 

time: 141 us -> 132 us (0.936)
  blocking collectives: 16.5 us -> 12 us
  waiting for transfers between devices: 54.1 us -> 51.1 us
  local copies, waits for them, and re-layouts: 4.36 us -> 6.21 us
  other arithmetic: 2.78 us -> 1.1 us
    ppermute x3, starting transfers between devices: 11.5 us -> 1.5 us  [the longest x2 1.41 us: per_device(): across = [lax.ppermute(value, 'lm', OTHER_CORE) for value in across]]
    all_to_all x0 -> x1, waiting for transfers between devices: none -> 8.77 us  [turned(): lax.all_to_all(packed, ('pts', 'lm'), 0, 0, axis_index_groups=groups, til...]
    ppermute x9, waiting for transfers between devices: 19 us -> 12.1 us  [sum_along(): lax.ppermute(values[step], ('pts', 'lm'), plane_step(step, swapped))]
    all_to_all x0 -> x1, starting transfers between devices: none -> 5.57 us  [turned(): lax.all_to_all(packed, ('pts', 'lm'), 0, 0, axis_index_groups=groups, til...]
    ppermute x3, waiting for transfers between devices: 10.7 us -> 5.15 us  [the longest x1 5.14 us: per_device(): away = lax.ppermute(value, 'lm', OTHER_CHIP)]
    all_to_all x2 -> x1, blocking collectives: 16.5 us -> 12 us  [turned(): lax.all_to_all(packed, ('pts', 'lm'), 0, 0, axis_index_groups=groups, til...]
    add x3, other arithmetic: 2.65 us -> 0.28 us  [sum_along(): total += lax.ppermute(values[step], ('pts', 'lm'), plane_step(step, swapp...]
    ppermute x9, starting transfers between devices: 11.3 us -> 12.8 us  [sum_along(): lax.ppermute(values[step], ('pts', 'lm'), plane_step(step, swapped))]
  transfers between devices with their start and end apart: 26 -> 27, of which waited for: 20 -> 19; matrix products, arithmetic and copies ran while one was open for 4% -> 4% of each run, Pallas kernels for 14% -> 15%
where the time goes in v3:
time: 132 us
  waiting for transfers between devices  51.1 us (39%)
  starting transfers between devices  35.6 us (27%)
  Pallas kernels  25.4 us (19%)
  blocking collectives  12 us (9%)
  local copies, waits for them, and re-layouts  6.21 us (5%)
    pallas_call x9, Pallas kernels, kernel_call(): pl.pallas_call(body, out_shape=out_shape, in_specs=[smem] * len(scalars)...  25.4 us
    ppermute x9, starting transfers between devices, sum_along(): lax.ppermute(values[step], ('pts', 'lm'), plane_step(step, swapped))  12.8 us
    ppermute x9, waiting for transfers between devices, sum_along(): lax.ppermute(values[step], ('pts', 'lm'), plane_step(step, swapped))  12.1 us
    all_to_all x1, blocking collectives, turned(): lax.all_to_all(packed, ('pts', 'lm'), 0, 0, axis_index_groups=groups, til...  12 us
    ppermute x2, waiting for transfers between devices, hop(): got = lax.ppermute(value, 'lm', OTHER_CHIP)  9.38 us
    all_to_all x1, waiting for transfers between devices, turned(): lax.all_to_all(packed, ('pts', 'lm'), 0, 0, axis_index_groups=groups, til...  8.77 us
    ppermute x2, waiting for transfers between devices, per_device(): lax.ppermute(sent[:, at:at + w], 'lm', OTHER_CHIP)  5.87 us
    all_to_all x1, starting transfers between devices, turned(): lax.all_to_all(packed, ('pts', 'lm'), 0, 0, axis_index_groups=groups, til...  5.57 us
  transfers between devices with their start and end apart: 27, of which 19 were waited for; matrix products, arithmetic and copies ran while one was open for 4% of the time, Pallas kernels for 15%

profile of v3, /device:TPU:1, one launch (start us, length us, event | category | flops | bytes accessed | tf_op | source)
XLA Modules:
  0.0 131.6 jit_solution(12230793626176800226)
XLA Ops:
  0.0 1.4 %collective-permute-start = (f32[1024,512]{1,0:T(8,128)}, f32[1024,512]{1,0:T(8,128)}, u32[]{:S(2)}, u32[]{:S(2)}) collective-permute-start(f32[1024,512]{1,0:T(8,128)} %refs_1_.7), channel_id=1, source_target_pairs={{0,1},{1,0},{2,3},{3,2},{4,5},{5,4},{6,7},{7,6},{8,9},{9,8},{10,11... | collective-permute-start | bytes 6291464 | tf_op jit(solution)/shard_map/ppermute | solution.py:308
  1.4 1.0 constant_dynamic-slice_fusion
  2.4 1.8 %collective-permute-start.1 = (f32[512,128]{1,0:T(8,128)S(1)}, f32[512,128]{1,0:T(8,128)S(1)}, u32[]{:S(2)}, u32[]{:S(2)}) collective-permute-start(f32[512,128]{1,0:T(8,128)S(1)} %constant_dynamic-slice_fusion), channel_id=1, source_target_pairs={{0,2},{1,3},{2,0},{3,1},{4,6},{5,7},{6,4},{7,5},{8,10},{9,11},{10,... | collective-permute-start | bytes 786440 | tf_op jit(solution)/shard_map/ppermute | solution.py:310
  4.2 1.2 dynamic-slice.1
  5.5 3.2 %slice.11 = f32[1024,512]{1,0:T(8,128)} slice(f32[2048,512]{1,0:T(8,128)} %refs_3_.1), slice={[0:1024], [0:512]} | slice | bytes 4194304 | tf_op jit(solution)/shard_map/slice | solution.py:331
  9.1 1.8 %collective-permute-done.1 = f32[512,128]{1,0:T(8,128)S(1)} collective-permute-done((f32[512,128]{1,0:T(8,128)S(1)}, f32[512,128]{1,0:T(8,128)S(1)}, u32[]{:S(2)}, u32[]{:S(2)}) %collective-permute-start.1) | collective-permute-done | bytes 262176 | tf_op jit(solution)/shard_map/ppermute | solution.py:310
  10.9 0.8 collective-permute-start.2
  11.7 4.5 %shard_map.46.refs_4_ = f32[512,768]{1,0:T(8,128)S(1)} custom-call(s32[7]{0:T(128)S(1)} %stack.49.refs_0_, f32[1024,512]{1,0:T(8,128)S(1)} %copy-done.1, f32[1024,512]{1,0:T(8,128)} %collective-permute-done.refs_2_), custom_call_target="tpu_custom_call" | custom-call | flops 40000000000 | bytes 120000000 | tf_op jit(solution)/shard_map/pallas_call | solution.py:259
  16.2 3.0 %shard_map.47 = (f32[4,32,1024]{2,1,0:T(8,128)S(1)}, f32[4,32,1024]{2,1,0:T(8,128)S(1)}, f32[4,32,1024]{2,1,0:T(8,128)S(1)}, f32[4,32,1024]{2,1,0:T(8,128)S(1)}) custom-call(s32[7]{0:T(128)S(1)} %stack.49.refs_0_, f32[1024,512]{1,0:T(8,128)S(1)} %copy-done.1, f32[1024,512]{1,0:T(8,128)} %collective-permute-done.refs_2_, ...), custom_call_target="tpu_custom_call" | custom-call | flops 6000000000 | bytes 18000000 | tf_op jit(solution)/shard_map/pallas_call | solution.py:259
  19.2 3.1 %collective-permute-start.5 = (f32[4,32,1024]{2,1,0:T(8,128)S(1)}, f32[4,32,1024]{2,1,0:T(8,128)S(1)}, u32[]{:S(2)}, u32[]{:S(2)}) collective-permute-start(f32[4,32,1024]{2,1,0:T(8,128)S(1)} %get-tuple-element.30), channel_id=1, source_target_pairs={{0,32},{1,9},{2,34},{3,11},{4,36},{5,13},{6,38},{7,15},{8,40},{9,1... | collective-permute-start | bytes 1572872 | tf_op jit(solution)/shard_map/ppermute | solution.py:289
  22.2 0.8 collective-permute-start.4
  23.0 0.7 collective-permute-start.3
  23.7 4.1 %collective-permute-done.6 = f32[512,384]{1,0:T(8,128)} collective-permute-done((f32[512,384]{1,0:T(8,128)S(1)}, f32[512,384]{1,0:T(8,128)}, u32[]{:S(2)}, u32[]{:S(2)}) %collective-permute-start.6) | collective-permute-done | bytes 786464 | tf_op jit(solution)/shard_map/ppermute | solution.py:310
  28.4 0.7 collective-permute-done.5
  29.1 0.9 collective-permute-start.11
  30.0 5.1 %collective-permute-done.4 = f32[4,32,1024]{2,1,0:T(8,128)S(1)} collective-permute-done((f32[4,32,1024]{2,1,0:T(8,128)S(1)}, f32[4,32,1024]{2,1,0:T(8,128)S(1)}, u32[]{:S(2)}, u32[]{:S(2)}) %collective-permute-start.4) | collective-permute-done | bytes 524320 | tf_op jit(solution)/shard_map/ppermute | solution.py:289
  35.3 3.7 %shard_map.48 = (f32[4,32,768]{2,1,0:T(8,128)S(1)}, f32[4,32,768]{2,1,0:T(8,128)S(1)}, f32[4,32,768]{2,1,0:T(8,128)S(1)}, f32[4,32,768]{2,1,0:T(8,128)S(1)}) custom-call(s32[7]{0:T(128)S(1)} %stack.49.refs_0_, f32[1024,512]{1,0:T(8,128)S(1)} %copy-done.1, f32[1024,512]{1,0:T(8,128)} %collective-permute-done.refs_2_, ...), custom_call_target="tpu_custom_call" | custom-call | flops 4000000000 | bytes 12000000 | tf_op jit(solution)/shard_map/pallas_call | solution.py:259
  39.0 2.6 %collective-permute-start.10 = (f32[4,32,768]{2,1,0:T(8,128)S(1)}, f32[4,32,768]{2,1,0:T(8,128)S(1)}, u32[]{:S(2)}, u32[]{:S(2)}) collective-permute-start(f32[4,32,768]{2,1,0:T(8,128)S(1)} %get-tuple-element.34), channel_id=1, source_target_pairs={{0,32},{1,9},{2,34},{3,11},{4,36},{5,13},{6,38},{7,15},{8,40},{9,1... | collective-permute-start | bytes 1179656 | tf_op jit(solution)/shard_map/ppermute | solution.py:289
  41.7 0.9 collective-permute-start.9
  43.1 8.0 %shard_map.49 = (bf16[1024,512]{1,0:T(8,128)(2,1)S(1)}, bf16[1024,512]{1,0:T(8,128)(2,1)S(1)}, bf16[1024,512]{1,0:T(8,128)(2,1)S(1)}, bf16[1024,512]{1,0:T(8,128)(2,1)S(1)}) custom-call(s32[7]{0:T(128)S(1)} %stack.49.refs_0_, f32[512,512]{1,0:T(8,128)S(1)} %bitcast.33, f32[512,512]{1,0:T(8,128)S(1)} %collective-permute-done.11.refs_2_, ...), custom_call_target="tpu_custom_call" | custom-call | flops 4000000000 | bytes 12000000 | tf_op jit(solution)/shard_map/pallas_call | solution.py:259
  52.5 0.7 pad_maximum_fusion.3
  53.2 2.8 %collective-permute-start.15 = (f32[32,1792]{1,0:T(8,128)}, f32[32,1792]{1,0:T(8,128)S(1)}, u32[]{:S(2)}, u32[]{:S(2)}) collective-permute-start(f32[32,1792]{1,0:T(8,128)} %get-tuple-element.39), channel_id=1, source_target_pairs={{0,8},{1,33},{2,10},{3,35},{4,12},{5,37},{6,14},{7,39},{8,0},{9,41... | collective-permute-start | bytes 688136 | tf_op jit(solution)/shard_map/ppermute | solution.py:289
  56.0 0.8 collective-permute-start.14
  57.5 2.7 %collective-permute-done.15 = f32[32,1792]{1,0:T(8,128)S(1)} collective-permute-done((f32[32,1792]{1,0:T(8,128)}, f32[32,1792]{1,0:T(8,128)S(1)}, u32[]{:S(2)}, u32[]{:S(2)}) %collective-permute-start.15) | collective-permute-done | bytes 229408 | tf_op jit(solution)/shard_map/ppermute | solution.py:289
  60.1 2.6 %collective-permute-done.14 = f32[32,1792]{1,0:T(8,128)S(1)} collective-permute-done((f32[32,1792]{1,0:T(8,128)S(1)}, f32[32,1792]{1,0:T(8,128)S(1)}, u32[]{:S(2)}, u32[]{:S(2)}) %collective-permute-start.14) | collective-permute-done | bytes 229408 | tf_op jit(solution)/shard_map/ppermute | solution.py:289
  63.3 3.6 %collective-permute-start.16 = (f32[16,1792]{1,0:T(8,128)S(1)}, f32[16,1792]{1,0:T(8,128)S(1)}, u32[]{:S(2)}, u32[]{:S(2)}) collective-permute-start(f32[16,1792]{1,0:T(8,128)S(1)} %get-tuple-element.41), channel_id=1, source_target_pairs={{0,64},{1,65},{2,66},{3,67},{4,68},{5,69},{6,70},{7,71},{8,72},{9,... | collective-permute-start | bytes 344072 | tf_op jit(solution)/shard_map/ppermute | solution.py:341
  66.9 0.7 collective-permute-start.17
  67.6 1.5 %collective-permute-done.16 = f32[16,1792]{1,0:T(8,128)S(1)} collective-permute-done((f32[16,1792]{1,0:T(8,128)S(1)}, f32[16,1792]{1,0:T(8,128)S(1)}, u32[]{:S(2)}, u32[]{:S(2)}) %collective-permute-start.16) | collective-permute-done | bytes 114720 | tf_op jit(solution)/shard_map/ppermute | solution.py:341
  69.1 2.2 %collective-permute-done.17 = f32[16,1792]{1,0:T(8,128)S(1)} collective-permute-done((f32[16,1792]{1,0:T(8,128)S(1)}, f32[16,1792]{1,0:T(8,128)S(1)}, u32[]{:S(2)}, u32[]{:S(2)}) %collective-permute-start.17) | collective-permute-done | bytes 114720 | tf_op jit(solution)/shard_map/ppermute | solution.py:339
  71.3 1.8 %collective-permute-done.18 = f32[16,1792]{1,0:T(8,128)S(1)} collective-permute-done((f32[16,1792]{1,0:T(8,128)S(1)}, f32[16,1792]{1,0:T(8,128)S(1)}, u32[]{:S(2)}, u32[]{:S(2)}) %collective-permute-start.18) | collective-permute-done | bytes 114720 | tf_op jit(solution)/shard_map/ppermute | solution.py:340
  73.2 3.5 %collective-permute-start.19 = (f32[2,16,1792]{2,1,0:T(8,128)S(1)}, f32[2,16,1792]{2,1,0:T(8,128)S(1)}, u32[]{:S(2)}, u32[]{:S(2)}) collective-permute-start(f32[2,16,1792]{2,1,0:T(8,128)S(1)} %pad_maximum_fusion.5), channel_id=1, source_target_pairs={{0,1},{1,0},{2,3},{3,2},{4,5},{5,4},{6,7},{7,6},{8,9},{9,8},{10,11... | collective-permute-start | bytes 688136 | tf_op jit(solution)/shard_map/ppermute | solution.py:345
  76.7 1.1 collective-permute-done.19.refs_4_
  77.8 1.2 shard_map.50.refs_1_
  79.2 4.7 %collective-permute-done.20.refs_2_ = f32[64,512]{1,0:T(8,128)S(1)} collective-permute-done((f32[64,512]{1,0:T(8,128)S(1)}, f32[64,512]{1,0:T(8,128)S(1)}, u32[]{:S(2)}, u32[]{:S(2)}) %collective-permute-start.20) | collective-permute-done | bytes 131104 | tf_op jit(solution)/shard_map/ppermute | solution.py:348
  83.9 1.2 collective-permute-start.21
  85.1 1.0 collective-permute-done.21.refs_3_
  86.1 1.4 %shard_map.51 = (f32[64,512]{1,0:T(8,128)}, f32[16,32,128]{2,1,0:T(8,128)}) custom-call(s32[7]{0:T(128)S(1)} %stack.49.refs_0_, f32[64,512]{1,0:T(8,128)S(1)} %shard_map.50.refs_1_, f32[64,512]{1,0:T(8,128)S(1)} %collective-permute-done.20.refs_2_, f32[64,512]{1,0:T(8,128)S(1)} %collective-permute-done.21.refs_3_, bf16[1024,512]{1,0:T(8,128)(2,1)S(1)} %copy-done.5, ...), custom_call_target="tpu_custom_call" | custom-call | flops 2000000000 | bytes 6000000 | tf_op jit(solution)/shard_map/pallas_call | solution.py:259
  87.4 5.6 %all-to-all-start = ((f32[16,32,128]{2,1,0:T(8,128)}), f32[16,32,128]{2,1,0:T(8,128)S(1)}, u32[]{:S(2)}, u32[]{:S(2)}) async-start(f32[16,32,128]{2,1,0:T(8,128)} %get-tuple-element.46), calls=%async_computation | async-start | bytes 524288 | tf_op jit(solution)/shard_map/all_to_all | solution.py:353
  93.0 8.8 %all-to-all-done = f32[16,32,128]{2,1,0:T(8,128)S(1)} async-done(((f32[16,32,128]{2,1,0:T(8,128)}), f32[16,32,128]{2,1,0:T(8,128)S(1)}, u32[]{:S(2)}, u32[]{:S(2)}) %all-to-all-start) | async-done | bytes 262176 | tf_op jit(solution)/shard_map/all_to_all | solution.py:353
  101.9 5.1 %collective-permute-done.22.refs_3_ = f32[8,32,128]{2,1,0:T(8,128)S(1)} collective-permute-done((f32[8,32,128]{2,1,0:T(8,128)S(1)}, f32[8,32,128]{2,1,0:T(8,128)S(1)}, u32[]{:S(2)}, u32[]{:S(2)}) %collective-permute-start.22) | collective-permute-done | bytes 131104 | tf_op jit(solution)/shard_map/ppermute | solution.py:370
  107.1 0.8 collective-permute-start.23
  107.9 1.2 collective-permute-done.23.refs_4_
  109.1 1.5 %shard_map.52.refs_1_ = f32[64,512]{1,0:T(8,128)S(1)} custom-call(s32[7]{0:T(128)S(1)} %stack.49.refs_0_, s32[16]{0:T(128)S(1)} %copy-done.3, f32[8,32,128]{2,1,0:T(8,128)S(1)} %constant_dynamic-slice_fusion.1.refs_2_, f32[8,32,128]{2,1,0:T(8,128)S(1)} %collective-permute-done.22.refs_3_, f32[2,8,32,128]{3,2,1,0:T(8,128)S(1)} %collective-permute-done.23.refs_4_, ...), custom_call_target="tpu_custom_call" | custom-call | flops 2000000000 | bytes 6000000 | tf_op jit(solution)/shard_map/pallas_call | solution.py:259
  110.7 4.7 %collective-permute-done.24.refs_2_ = f32[64,512]{1,0:T(8,128)S(1)} collective-permute-done((f32[64,512]{1,0:T(8,128)S(1)}, f32[64,512]{1,0:T(8,128)S(1)}, u32[]{:S(2)}, u32[]{:S(2)}) %collective-permute-start.24) | collective-permute-done | bytes 131104 | tf_op jit(solution)/shard_map/ppermute | solution.py:348
  115.4 1.2 collective-permute-start.25
  116.6 1.0 collective-permute-done.25.refs_3_
  118.3 12.0 %all_to_all.10.refs_3_ = f32[16,32,128]{2,1,0:T(8,128)S(1)} all-to-all(f32[16,32,128]{2,1,0:T(8,128)S(1)} %get-tuple-element.48), channel_id=1, replica_groups={{1,5,9,13,17,21,25,29,32,36,40,44,48,52,56,60},{2,6,10,14,18,22,26,30,6..., dimensions={0} | all-to-all | bytes 524288 | tf_op jit(solution)/shard_map/all_to_all | solution.py:353
  130.2 1.4 %shard_map.54 = f32[64,512]{1,0:T(8,128)} custom-call(s32[7]{0:T(128)S(1)} %stack.49.refs_0_, f32[1]{0:T(128)} %constant.82.clone.1.refs_1_, f32[64,512]{1,0:T(8,128)S(1)} %get-tuple-element.47.refs_2_, f32[16,32,128]{2,1,0:T(8,128)S(1)} %all_to_all.10.refs_3_), custom_call_target="tpu_custom_call" | custom-call | tf_op jit(solution)/shard_map/pallas_call | solution.py:259
  (54 shorter events, 5.3 us)
Async XLA Ops:
  0.0 11.7 %collective-permute-start = (f32[1024,512]{1,0:T(8,128)}, f32[1024,512]{1,0:T(8,128)}, u32[]{:S(2)}, u32[]{:S(2)}) collective-permute-start(f32[1024,512]{1,0:T(8,128)} %refs_1_.7), channel_id=1, source_target_pairs={{0,1},{1,0},{2,3},{3,2},{4,5},{5,4},{6,7},{7,6},{8,9},{9,8},{10,11... | collective-permute-start | bytes 6291464 | tf_op jit(solution)/shard_map/ppermute | solution.py:308
  2.4 8.5 %collective-permute-start.1 = (f32[512,128]{1,0:T(8,128)S(1)}, f32[512,128]{1,0:T(8,128)S(1)}, u32[]{:S(2)}, u32[]{:S(2)}) collective-permute-start(f32[512,128]{1,0:T(8,128)S(1)} %constant_dynamic-slice_fusion), channel_id=1, source_target_pairs={{0,2},{1,3},{2,0},{3,1},{4,6},{5,7},{6,4},{7,5},{8,10},{9,11},{10,... | collective-permute-start | bytes 786440 | tf_op jit(solution)/shard_map/ppermute | solution.py:310
  5.4 6.3 %copy-start.1 = (f32[1024,512]{1,0:T(8,128)S(1)}, f32[1024,512]{1,0:T(8,128)}, u32[]{:S(2)}) copy-start(f32[1024,512]{1,0:T(8,128)} %refs_1_.7) | copy-start | bytes 6291460
  5.4 22.4 %collective-permute-start.6 = (f32[512,384]{1,0:T(8,128)S(1)}, f32[512,384]{1,0:T(8,128)}, u32[]{:S(2)}, u32[]{:S(2)}) collective-permute-start(f32[512,384]{1,0:T(8,128)S(1)} %dynamic-slice.1), channel_id=1, source_target_pairs={{0,2},{1,3},{2,0},{3,1},{4,6},{5,7},{6,4},{7,5},{8,10},{9,11},{10,... | collective-permute-start | bytes 2359304 | tf_op jit(solution)/shard_map/ppermute | solution.py:310
  8.7 34.4 %collective-permute-start.12 = (f32[1024,512]{1,0:T(8,128)}, f32[1024,512]{1,0:T(8,128)}, u32[]{:S(2)}, u32[]{:S(2)}) collective-permute-start(f32[1024,512]{1,0:T(8,128)} %slice.11), channel_id=1, source_target_pairs={{0,1},{1,0},{2,3},{3,2},{4,5},{5,4},{6,7},{7,6},{8,9},{9,8},{10,11... | collective-permute-start | bytes 6291464 | tf_op jit(solution)/shard_map/ppermute | solution.py:331
  10.9 5.3 %collective-permute-start.2 = (f32[512,128]{1,0:T(8,128)S(1)}, f32[512,128]{1,0:T(8,128)S(1)}, u32[]{:S(2)}, u32[]{:S(2)}) collective-permute-start(f32[512,128]{1,0:T(8,128)S(1)} %collective-permute-done.1), channel_id=1, source_target_pairs={{0,1},{1,0},{2,3},{3,2},{4,5},{5,4},{6,7},{7,6},{8,9},{9,8},{10,11... | collective-permute-start | bytes 786440 | tf_op jit(solution)/shard_map/ppermute | solution.py:311
  16.2 13.0 %copy-start.2 = (f32[1,512,512]{2,1,0:T(8,128)S(1)}, f32[1,512,512]{2,1,0:T(8,128)}, u32[]{:S(2)}) copy-start(f32[1,512,512]{2,1,0:T(8,128)} %param.6) | copy-start | bytes 3145732
  19.2 10.0 %collective-permute-start.5 = (f32[4,32,1024]{2,1,0:T(8,128)S(1)}, f32[4,32,1024]{2,1,0:T(8,128)S(1)}, u32[]{:S(2)}, u32[]{:S(2)}) collective-permute-start(f32[4,32,1024]{2,1,0:T(8,128)S(1)} %get-tuple-element.30), channel_id=1, source_target_pairs={{0,32},{1,9},{2,34},{3,11},{4,36},{5,13},{6,38},{7,15},{8,40},{9,1... | collective-permute-start | bytes 1572872 | tf_op jit(solution)/shard_map/ppermute | solution.py:289
  22.2 12.9 %collective-permute-start.4 = (f32[4,32,1024]{2,1,0:T(8,128)S(1)}, f32[4,32,1024]{2,1,0:T(8,128)S(1)}, u32[]{:S(2)}, u32[]{:S(2)}) collective-permute-start(f32[4,32,1024]{2,1,0:T(8,128)S(1)} %get-tuple-element.29), channel_id=1, source_target_pairs={{0,48},{1,13},{2,50},{3,15},{4,52},{5,1},{6,54},{7,3},{8,56},{9,5}... | collective-permute-start | bytes 1572872 | tf_op jit(solution)/shard_map/ppermute | solution.py:289
  23.0 12.1 %collective-permute-start.3 = (f32[4,32,1024]{2,1,0:T(8,128)S(1)}, f32[4,32,1024]{2,1,0:T(8,128)S(1)}, u32[]{:S(2)}, u32[]{:S(2)}) collective-permute-start(f32[4,32,1024]{2,1,0:T(8,128)S(1)} %get-tuple-element.28), channel_id=1, source_target_pairs={{0,16},{1,5},{2,18},{3,7},{4,20},{5,9},{6,22},{7,11},{8,24},{9,13}... | collective-permute-start | bytes 1572872 | tf_op jit(solution)/shard_map/ppermute | solution.py:289
  27.8 7.5 %collective-permute-start.7 = (f32[512,384]{1,0:T(8,128)}, f32[512,384]{1,0:T(8,128)S(1)}, u32[]{:S(2)}, u32[]{:S(2)}) collective-permute-start(f32[512,384]{1,0:T(8,128)} %collective-permute-done.6), channel_id=1, source_target_pairs={{0,1},{1,0},{2,3},{3,2},{4,5},{5,4},{6,7},{7,6},{8,9},{9,8},{10,11... | collective-permute-start | bytes 2359304 | tf_op jit(solution)/shard_map/ppermute | solution.py:311
  29.1 14.0 %collective-permute-start.11 = (f32[512,512]{1,0:T(8,128)S(1)}, f32[512,512]{1,0:T(8,128)S(1)}, u32[]{:S(2)}, u32[]{:S(2)}) collective-permute-start(f32[512,512]{1,0:T(8,128)S(1)} %bitcast.32), channel_id=1, source_target_pairs={{0,1},{1,0},{2,3},{3,2},{4,5},{5,4},{6,7},{7,6},{8,9},{9,8},{10,11... | collective-permute-start | bytes 3145736 | tf_op jit(solution)/shard_map/ppermute | solution.py:330
  35.3 7.8 %copy-start = (f32[2048,512]{1,0:T(8,128)S(1)}, f32[2048,512]{1,0:T(8,128)}, u32[]{:S(2)}) copy-start(f32[2048,512]{1,0:T(8,128)} %refs_3_.1) | copy-start | bytes 12582916
  39.0 12.2 %collective-permute-start.10 = (f32[4,32,768]{2,1,0:T(8,128)S(1)}, f32[4,32,768]{2,1,0:T(8,128)S(1)}, u32[]{:S(2)}, u32[]{:S(2)}) collective-permute-start(f32[4,32,768]{2,1,0:T(8,128)S(1)} %get-tuple-element.34), channel_id=1, source_target_pairs={{0,32},{1,9},{2,34},{3,11},{4,36},{5,13},{6,38},{7,15},{8,40},{9,1... | collective-permute-start | bytes 1179656 | tf_op jit(solution)/shard_map/ppermute | solution.py:289
  41.7 10.1 %collective-permute-start.9 = (f32[4,32,768]{2,1,0:T(8,128)S(1)}, f32[4,32,768]{2,1,0:T(8,128)S(1)}, u32[]{:S(2)}, u32[]{:S(2)}) collective-permute-start(f32[4,32,768]{2,1,0:T(8,128)S(1)} %get-tuple-element.33), channel_id=1, source_target_pairs={{0,48},{1,13},{2,50},{3,15},{4,52},{5,1},{6,54},{7,3},{8,56},{9,5}... | collective-permute-start | bytes 1179656 | tf_op jit(solution)/shard_map/ppermute | solution.py:289
  42.6 9.2 %collective-permute-start.8 = (f32[4,32,768]{2,1,0:T(8,128)S(1)}, f32[4,32,768]{2,1,0:T(8,128)S(1)}, u32[]{:S(2)}, u32[]{:S(2)}) collective-permute-start(f32[4,32,768]{2,1,0:T(8,128)S(1)} %get-tuple-element.32), channel_id=1, source_target_pairs={{0,16},{1,5},{2,18},{3,7},{4,20},{5,9},{6,22},{7,11},{8,24},{9,13}... | collective-permute-start | bytes 1179656 | tf_op jit(solution)/shard_map/ppermute | solution.py:289
  51.2 1.0 copy-start.4
  51.2 1.3 %copy-start.7 = (bf16[1024,512]{1,0:T(8,128)(2,1)}, bf16[1024,512]{1,0:T(8,128)(2,1)S(1)}, u32[]{:S(2)}) copy-start(bf16[1024,512]{1,0:T(8,128)(2,1)S(1)} %get-tuple-element.45.refs_5_) | copy-start | bytes 3145732
  52.5 25.3 %copy-start.3 = (s32[16]{0:T(128)S(1)}, s32[16]{0:T(128)}, u32[]{:S(2)}) copy-start(s32[16]{0:T(128)} %refs_1_.9) | copy-start | bytes 196
  53.2 6.9 %collective-permute-start.15 = (f32[32,1792]{1,0:T(8,128)}, f32[32,1792]{1,0:T(8,128)S(1)}, u32[]{:S(2)}, u32[]{:S(2)}) collective-permute-start(f32[32,1792]{1,0:T(8,128)} %get-tuple-element.39), channel_id=1, source_target_pairs={{0,8},{1,33},{2,10},{3,35},{4,12},{5,37},{6,14},{7,39},{8,0},{9,41... | collective-permute-start | bytes 688136 | tf_op jit(solution)/shard_map/ppermute | solution.py:289
  56.0 6.7 %collective-permute-start.14 = (f32[32,1792]{1,0:T(8,128)S(1)}, f32[32,1792]{1,0:T(8,128)S(1)}, u32[]{:S(2)}, u32[]{:S(2)}) collective-permute-start(f32[32,1792]{1,0:T(8,128)S(1)} %get-tuple-element.38), channel_id=1, source_target_pairs={{0,12},{1,49},{2,14},{3,51},{4,0},{5,53},{6,2},{7,55},{8,4},{9,57}... | collective-permute-start | bytes 688136 | tf_op jit(solution)/shard_map/ppermute | solution.py:289
  56.8 6.4 %collective-permute-start.13 = (f32[32,1792]{1,0:T(8,128)S(1)}, f32[32,1792]{1,0:T(8,128)S(1)}, u32[]{:S(2)}, u32[]{:S(2)}) collective-permute-start(f32[32,1792]{1,0:T(8,128)S(1)} %get-tuple-element.37), channel_id=1, source_target_pairs={{0,4},{1,17},{2,6},{3,19},{4,8},{5,21},{6,10},{7,23},{8,12},{9,25}... | collective-permute-start | bytes 688136 | tf_op jit(solution)/shard_map/ppermute | solution.py:289
  63.3 5.8 %collective-permute-start.16 = (f32[16,1792]{1,0:T(8,128)S(1)}, f32[16,1792]{1,0:T(8,128)S(1)}, u32[]{:S(2)}, u32[]{:S(2)}) collective-permute-start(f32[16,1792]{1,0:T(8,128)S(1)} %get-tuple-element.41), channel_id=1, source_target_pairs={{0,64},{1,65},{2,66},{3,67},{4,68},{5,69},{6,70},{7,71},{8,72},{9,... | collective-permute-start | bytes 344072 | tf_op jit(solution)/shard_map/ppermute | solution.py:341
  66.9 4.4 %collective-permute-start.17 = (f32[16,1792]{1,0:T(8,128)S(1)}, f32[16,1792]{1,0:T(8,128)S(1)}, u32[]{:S(2)}, u32[]{:S(2)}) collective-permute-start(f32[16,1792]{1,0:T(8,128)S(1)} %get-tuple-element.40), channel_id=1, source_target_pairs={{0,2},{1,3},{2,0},{3,1},{4,6},{5,7},{6,4},{7,5},{8,10},{9,11},{10,... | collective-permute-start | bytes 344072 | tf_op jit(solution)/shard_map/ppermute | solution.py:339
  67.6 5.5 %collective-permute-start.18 = (f32[16,1792]{1,0:T(8,128)S(1)}, f32[16,1792]{1,0:T(8,128)S(1)}, u32[]{:S(2)}, u32[]{:S(2)}) collective-permute-start(f32[16,1792]{1,0:T(8,128)S(1)} %get-tuple-element.41), channel_id=1, source_target_pairs={{0,66},{1,67},{2,64},{3,65},{4,70},{5,71},{6,68},{7,69},{8,74},{9,... | collective-permute-start | bytes 344072 | tf_op jit(solution)/shard_map/ppermute | solution.py:340
  73.2 4.6 %collective-permute-start.19 = (f32[2,16,1792]{2,1,0:T(8,128)S(1)}, f32[2,16,1792]{2,1,0:T(8,128)S(1)}, u32[]{:S(2)}, u32[]{:S(2)}) collective-permute-start(f32[2,16,1792]{2,1,0:T(8,128)S(1)} %pad_maximum_fusion.5), channel_id=1, source_target_pairs={{0,1},{1,0},{2,3},{3,2},{4,5},{5,4},{6,7},{7,6},{8,9},{9,8},{10,11... | collective-permute-start | bytes 688136 | tf_op jit(solution)/shard_map/ppermute | solution.py:345
  77.8 8.2 %copy-start.5 = (bf16[1024,512]{1,0:T(8,128)(2,1)S(1)}, bf16[1024,512]{1,0:T(8,128)(2,1)}, u32[]{:S(2)}) copy-start(bf16[1024,512]{1,0:T(8,128)(2,1)} %copy-done.4) | copy-start | bytes 3145732
  77.8 8.2 %copy-start.8 = (bf16[1024,512]{1,0:T(8,128)(2,1)S(1)}, bf16[1024,512]{1,0:T(8,128)(2,1)}, u32[]{:S(2)}) copy-start(bf16[1024,512]{1,0:T(8,128)(2,1)} %copy-done.7) | copy-start | bytes 3145732
  79.1 4.8 %collective-permute-start.20 = (f32[64,512]{1,0:T(8,128)S(1)}, f32[64,512]{1,0:T(8,128)S(1)}, u32[]{:S(2)}, u32[]{:S(2)}) collective-permute-start(f32[64,512]{1,0:T(8,128)S(1)} %shard_map.50.refs_1_), channel_id=1, source_target_pairs={{0,2},{1,3},{2,0},{3,1},{4,6},{5,7},{6,4},{7,5},{8,10},{9,11},{10,... | collective-permute-start | bytes 393224 | tf_op jit(solution)/shard_map/ppermute | solution.py:348
  83.9 2.2 %collective-permute-start.21 = (f32[64,512]{1,0:T(8,128)S(1)}, f32[64,512]{1,0:T(8,128)S(1)}, u32[]{:S(2)}, u32[]{:S(2)}) collective-permute-start(f32[64,512]{1,0:T(8,128)S(1)} %collective-permute-done.20.refs_2_), channel_id=1, source_target_pairs={{0,1},{1,0},{2,3},{3,2},{4,5},{5,4},{6,7},{7,6},{8,9},{9,8},{10,11... | collective-permute-start | bytes 393224 | tf_op jit(solution)/shard_map/ppermute | solution.py:349
  87.4 14.4 %all-to-all-start = ((f32[16,32,128]{2,1,0:T(8,128)}), f32[16,32,128]{2,1,0:T(8,128)S(1)}, u32[]{:S(2)}, u32[]{:S(2)}) async-start(f32[16,32,128]{2,1,0:T(8,128)} %get-tuple-element.46), calls=%async_computation | async-start | bytes 524288 | tf_op jit(solution)/shard_map/all_to_all | solution.py:353
  101.8 5.3 %collective-permute-start.22 = (f32[8,32,128]{2,1,0:T(8,128)S(1)}, f32[8,32,128]{2,1,0:T(8,128)S(1)}, u32[]{:S(2)}, u32[]{:S(2)}) collective-permute-start(f32[8,32,128]{2,1,0:T(8,128)S(1)} %constant_dynamic-slice_fusion.1.refs_2_), channel_id=1, source_target_pairs={{0,2},{1,3},{2,0},{3,1},{4,6},{5,7},{6,4},{7,5},{8,10},{9,11},{10,... | collective-permute-start | bytes 393224 | tf_op jit(solution)/shard_map/ppermute | solution.py:370
  107.1 10.5 %copy-start.6 = (bf16[1024,512]{1,0:T(8,128)(2,1)S(1)}, bf16[1024,512]{1,0:T(8,128)(2,1)}, u32[]{:S(2)}) copy-start(bf16[1024,512]{1,0:T(8,128)(2,1)} %copy-done.4) | copy-start | bytes 3145732
  107.1 10.5 %copy-start.9 = (bf16[1024,512]{1,0:T(8,128)(2,1)S(1)}, bf16[1024,512]{1,0:T(8,128)(2,1)}, u32[]{:S(2)}) copy-start(bf16[1024,512]{1,0:T(8,128)(2,1)} %copy-done.7) | copy-start | bytes 3145732
  107.1 2.0 %collective-permute-start.23 = (f32[2,8,32,128]{3,2,1,0:T(8,128)S(1)}, f32[2,8,32,128]{3,2,1,0:T(8,128)S(1)}, u32[]{:S(2)}, u32[]{:S(2)}) collective-permute-start(f32[2,8,32,128]{3,2,1,0:T(8,128)S(1)} %pad_maximum_fusion), channel_id=1, source_target_pairs={{0,1},{1,0},{2,3},{3,2},{4,5},{5,4},{6,7},{7,6},{8,9},{9,8},{10,11... | collective-permute-start | bytes 786440 | tf_op jit(solution)/shard_map/ppermute | solution.py:345
  110.6 4.8 %collective-permute-start.24 = (f32[64,512]{1,0:T(8,128)S(1)}, f32[64,512]{1,0:T(8,128)S(1)}, u32[]{:S(2)}, u32[]{:S(2)}) collective-permute-start(f32[64,512]{1,0:T(8,128)S(1)} %shard_map.52.refs_1_), channel_id=1, source_target_pairs={{0,2},{1,3},{2,0},{3,1},{4,6},{5,7},{6,4},{7,5},{8,10},{9,11},{10,... | collective-permute-start | bytes 393224 | tf_op jit(solution)/shard_map/ppermute | solution.py:348
  115.4 2.2 %collective-permute-start.25 = (f32[64,512]{1,0:T(8,128)S(1)}, f32[64,512]{1,0:T(8,128)S(1)}, u32[]{:S(2)}, u32[]{:S(2)}) collective-permute-start(f32[64,512]{1,0:T(8,128)S(1)} %collective-permute-done.24.refs_2_), channel_id=1, source_target_pairs={{0,1},{1,0},{2,3},{3,2},{4,5},{5,4},{6,7},{7,6},{8,9},{9,8},{10,11... | collective-permute-start | bytes 393224 | tf_op jit(solution)/shard_map/ppermute | solution.py:349

commit v4 on v3

--- a/solution.py
+++ b/solution.py
@@ -10,6 +10,7 @@
 COSTS = (40, 6, 4, 4)
 PIECES = ((0, 128), (128, 384))
 ROWS = 64
+KEPT = 3 * CLUSTER
 
 CELLS = [(zh, x, y) for zh in range(2) for x in range(4) for y in range(4)]
 
@@ -64,23 +65,34 @@
     def one(u, v):
         return jnp.dot(u, v, preferred_element_type=jnp.float32)
 
-    return one(a[0], b[0]) + (one(a[0], b[1]) + one(a[1], b[0]))
-
-
-def write_strips(place, product, outs):
+    rows = a[0].shape[0]
+    both = one(jnp.concatenate(a, 0), b[0])
+    return both[:rows] + (both[rows:] + one(a[0], b[1]))
+
+
+def write_strips(place, product, outs, wrapped=0):
     core, first, second = place[0], place[2], place[3]
+    kept = KEPT if wrapped else 0
+    if wrapped:
+        block = lax.broadcasted_iota(jnp.int32, (32, KEPT), 1) // CLUSTER
+        weight = jnp.where(block == 1, 1.0, 0.5)
     for k in range(4):
         for m in range(4):
             f, g = (first + k) % 4, (second + m) % 4
             strip = jnp.where(core == 0, 4 * f + g, 4 * g + f)
-            outs[k][m] = product[pl.ds(pl.multiple_of(strip * 32, 32), 32), :]
+            rows = pl.ds(pl.multiple_of(strip * 32, 32), 32)
+            if wrapped:
+                start = jnp.where(core == 0, f, g) * CLUSTER
+                columns = pl.ds(pl.multiple_of(start, CLUSTER), KEPT)
+                outs[k][m, :, :KEPT] = product[rows, columns] * weight
+            outs[k][m, :, kept:] = product[rows, wrapped:]
 
 
 def near_kernel(place, own, pair, product):
     panel = own.shape[1]
     thin = panel // 2
     a = halves(own[...])
-    product[:, :panel] = contract(a, a) * 0.5
+    product[:, :panel] = contract(a, a)
 
     @pl.when(place[0] == 0)
     def _():
@@ -92,16 +104,35 @@
         product[:, panel:] = contract(halves(pair[...]), b)
 
 
-def across_kernel(place, own, pair, value, *refs):
-    *others, out0, out1, out2, out3, product = refs
+def early_kernel(place, own, pair, value, other, out0, out1, out2, out3, product):
     half, width = value.shape
+    panel = own.shape[1]
     rows = pl.ds(pl.multiple_of(place[1] * half, half), half)
     b = halves(value[...])
-    start = product.shape[1] - 2 * width
-    for other in others:
-        product[:, :start] = other[...]
+    again = panel + 2 * CLUSTER
+    product[:, :panel] = other[:, :panel]
+    product[:, panel:again] = other[:, : 2 * CLUSTER]
+    start = again + other.shape[1] - panel
+    product[:, again:start] = other[:, panel:]
     product[:, start : start + width] = contract(halves(own[rows, :]), b)
     product[:, start + width :] = contract(halves(pair[rows, :]), b)
+    write_strips(place, product, (out0, out1, out2, out3), again)
+
+
+def prepare_kernel(place, own, pair, first, second):
+    panel, half = own.shape[1], own.shape[0] // 2
+    rows = pl.ds(pl.multiple_of(place[1] * half, half), half)
+    for k, panel_of in enumerate((own, pair)):
+        into = slice(k * panel, (k + 1) * panel)
+        first[into, :], second[into, :] = halves(panel_of[rows, :].T)
+
+
+def late_kernel(place, first, second, value, out0, out1, out2, out3, product):
+    panel, width = first.shape[0] // 2, value.shape[1]
+    b = halves(value[...])
+    for k in range(2):
+        rows = slice(k * panel, (k + 1) * panel)
+        product[:, k * width : (k + 1) * width] = multiply((first[rows, :], second[rows, :]), b)
     write_strips(place, product, (out0, out1, out2, out3))
 
 
@@ -166,21 +197,26 @@
             source, :, first : first + width
         ]
 
+    nothing = jnp.zeros((part, CLUSTER), jnp.float32)
     for q in range(4):
         chip, core = divmod(q, 2)
-        put(q, q * panel, q, 0, panel)
+        for t in range(4):
+            start = q * panel + (place[7] + t) % 4 * CLUSTER
+            columns = pl.ds(pl.multiple_of(start, CLUSTER), CLUSTER)
+            kept = held[q, :, t * CLUSTER : (t + 1) * CLUSTER] if t < 3 else nothing
+            upper[part * q : part * (q + 1), columns] = kept
         if core == 0:
-            put(q, (q + 1) * panel, q, panel, thin)
-            put(q, (q + 1) * panel + thin, q + 1, panel, thin)
+            put(q, (q + 1) * panel, q, KEPT, thin)
+            put(q, (q + 1) * panel + thin, q + 1, KEPT, thin)
         else:
             upper[part * q : part * (q + 1), (q - 1) * panel : q * panel] = jnp.zeros(
                 (part, panel), jnp.float32
             )
         for c in range(2):
-            first = panel + thin
-            for at, width in PIECES:
+            first = KEPT + thin
+            for (at, width), straight in zip(PIECES, (c == core, c != core)):
                 column = (2 * (1 - chip) + c) * panel + at
-                put(q, column, q if c != core else q ^ 1, first + width * (c == core), width)
+                put(q, column, q if straight else q ^ 1, first + width * (not straight), width)
                 first += 2 * width
     for k in range(8):
         block = order[place[1] * 8 + k]
@@ -234,7 +270,16 @@
         ordered[k * CLUSTER : (k + 1) * CLUSTER, :] = jnp.where(
             block >= 8, pltpu.roll(taken, ROWS, 1), taken
         )
-    out[...] = contract(halves(ordered[...]), (near[...], near_low[...]))[:ROWS]
+    first, second = halves(ordered[...])
+    left = lax.broadcasted_iota(jnp.int32, ordered.shape, 1) < ROWS
+    beside = pltpu.roll(second.astype(jnp.float32), ROWS, 1)
+    beside = jnp.where(left, first.astype(jnp.float32), beside).astype(jnp.bfloat16)
+
+    def one(u, v):
+        return lax.dot_general(u, v, (((0,), (0,)), ((), ())), preferred_element_type=jnp.float32)
+
+    both = one(beside, near[...])
+    out[...] = both[:ROWS] + (both[ROWS:] + one(first, near_low[...])[:ROWS])
 
 
 def last_kernel(place, scale, result, turned, out, rows):
@@ -277,17 +322,11 @@
     return jax.ShapeDtypeStruct(dims, dtype)
 
 
-def strips(kernel, width, place, cost, *arrays, extra=(), **options):
-    panel = arrays[0].shape[1]
-    outs = [shape(4, panel // 16, width)] * 4
-    return kernel_call(kernel, [place], [*outs, *extra], [(panel, width)], cost, *arrays, **options)
-
-
 def sum_along(values, swapped):
-    total = values[0]
-    for step in (1, 3, 2):
-        total += lax.ppermute(values[step], ("pts", "lm"), plane_step(step, swapped))
-    return total
+    got = [
+        lax.ppermute(values[step], ("pts", "lm"), plane_step(step, swapped)) for step in (1, 3, 2)
+    ]
+    return values[0] + got[0] + got[1] + got[2], got
 
 
 def per_device(kernel_features, factor, diag_inverse, block_order):
@@ -301,23 +340,56 @@
     group = i // 8
     row = jnp.where(group < j, 1, jnp.where(group > j, 0, j % 2))
     place = jnp.stack(
-        [core, chip, jnp.where(first_core, x, y), jnp.where(first_core, y, x), j, group, row]
+        [core, chip, jnp.where(first_core, x, y), jnp.where(first_core, y, x), j, group, row, x]
     ).astype(jnp.int32)
     order = block_order
 
     pair = lax.ppermute(own, "lm", OTHER_CORE)
     sent = lax.dynamic_slice_in_dim(own, (1 - chip) * half, half)
-    across = [lax.ppermute(sent[:, at : at + w], "lm", OTHER_CHIP) for at, w in PIECES]
-    across = [lax.ppermute(value, "lm", OTHER_CORE) for value in across]
+    across = [sent[:, at : at + w] for at, w in PIECES]
+    pair, across[1] = lax.optimization_barrier((pair, across[1]))
+    across = [lax.ppermute(value, "lm", OTHER_CHIP) for value in across]
 
     product = kernel_call(
         near_kernel, [place], shape(panel, panel + thin), [], COSTS[0], own, pair
     )
-    widths = [panel + thin + 2 * PIECES[0][1], 2 * PIECES[1][1]]
-    early = strips(across_kernel, widths[0], place, COSTS[1], own, pair, across[0], product)
-    early_sum = sum_along(early, False)
-    late = strips(across_kernel, widths[1], place, COSTS[3], own, pair, across[1], after=(early_sum,))
-    late_sum = sum_along(late, False)
+    widths = [KEPT + thin + 2 * PIECES[0][1], 2 * PIECES[1][1]]
+    early = kernel_call(
+        early_kernel,
+        [place],
+        [shape(4, panel // 16, widths[0])] * 4,
+        [(panel, panel + 2 * CLUSTER + thin + 2 * PIECES[0][1])],
+        COSTS[1],
+        own,
+        pair,
+        across[0],
+        product,
+    )
+    early_sum, arrived = sum_along(early, False)
+    prepared = kernel_call(
+        prepare_kernel,
+        [place],
+        [shape(2 * panel, half, dtype=jnp.bfloat16)] * 2,
+        [],
+        COSTS[3],
+        own,
+        pair,
+        after=(early[0],),
+    )
+    across[1], *prepared_and = lax.optimization_barrier((across[1], *prepared, *arrived))
+    prepared = prepared_and[:2]
+    across[1] = lax.ppermute(across[1], "lm", OTHER_CORE)
+    late = kernel_call(
+        late_kernel,
+        [place],
+        [shape(4, panel // 16, widths[1])] * 4,
+        [(panel, widths[1])],
+        COSTS[3],
+        *prepared,
+        across[1],
+        after=(early_sum,),
+    )
+    late_sum, _ = sum_along(late, False)
     parts = [jnp.concatenate([a, b], -1) for a, b in zip(early_sum, late_sum)]
     inverse = diag_inverse[0]
     near, near_low, far, far_low = kernel_call(
@@ -332,7 +404,7 @@
         after=(early[0],),
     )
     parts, far_low = lax.optimization_barrier((parts, far_low))
-    mine = sum_along(parts, True)
+    mine, _ = sum_along(parts, True)
     here, there = lax.optimization_barrier(
         tuple(lax.dynamic_slice_in_dim(mine, at * part, part) for at in (high, 1 - high))
     )

time: 132 us -> 127 us (0.962)
  starting transfers between devices: 35.6 us -> 32.9 us
  waiting for transfers between devices: 51.1 us -> 49.6 us
  local copies, waits for them, and re-layouts: 6.21 us -> 4.87 us
    ppermute x4 -> x3, waiting for transfers between devices: 5.88 us -> 1.7 us  [the longest x1 1.69 us: per_device(): across[1] = lax.ppermute(across[1], 'lm', OTHER_CORE)]
    ppermute x9, waiting for transfers between devices: 12.1 us -> 15.1 us  [sum_along(): lax.ppermute(values[step], ('pts', 'lm'), plane_step(step, swapped))]
    pallas_call x9 -> x10, Pallas kernels: 25.4 us -> 25.9 us  [kernel_call(): pl.pallas_call(body, out_shape=out_shape, in_specs=[smem] * len(scalars)...]
    ppermute x4 -> x3, starting transfers between devices: 3.31 us -> 3.09 us  [the longest x2 1.89 us: per_device(): across = [lax.ppermute(value, 'lm', OTHER_CHIP) for value in across]]
  transfers between devices with their start and end apart: 27 -> 26, of which waited for: 19 -> 19; matrix products, arithmetic and copies ran while one was open for 4% -> 3% of each run, Pallas kernels for 15% -> 16%
where the time goes in v4:
time: 127 us
  waiting for transfers between devices  49.6 us (39%)
  starting transfers between devices  32.9 us (26%)
  Pallas kernels  25.9 us (20%)
  blocking collectives  12 us (9%)
  local copies, waits for them, and re-layouts  4.87 us (4%)
    pallas_call x10, Pallas kernels, kernel_call(): pl.pallas_call(body, out_shape=out_shape, in_specs=[smem] * len(scalars)...  25.9 us
    ppermute x9, waiting for transfers between devices, sum_along(): lax.ppermute(values[step], ('pts', 'lm'), plane_step(step, swapped))  15.1 us
    ppermute x9, starting transfers between devices, sum_along(): lax.ppermute(values[step], ('pts', 'lm'), plane_step(step, swapped))  12.4 us
    all_to_all x1, blocking collectives, turned(): lax.all_to_all(packed, ('pts', 'lm'), 0, 0, axis_index_groups=groups, til...  12 us
    ppermute x2, waiting for transfers between devices, hop(): got = lax.ppermute(value, 'lm', OTHER_CHIP)  9.39 us
    all_to_all x1, waiting for transfers between devices, turned(): lax.all_to_all(packed, ('pts', 'lm'), 0, 0, axis_index_groups=groups, til...  8.77 us
    ppermute x1, waiting for transfers between devices, per_device(): away = lax.ppermute(value, 'lm', OTHER_CHIP)  5.14 us
    all_to_all x1, starting transfers between devices, turned(): lax.all_to_all(packed, ('pts', 'lm'), 0, 0, axis_index_groups=groups, til...  4.77 us
  transfers between devices with their start and end apart: 26, of which 19 were waited for; matrix products, arithmetic and copies ran while one was open for 3% of the time, Pallas kernels for 16%

profile of v4, /device:TPU:1, one launch (start us, length us, event | category | flops | bytes accessed | tf_op | source)
XLA Modules:
  0.0 126.6 jit_solution(8275613400366990192)
XLA Ops:
  0.0 1.4 %collective-permute-start = (f32[1024,512]{1,0:T(8,128)}, f32[1024,512]{1,0:T(8,128)}, u32[]{:S(2)}, u32[]{:S(2)}) collective-permute-start(f32[1024,512]{1,0:T(8,128)} %refs_1_.7), channel_id=1, source_target_pairs={{0,1},{1,0},{2,3},{3,2},{4,5},{5,4},{6,7},{7,6},{8,9},{9,8},{10,11... | collective-permute-start | bytes 6291464 | tf_op jit(solution)/shard_map/ppermute | solution.py:347
  1.4 1.0 constant_dynamic-slice_fusion.3
  2.4 1.8 %collective-permute-start.1 = (f32[512,128]{1,0:T(8,128)S(1)}, f32[512,128]{1,0:T(8,128)S(1)}, u32[]{:S(2)}, u32[]{:S(2)}) collective-permute-start(f32[512,128]{1,0:T(8,128)S(1)} %constant_dynamic-slice_fusion.3), channel_id=1, source_target_pairs={{0,2},{1,3},{2,0},{3,1},{4,6},{5,7},{6,4},{7,5},{8,10},{9,11},{10,... | collective-permute-start | bytes 786440 | tf_op jit(solution)/shard_map/ppermute | solution.py:351
  4.2 3.1 %slice.11 = f32[1024,512]{1,0:T(8,128)} slice(f32[2048,512]{1,0:T(8,128)} %refs_3_.1), slice={[0:1024], [0:512]} | slice | bytes 4194304 | tf_op jit(solution)/shard_map/slice | solution.py:403
  7.9 4.5 %shard_map.46.refs_4_ = f32[512,768]{1,0:T(8,128)S(1)} custom-call(s32[8]{0:T(128)S(1)} %stack.53.refs_0_, f32[1024,512]{1,0:T(8,128)S(1)} %copy-done.1, f32[1024,512]{1,0:T(8,128)} %collective-permute-done.refs_2_), custom_call_target="tpu_custom_call" | custom-call | flops 40000000000 | bytes 120000000 | tf_op jit(solution)/shard_map/pallas_call | solution.py:304
  12.3 2.9 %shard_map.47 = (f32[4,32,896]{2,1,0:T(8,128)S(1)}, f32[4,32,896]{2,1,0:T(8,128)S(1)}, f32[4,32,896]{2,1,0:T(8,128)S(1)}, f32[4,32,896]{2,1,0:T(8,128)S(1)}) custom-call(s32[8]{0:T(128)S(1)} %stack.53.refs_0_, f32[1024,512]{1,0:T(8,128)S(1)} %copy-done.1, f32[1024,512]{1,0:T(8,128)} %collective-permute-done.refs_2_, ...), custom_call_target="tpu_custom_call" | custom-call | flops 6000000000 | bytes 18000000 | tf_op jit(solution)/shard_map/pallas_call | solution.py:304
  15.2 1.4 %collective-permute-start.2 = (f32[4,32,896]{2,1,0:T(8,128)S(1)}, f32[4,32,896]{2,1,0:T(8,128)S(1)}, u32[]{:S(2)}, u32[]{:S(2)}) collective-permute-start(f32[4,32,896]{2,1,0:T(8,128)S(1)} %get-tuple-element.36), channel_id=1, source_target_pairs={{0,16},{1,5},{2,18},{3,7},{4,20},{5,9},{6,22},{7,11},{8,24},{9,13}... | collective-permute-start | bytes 1376264 | tf_op jit(solution)/shard_map/ppermute | solution.py:327
  16.6 1.5 %collective-permute-start.3 = (f32[4,32,896]{2,1,0:T(8,128)S(1)}, f32[4,32,896]{2,1,0:T(8,128)S(1)}, u32[]{:S(2)}, u32[]{:S(2)}) collective-permute-start(f32[4,32,896]{2,1,0:T(8,128)S(1)} %get-tuple-element.37), channel_id=1, source_target_pairs={{0,48},{1,13},{2,50},{3,15},{4,52},{5,1},{6,54},{7,3},{8,56},{9,5}... | collective-permute-start | bytes 1376264 | tf_op jit(solution)/shard_map/ppermute | solution.py:327
  18.1 1.6 %collective-permute-start.4 = (f32[4,32,896]{2,1,0:T(8,128)S(1)}, f32[4,32,896]{2,1,0:T(8,128)S(1)}, u32[]{:S(2)}, u32[]{:S(2)}) collective-permute-start(f32[4,32,896]{2,1,0:T(8,128)S(1)} %get-tuple-element.38), channel_id=1, source_target_pairs={{0,32},{1,9},{2,34},{3,11},{4,36},{5,13},{6,38},{7,15},{8,40},{9,1... | collective-permute-start | bytes 1376264 | tf_op jit(solution)/shard_map/ppermute | solution.py:327
  19.7 2.3 %shard_map.48 = (bf16[1024,512]{1,0:T(8,128)(2,1)S(1)}, bf16[1024,512]{1,0:T(8,128)(2,1)S(1)}) custom-call(s32[8]{0:T(128)S(1)} %stack.53.refs_0_, f32[1024,512]{1,0:T(8,128)S(1)} %copy-done.1, f32[1024,512]{1,0:T(8,128)} %collective-permute-done.refs_2_, f32[4,32,896]{2,1,0:T(8,128)S(1)} %get-tuple-element.35.refs_3_.refs_5_), custom_call_target="tpu_custom_call" | custom-call | flops 4000000000 | bytes 12000000 | tf_op jit(solution)/shard_map/pallas_call | solution.py:304
  22.0 2.2 %collective-permute-done.2 = f32[4,32,896]{2,1,0:T(8,128)S(1)} collective-permute-done((f32[4,32,896]{2,1,0:T(8,128)S(1)}, f32[4,32,896]{2,1,0:T(8,128)S(1)}, u32[]{:S(2)}, u32[]{:S(2)}) %collective-permute-start.2) | collective-permute-done | bytes 458784 | tf_op jit(solution)/shard_map/ppermute | solution.py:327
  24.2 4.3 %collective-permute-done.3 = f32[4,32,896]{2,1,0:T(8,128)S(1)} collective-permute-done((f32[4,32,896]{2,1,0:T(8,128)S(1)}, f32[4,32,896]{2,1,0:T(8,128)S(1)}, u32[]{:S(2)}, u32[]{:S(2)}) %collective-permute-start.3) | collective-permute-done | bytes 458784 | tf_op jit(solution)/shard_map/ppermute | solution.py:327
  28.5 1.8 %collective-permute-done.4 = f32[4,32,896]{2,1,0:T(8,128)S(1)} collective-permute-done((f32[4,32,896]{2,1,0:T(8,128)S(1)}, f32[4,32,896]{2,1,0:T(8,128)S(1)}, u32[]{:S(2)}, u32[]{:S(2)}) %collective-permute-start.4) | collective-permute-done | bytes 458784 | tf_op jit(solution)/shard_map/ppermute | solution.py:327
  30.3 1.2 collective-permute-start.6
  31.7 1.7 %collective-permute-done.6.refs_3_ = f32[512,384]{1,0:T(8,128)S(1)} collective-permute-done((f32[512,384]{1,0:T(8,128)S(1)}, f32[512,384]{1,0:T(8,128)S(1)}, u32[]{:S(2)}, u32[]{:S(2)}) %collective-permute-start.6) | collective-permute-done | bytes 786464 | tf_op jit(solution)/shard_map/ppermute | solution.py:381
  33.4 2.4 %shard_map.49 = (f32[4,32,768]{2,1,0:T(8,128)S(1)}, f32[4,32,768]{2,1,0:T(8,128)S(1)}, f32[4,32,768]{2,1,0:T(8,128)S(1)}, f32[4,32,768]{2,1,0:T(8,128)S(1)}) custom-call(s32[8]{0:T(128)S(1)} %stack.53.refs_0_, bf16[1024,512]{1,0:T(8,128)(2,1)S(1)} %get-tuple-element.42.refs_1_, bf16[1024,512]{1,0:T(8,128)(2,1)S(1)} %get-tuple-element.43.refs_2_, ...), custom_call_target="tpu_custom_call" | custom-call | flops 4000000000 | bytes 12000000 | tf_op jit(solution)/shard_map/pallas_call | solution.py:304
  35.8 3.0 %collective-permute-start.9 = (f32[4,32,768]{2,1,0:T(8,128)S(1)}, f32[4,32,768]{2,1,0:T(8,128)S(1)}, u32[]{:S(2)}, u32[]{:S(2)}) collective-permute-start(f32[4,32,768]{2,1,0:T(8,128)S(1)} %get-tuple-element.48), channel_id=1, source_target_pairs={{0,32},{1,9},{2,34},{3,11},{4,36},{5,13},{6,38},{7,15},{8,40},{9,1... | collective-permute-start | bytes 1179656 | tf_op jit(solution)/shard_map/ppermute | solution.py:327
  38.8 0.8 collective-permute-start.8
  39.6 0.7 collective-permute-start.7
  40.3 7.9 %shard_map.50 = (bf16[1024,512]{1,0:T(8,128)(2,1)S(1)}, bf16[1024,512]{1,0:T(8,128)(2,1)S(1)}, bf16[1024,512]{1,0:T(8,128)(2,1)S(1)}, bf16[1024,512]{1,0:T(8,128)(2,1)S(1)}) custom-call(s32[8]{0:T(128)S(1)} %stack.53.refs_0_, f32[512,512]{1,0:T(8,128)S(1)} %bitcast.34, f32[512,512]{1,0:T(8,128)S(1)} %collective-permute-done.10.refs_2_, ...), custom_call_target="tpu_custom_call" | custom-call | flops 4000000000 | bytes 12000000 | tf_op jit(solution)/shard_map/pallas_call | solution.py:304
  49.6 0.8 pad_maximum_fusion.3
  51.0 3.0 %collective-permute-start.13 = (f32[32,1664]{1,0:T(8,128)}, f32[32,1664]{1,0:T(8,128)S(1)}, u32[]{:S(2)}, u32[]{:S(2)}) collective-permute-start(f32[32,1664]{1,0:T(8,128)} %get-tuple-element.52), channel_id=1, source_target_pairs={{0,12},{1,49},{2,14},{3,51},{4,0},{5,53},{6,2},{7,55},{8,4},{9,57}... | collective-permute-start | bytes 638984 | tf_op jit(solution)/shard_map/ppermute | solution.py:327
  53.9 3.2 %collective-permute-done.14 = f32[32,1664]{1,0:T(8,128)S(1)} collective-permute-done((f32[32,1664]{1,0:T(8,128)}, f32[32,1664]{1,0:T(8,128)S(1)}, u32[]{:S(2)}, u32[]{:S(2)}) %collective-permute-start.14) | collective-permute-done | bytes 213024 | tf_op jit(solution)/shard_map/ppermute | solution.py:327
  57.1 1.9 %collective-permute-done.13 = f32[32,1664]{1,0:T(8,128)S(1)} collective-permute-done((f32[32,1664]{1,0:T(8,128)}, f32[32,1664]{1,0:T(8,128)S(1)}, u32[]{:S(2)}, u32[]{:S(2)}) %collective-permute-start.13) | collective-permute-done | bytes 213024 | tf_op jit(solution)/shard_map/ppermute | solution.py:327
  59.0 1.2 collective-permute-done.12
  60.2 3.5 %collective-permute-start.15 = (f32[16,1664]{1,0:T(8,128)S(1)}, f32[16,1664]{1,0:T(8,128)S(1)}, u32[]{:S(2)}, u32[]{:S(2)}) collective-permute-start(f32[16,1664]{1,0:T(8,128)S(1)} %get-tuple-element.55), channel_id=1, source_target_pairs={{0,64},{1,65},{2,66},{3,67},{4,68},{5,69},{6,70},{7,71},{8,72},{9,... | collective-permute-start | bytes 319496 | tf_op jit(solution)/shard_map/ppermute | solution.py:413
  64.3 1.5 %collective-permute-done.15 = f32[16,1664]{1,0:T(8,128)S(1)} collective-permute-done((f32[16,1664]{1,0:T(8,128)S(1)}, f32[16,1664]{1,0:T(8,128)S(1)}, u32[]{:S(2)}, u32[]{:S(2)}) %collective-permute-start.15) | collective-permute-done | bytes 106528 | tf_op jit(solution)/shard_map/ppermute | solution.py:413
  65.8 2.0 %collective-permute-done.16 = f32[16,1664]{1,0:T(8,128)S(1)} collective-permute-done((f32[16,1664]{1,0:T(8,128)S(1)}, f32[16,1664]{1,0:T(8,128)S(1)}, u32[]{:S(2)}, u32[]{:S(2)}) %collective-permute-start.16) | collective-permute-done | bytes 106528 | tf_op jit(solution)/shard_map/ppermute | solution.py:411
  67.9 1.7 %collective-permute-done.17 = f32[16,1664]{1,0:T(8,128)S(1)} collective-permute-done((f32[16,1664]{1,0:T(8,128)S(1)}, f32[16,1664]{1,0:T(8,128)S(1)}, u32[]{:S(2)}, u32[]{:S(2)}) %collective-permute-start.17) | collective-permute-done | bytes 106528 | tf_op jit(solution)/shard_map/ppermute | solution.py:412
  69.6 3.2 %collective-permute-start.18 = (f32[2,16,1664]{2,1,0:T(8,128)S(1)}, f32[2,16,1664]{2,1,0:T(8,128)S(1)}, u32[]{:S(2)}, u32[]{:S(2)}) collective-permute-start(f32[2,16,1664]{2,1,0:T(8,128)S(1)} %pad_maximum_fusion.5), channel_id=1, source_target_pairs={{0,1},{1,0},{2,3},{3,2},{4,5},{5,4},{6,7},{7,6},{8,9},{9,8},{10,11... | collective-permute-start | bytes 638984 | tf_op jit(solution)/shard_map/ppermute | solution.py:417
  72.9 1.1 collective-permute-done.18.refs_4_
  74.0 1.0 shard_map.51.refs_1_
  75.1 4.7 %collective-permute-done.19.refs_2_ = f32[64,512]{1,0:T(8,128)S(1)} collective-permute-done((f32[64,512]{1,0:T(8,128)S(1)}, f32[64,512]{1,0:T(8,128)S(1)}, u32[]{:S(2)}, u32[]{:S(2)}) %collective-permute-start.19) | collective-permute-done | bytes 131104 | tf_op jit(solution)/shard_map/ppermute | solution.py:420
  79.8 1.2 collective-permute-start.20
  81.0 1.0 collective-permute-done.20.refs_3_
  82.0 1.4 %shard_map.52 = (f32[64,512]{1,0:T(8,128)}, f32[16,32,128]{2,1,0:T(8,128)}) custom-call(s32[8]{0:T(128)S(1)} %stack.53.refs_0_, f32[64,512]{1,0:T(8,128)S(1)} %shard_map.51.refs_1_, f32[64,512]{1,0:T(8,128)S(1)} %collective-permute-done.19.refs_2_, f32[64,512]{1,0:T(8,128)S(1)} %collective-permute-done.20.refs_3_, bf16[1024,512]{1,0:T(8,128)(2,1)S(1)} %copy-done.5, ...), custom_call_target="tpu_custom_call" | custom-call | flops 2000000000 | bytes 6000000 | tf_op jit(solution)/shard_map/pallas_call | solution.py:304
  83.4 4.8 %all-to-all-start = ((f32[16,32,128]{2,1,0:T(8,128)}), f32[16,32,128]{2,1,0:T(8,128)S(1)}, u32[]{:S(2)}, u32[]{:S(2)}) async-start(f32[16,32,128]{2,1,0:T(8,128)} %get-tuple-element.60), calls=%async_computation | async-start | bytes 524288 | tf_op jit(solution)/shard_map/all_to_all | solution.py:425
  88.1 8.8 %all-to-all-done = f32[16,32,128]{2,1,0:T(8,128)S(1)} async-done(((f32[16,32,128]{2,1,0:T(8,128)}), f32[16,32,128]{2,1,0:T(8,128)S(1)}, u32[]{:S(2)}, u32[]{:S(2)}) %all-to-all-start) | async-done | bytes 262176 | tf_op jit(solution)/shard_map/all_to_all | solution.py:425
  97.0 5.1 %collective-permute-done.21.refs_3_ = f32[8,32,128]{2,1,0:T(8,128)S(1)} collective-permute-done((f32[8,32,128]{2,1,0:T(8,128)S(1)}, f32[8,32,128]{2,1,0:T(8,128)S(1)}, u32[]{:S(2)}, u32[]{:S(2)}) %collective-permute-start.21) | collective-permute-done | bytes 131104 | tf_op jit(solution)/shard_map/ppermute | solution.py:442
  102.2 0.8 collective-permute-start.22
  103.0 1.2 collective-permute-done.22.refs_4_
  104.2 1.4 %shard_map.53.refs_1_ = f32[64,512]{1,0:T(8,128)S(1)} custom-call(s32[8]{0:T(128)S(1)} %stack.53.refs_0_, s32[16]{0:T(128)S(1)} %copy-done.3, f32[8,32,128]{2,1,0:T(8,128)S(1)} %constant_dynamic-slice_fusion.refs_2_, f32[8,32,128]{2,1,0:T(8,128)S(1)} %collective-permute-done.21.refs_3_, f32[2,8,32,128]{3,2,1,0:T(8,128)S(1)} %collective-permute-done.22.refs_4_, ...), custom_call_target="tpu_custom_call" | custom-call | flops 2000000000 | bytes 6000000 | tf_op jit(solution)/shard_map/pallas_call | solution.py:304
  105.7 4.7 %collective-permute-done.23.refs_2_ = f32[64,512]{1,0:T(8,128)S(1)} collective-permute-done((f32[64,512]{1,0:T(8,128)S(1)}, f32[64,512]{1,0:T(8,128)S(1)}, u32[]{:S(2)}, u32[]{:S(2)}) %collective-permute-start.23) | collective-permute-done | bytes 131104 | tf_op jit(solution)/shard_map/ppermute | solution.py:420
  110.4 1.2 collective-permute-start.24
  111.6 1.0 collective-permute-done.24.refs_3_
  112.6 0.7 shard_map.54
  113.3 12.0 %all_to_all.10.refs_3_ = f32[16,32,128]{2,1,0:T(8,128)S(1)} all-to-all(f32[16,32,128]{2,1,0:T(8,128)S(1)} %get-tuple-element.62), channel_id=1, replica_groups={{1,5,9,13,17,21,25,29,32,36,40,44,48,52,56,60},{2,6,10,14,18,22,26,30,6..., dimensions={0} | all-to-all | bytes 524288 | tf_op jit(solution)/shard_map/all_to_all | solution.py:425
  125.2 1.4 %shard_map.55 = f32[64,512]{1,0:T(8,128)} custom-call(s32[8]{0:T(128)S(1)} %stack.53.refs_0_, f32[1]{0:T(128)} %constant.82.clone.1.refs_1_, f32[64,512]{1,0:T(8,128)S(1)} %get-tuple-element.61.refs_2_, f32[16,32,128]{2,1,0:T(8,128)S(1)} %all_to_all.10.refs_3_), custom_call_target="tpu_custom_call" | custom-call | tf_op jit(solution)/shard_map/pallas_call | solution.py:304
  (53 shorter events, 3.7 us)
Async XLA Ops:
  0.0 7.8 %collective-permute-start = (f32[1024,512]{1,0:T(8,128)}, f32[1024,512]{1,0:T(8,128)}, u32[]{:S(2)}, u32[]{:S(2)}) collective-permute-start(f32[1024,512]{1,0:T(8,128)} %refs_1_.7), channel_id=1, source_target_pairs={{0,1},{1,0},{2,3},{3,2},{4,5},{5,4},{6,7},{7,6},{8,9},{9,8},{10,11... | collective-permute-start | bytes 6291464 | tf_op jit(solution)/shard_map/ppermute | solution.py:347
  2.4 5.2 %copy-start.1 = (f32[1024,512]{1,0:T(8,128)S(1)}, f32[1024,512]{1,0:T(8,128)}, u32[]{:S(2)}) copy-start(f32[1024,512]{1,0:T(8,128)} %refs_1_.7) | copy-start | bytes 6291460
  2.4 9.9 %collective-permute-start.1 = (f32[512,128]{1,0:T(8,128)S(1)}, f32[512,128]{1,0:T(8,128)S(1)}, u32[]{:S(2)}, u32[]{:S(2)}) collective-permute-start(f32[512,128]{1,0:T(8,128)S(1)} %constant_dynamic-slice_fusion.3), channel_id=1, source_target_pairs={{0,2},{1,3},{2,0},{3,1},{4,6},{5,7},{6,4},{7,5},{8,10},{9,11},{10,... | collective-permute-start | bytes 786440 | tf_op jit(solution)/shard_map/ppermute | solution.py:351
  7.3 33.0 %collective-permute-start.11 = (f32[1024,512]{1,0:T(8,128)}, f32[1024,512]{1,0:T(8,128)}, u32[]{:S(2)}, u32[]{:S(2)}) collective-permute-start(f32[1024,512]{1,0:T(8,128)} %slice.11), channel_id=1, source_target_pairs={{0,1},{1,0},{2,3},{3,2},{4,5},{5,4},{6,7},{7,6},{8,9},{9,8},{10,11... | collective-permute-start | bytes 6291464 | tf_op jit(solution)/shard_map/ppermute | solution.py:403
  7.8 22.5 %collective-permute-start.5 = (f32[512,384]{1,0:T(8,128)S(1)}, f32[512,384]{1,0:T(8,128)S(1)}, u32[]{:S(2)}, u32[]{:S(2)}) collective-permute-start(f32[512,384]{1,0:T(8,128)S(1)} %dynamic-slice), channel_id=1, source_target_pairs={{0,2},{1,3},{2,0},{3,1},{4,6},{5,7},{6,4},{7,5},{8,10},{9,11},{10,... | collective-permute-start | bytes 2359304 | tf_op jit(solution)/shard_map/ppermute | solution.py:351
  15.2 9.0 %collective-permute-start.2 = (f32[4,32,896]{2,1,0:T(8,128)S(1)}, f32[4,32,896]{2,1,0:T(8,128)S(1)}, u32[]{:S(2)}, u32[]{:S(2)}) collective-permute-start(f32[4,32,896]{2,1,0:T(8,128)S(1)} %get-tuple-element.36), channel_id=1, source_target_pairs={{0,16},{1,5},{2,18},{3,7},{4,20},{5,9},{6,22},{7,11},{8,24},{9,13}... | collective-permute-start | bytes 1376264 | tf_op jit(solution)/shard_map/ppermute | solution.py:327
  16.6 11.9 %collective-permute-start.3 = (f32[4,32,896]{2,1,0:T(8,128)S(1)}, f32[4,32,896]{2,1,0:T(8,128)S(1)}, u32[]{:S(2)}, u32[]{:S(2)}) collective-permute-start(f32[4,32,896]{2,1,0:T(8,128)S(1)} %get-tuple-element.37), channel_id=1, source_target_pairs={{0,48},{1,13},{2,50},{3,15},{4,52},{5,1},{6,54},{7,3},{8,56},{9,5}... | collective-permute-start | bytes 1376264 | tf_op jit(solution)/shard_map/ppermute | solution.py:327
  18.1 12.2 %collective-permute-start.4 = (f32[4,32,896]{2,1,0:T(8,128)S(1)}, f32[4,32,896]{2,1,0:T(8,128)S(1)}, u32[]{:S(2)}, u32[]{:S(2)}) collective-permute-start(f32[4,32,896]{2,1,0:T(8,128)S(1)} %get-tuple-element.38), channel_id=1, source_target_pairs={{0,32},{1,9},{2,34},{3,11},{4,36},{5,13},{6,38},{7,15},{8,40},{9,1... | collective-permute-start | bytes 1376264 | tf_op jit(solution)/shard_map/ppermute | solution.py:327
  19.7 11.8 %copy-start.2 = (f32[1,512,512]{2,1,0:T(8,128)S(1)}, f32[1,512,512]{2,1,0:T(8,128)}, u32[]{:S(2)}) copy-start(f32[1,512,512]{2,1,0:T(8,128)} %param.6) | copy-start | bytes 3145732
  30.3 3.1 %collective-permute-start.6 = (f32[512,384]{1,0:T(8,128)S(1)}, f32[512,384]{1,0:T(8,128)S(1)}, u32[]{:S(2)}, u32[]{:S(2)}) collective-permute-start(f32[512,384]{1,0:T(8,128)S(1)} %collective-permute-done.5), channel_id=1, source_target_pairs={{0,1},{1,0},{2,3},{3,2},{4,5},{5,4},{6,7},{7,6},{8,9},{9,8},{10,11... | collective-permute-start | bytes 2359304 | tf_op jit(solution)/shard_map/ppermute | solution.py:381
  31.5 8.8 %collective-permute-start.10 = (f32[512,512]{1,0:T(8,128)S(1)}, f32[512,512]{1,0:T(8,128)S(1)}, u32[]{:S(2)}, u32[]{:S(2)}) collective-permute-start(f32[512,512]{1,0:T(8,128)S(1)} %bitcast.33), channel_id=1, source_target_pairs={{0,1},{1,0},{2,3},{3,2},{4,5},{5,4},{6,7},{7,6},{8,9},{9,8},{10,11... | collective-permute-start | bytes 3145736 | tf_op jit(solution)/shard_map/ppermute | solution.py:402
  31.7 8.6 %copy-start = (f32[2048,512]{1,0:T(8,128)S(1)}, f32[2048,512]{1,0:T(8,128)}, u32[]{:S(2)}) copy-start(f32[2048,512]{1,0:T(8,128)} %refs_3_.1) | copy-start | bytes 12582916
  35.8 12.5 %collective-permute-start.9 = (f32[4,32,768]{2,1,0:T(8,128)S(1)}, f32[4,32,768]{2,1,0:T(8,128)S(1)}, u32[]{:S(2)}, u32[]{:S(2)}) collective-permute-start(f32[4,32,768]{2,1,0:T(8,128)S(1)} %get-tuple-element.48), channel_id=1, source_target_pairs={{0,32},{1,9},{2,34},{3,11},{4,36},{5,13},{6,38},{7,15},{8,40},{9,1... | collective-permute-start | bytes 1179656 | tf_op jit(solution)/shard_map/ppermute | solution.py:327
  38.8 10.1 %collective-permute-start.8 = (f32[4,32,768]{2,1,0:T(8,128)S(1)}, f32[4,32,768]{2,1,0:T(8,128)S(1)}, u32[]{:S(2)}, u32[]{:S(2)}) collective-permute-start(f32[4,32,768]{2,1,0:T(8,128)S(1)} %get-tuple-element.47), channel_id=1, source_target_pairs={{0,48},{1,13},{2,50},{3,15},{4,52},{5,1},{6,54},{7,3},{8,56},{9,5}... | collective-permute-start | bytes 1179656 | tf_op jit(solution)/shard_map/ppermute | solution.py:327
  39.6 9.3 %collective-permute-start.7 = (f32[4,32,768]{2,1,0:T(8,128)S(1)}, f32[4,32,768]{2,1,0:T(8,128)S(1)}, u32[]{:S(2)}, u32[]{:S(2)}) collective-permute-start(f32[4,32,768]{2,1,0:T(8,128)S(1)} %get-tuple-element.46), channel_id=1, source_target_pairs={{0,16},{1,5},{2,18},{3,7},{4,20},{5,9},{6,22},{7,11},{8,24},{9,13}... | collective-permute-start | bytes 1179656 | tf_op jit(solution)/shard_map/ppermute | solution.py:327
  48.3 1.0 copy-start.4
  48.3 1.3 %copy-start.7 = (bf16[1024,512]{1,0:T(8,128)(2,1)}, bf16[1024,512]{1,0:T(8,128)(2,1)S(1)}, u32[]{:S(2)}) copy-start(bf16[1024,512]{1,0:T(8,128)(2,1)S(1)} %get-tuple-element.59.refs_5_) | copy-start | bytes 3145732
  49.1 24.9 %copy-start.3 = (s32[16]{0:T(128)S(1)}, s32[16]{0:T(128)}, u32[]{:S(2)}) copy-start(s32[16]{0:T(128)} %refs_1_.9) | copy-start | bytes 196
  50.4 6.7 %collective-permute-start.14 = (f32[32,1664]{1,0:T(8,128)}, f32[32,1664]{1,0:T(8,128)S(1)}, u32[]{:S(2)}, u32[]{:S(2)}) collective-permute-start(f32[32,1664]{1,0:T(8,128)} %get-tuple-element.53), channel_id=1, source_target_pairs={{0,8},{1,33},{2,10},{3,35},{4,12},{5,37},{6,14},{7,39},{8,0},{9,41... | collective-permute-start | bytes 638984 | tf_op jit(solution)/shard_map/ppermute | solution.py:327
  51.0 8.0 %collective-permute-start.13 = (f32[32,1664]{1,0:T(8,128)}, f32[32,1664]{1,0:T(8,128)S(1)}, u32[]{:S(2)}, u32[]{:S(2)}) collective-permute-start(f32[32,1664]{1,0:T(8,128)} %get-tuple-element.52), channel_id=1, source_target_pairs={{0,12},{1,49},{2,14},{3,51},{4,0},{5,53},{6,2},{7,55},{8,4},{9,57}... | collective-permute-start | bytes 638984 | tf_op jit(solution)/shard_map/ppermute | solution.py:327
  53.9 6.2 %collective-permute-start.12 = (f32[32,1664]{1,0:T(8,128)S(1)}, f32[32,1664]{1,0:T(8,128)S(1)}, u32[]{:S(2)}, u32[]{:S(2)}) collective-permute-start(f32[32,1664]{1,0:T(8,128)S(1)} %get-tuple-element.51), channel_id=1, source_target_pairs={{0,4},{1,17},{2,6},{3,19},{4,8},{5,21},{6,10},{7,23},{8,12},{9,25}... | collective-permute-start | bytes 638984 | tf_op jit(solution)/shard_map/ppermute | solution.py:327
  60.2 5.6 %collective-permute-start.15 = (f32[16,1664]{1,0:T(8,128)S(1)}, f32[16,1664]{1,0:T(8,128)S(1)}, u32[]{:S(2)}, u32[]{:S(2)}) collective-permute-start(f32[16,1664]{1,0:T(8,128)S(1)} %get-tuple-element.55), channel_id=1, source_target_pairs={{0,64},{1,65},{2,66},{3,67},{4,68},{5,69},{6,70},{7,71},{8,72},{9,... | collective-permute-start | bytes 319496 | tf_op jit(solution)/shard_map/ppermute | solution.py:413
  63.7 4.2 %collective-permute-start.16 = (f32[16,1664]{1,0:T(8,128)S(1)}, f32[16,1664]{1,0:T(8,128)S(1)}, u32[]{:S(2)}, u32[]{:S(2)}) collective-permute-start(f32[16,1664]{1,0:T(8,128)S(1)} %get-tuple-element.54), channel_id=1, source_target_pairs={{0,2},{1,3},{2,0},{3,1},{4,6},{5,7},{6,4},{7,5},{8,10},{9,11},{10,... | collective-permute-start | bytes 319496 | tf_op jit(solution)/shard_map/ppermute | solution.py:411
  64.3 5.2 %collective-permute-start.17 = (f32[16,1664]{1,0:T(8,128)S(1)}, f32[16,1664]{1,0:T(8,128)S(1)}, u32[]{:S(2)}, u32[]{:S(2)}) collective-permute-start(f32[16,1664]{1,0:T(8,128)S(1)} %get-tuple-element.55), channel_id=1, source_target_pairs={{0,66},{1,67},{2,64},{3,65},{4,70},{5,71},{6,68},{7,69},{8,74},{9,... | collective-permute-start | bytes 319496 | tf_op jit(solution)/shard_map/ppermute | solution.py:412
  69.6 4.3 %collective-permute-start.18 = (f32[2,16,1664]{2,1,0:T(8,128)S(1)}, f32[2,16,1664]{2,1,0:T(8,128)S(1)}, u32[]{:S(2)}, u32[]{:S(2)}) collective-permute-start(f32[2,16,1664]{2,1,0:T(8,128)S(1)} %pad_maximum_fusion.5), channel_id=1, source_target_pairs={{0,1},{1,0},{2,3},{3,2},{4,5},{5,4},{6,7},{7,6},{8,9},{9,8},{10,11... | collective-permute-start | bytes 638984 | tf_op jit(solution)/shard_map/ppermute | solution.py:417
  74.0 8.0 %copy-start.5 = (bf16[1024,512]{1,0:T(8,128)(2,1)S(1)}, bf16[1024,512]{1,0:T(8,128)(2,1)}, u32[]{:S(2)}) copy-start(bf16[1024,512]{1,0:T(8,128)(2,1)} %copy-done.4) | copy-start | bytes 3145732
  74.0 8.0 %copy-start.8 = (bf16[1024,512]{1,0:T(8,128)(2,1)S(1)}, bf16[1024,512]{1,0:T(8,128)(2,1)}, u32[]{:S(2)}) copy-start(bf16[1024,512]{1,0:T(8,128)(2,1)} %copy-done.7) | copy-start | bytes 3145732
  75.0 4.8 %collective-permute-start.19 = (f32[64,512]{1,0:T(8,128)S(1)}, f32[64,512]{1,0:T(8,128)S(1)}, u32[]{:S(2)}, u32[]{:S(2)}) collective-permute-start(f32[64,512]{1,0:T(8,128)S(1)} %shard_map.51.refs_1_), channel_id=1, source_target_pairs={{0,2},{1,3},{2,0},{3,1},{4,6},{5,7},{6,4},{7,5},{8,10},{9,11},{10,... | collective-permute-start | bytes 393224 | tf_op jit(solution)/shard_map/ppermute | solution.py:420
  79.8 2.2 %collective-permute-start.20 = (f32[64,512]{1,0:T(8,128)S(1)}, f32[64,512]{1,0:T(8,128)S(1)}, u32[]{:S(2)}, u32[]{:S(2)}) collective-permute-start(f32[64,512]{1,0:T(8,128)S(1)} %collective-permute-done.19.refs_2_), channel_id=1, source_target_pairs={{0,1},{1,0},{2,3},{3,2},{4,5},{5,4},{6,7},{7,6},{8,9},{9,8},{10,11... | collective-permute-start | bytes 393224 | tf_op jit(solution)/shard_map/ppermute | solution.py:421
  83.4 13.6 %all-to-all-start = ((f32[16,32,128]{2,1,0:T(8,128)}), f32[16,32,128]{2,1,0:T(8,128)S(1)}, u32[]{:S(2)}, u32[]{:S(2)}) async-start(f32[16,32,128]{2,1,0:T(8,128)} %get-tuple-element.60), calls=%async_computation | async-start | bytes 524288 | tf_op jit(solution)/shard_map/all_to_all | solution.py:425
  96.9 5.3 %collective-permute-start.21 = (f32[8,32,128]{2,1,0:T(8,128)S(1)}, f32[8,32,128]{2,1,0:T(8,128)S(1)}, u32[]{:S(2)}, u32[]{:S(2)}) collective-permute-start(f32[8,32,128]{2,1,0:T(8,128)S(1)} %constant_dynamic-slice_fusion.refs_2_), channel_id=1, source_target_pairs={{0,2},{1,3},{2,0},{3,1},{4,6},{5,7},{6,4},{7,5},{8,10},{9,11},{10,... | collective-permute-start | bytes 393224 | tf_op jit(solution)/shard_map/ppermute | solution.py:442
  102.2 10.4 %copy-start.6 = (bf16[1024,512]{1,0:T(8,128)(2,1)S(1)}, bf16[1024,512]{1,0:T(8,128)(2,1)}, u32[]{:S(2)}) copy-start(bf16[1024,512]{1,0:T(8,128)(2,1)} %copy-done.4) | copy-start | bytes 3145732
  102.2 10.4 %copy-start.9 = (bf16[1024,512]{1,0:T(8,128)(2,1)S(1)}, bf16[1024,512]{1,0:T(8,128)(2,1)}, u32[]{:S(2)}) copy-start(bf16[1024,512]{1,0:T(8,128)(2,1)} %copy-done.7) | copy-start | bytes 3145732
  102.2 2.0 %collective-permute-start.22 = (f32[2,8,32,128]{3,2,1,0:T(8,128)S(1)}, f32[2,8,32,128]{3,2,1,0:T(8,128)S(1)}, u32[]{:S(2)}, u32[]{:S(2)}) collective-permute-start(f32[2,8,32,128]{3,2,1,0:T(8,128)S(1)} %pad_maximum_fusion), channel_id=1, source_target_pairs={{0,1},{1,0},{2,3},{3,2},{4,5},{5,4},{6,7},{7,6},{8,9},{9,8},{10,11... | collective-permute-start | bytes 786440 | tf_op jit(solution)/shard_map/ppermute | solution.py:417
  105.6 4.8 %collective-permute-start.23 = (f32[64,512]{1,0:T(8,128)S(1)}, f32[64,512]{1,0:T(8,128)S(1)}, u32[]{:S(2)}, u32[]{:S(2)}) collective-permute-start(f32[64,512]{1,0:T(8,128)S(1)} %shard_map.53.refs_1_), channel_id=1, source_target_pairs={{0,2},{1,3},{2,0},{3,1},{4,6},{5,7},{6,4},{7,5},{8,10},{9,11},{10,... | collective-permute-start | bytes 393224 | tf_op jit(solution)/shard_map/ppermute | solution.py:420
  110.4 2.2 %collective-permute-start.24 = (f32[64,512]{1,0:T(8,128)S(1)}, f32[64,512]{1,0:T(8,128)S(1)}, u32[]{:S(2)}, u32[]{:S(2)}) collective-permute-start(f32[64,512]{1,0:T(8,128)S(1)} %collective-permute-done.23.refs_2_), channel_id=1, source_target_pairs={{0,1},{1,0},{2,3},{3,2},{4,5},{5,4},{6,7},{7,6},{8,9},{9,8},{10,11... | collective-permute-start | bytes 393224 | tf_op jit(solution)/shard_map/ppermute | solution.py:421

commit v5 on v4

--- a/solution.py
+++ b/solution.py
@@ -70,53 +70,53 @@
     return both[:rows] + (both[rows:] + one(a[0], b[1]))
 
 
-def write_strips(place, product, outs, wrapped=0):
+def write_strips(place, product, outs, own_product=None):
     core, first, second = place[0], place[2], place[3]
-    kept = KEPT if wrapped else 0
-    if wrapped:
+    start = 0
+    if own_product is not None:
         block = lax.broadcasted_iota(jnp.int32, (32, KEPT), 1) // CLUSTER
         weight = jnp.where(block == 1, 1.0, 0.5)
+        wrapped = PANEL + 2 * CLUSTER
+        start = KEPT + own_product.shape[1] - wrapped
     for k in range(4):
         for m in range(4):
             f, g = (first + k) % 4, (second + m) % 4
             strip = jnp.where(core == 0, 4 * f + g, 4 * g + f)
             rows = pl.ds(pl.multiple_of(strip * 32, 32), 32)
-            if wrapped:
-                start = jnp.where(core == 0, f, g) * CLUSTER
-                columns = pl.ds(pl.multiple_of(start, CLUSTER), KEPT)
-                outs[k][m, :, :KEPT] = product[rows, columns] * weight
-            outs[k][m, :, kept:] = product[rows, wrapped:]
+            if own_product is not None:
+                at = jnp.where(core == 0, f, g) * CLUSTER
+                columns = pl.ds(pl.multiple_of(at, CLUSTER), KEPT)
+                outs[k][m, :, :KEPT] = own_product[rows, columns] * weight
+                outs[k][m, :, KEPT:start] = own_product[rows, wrapped:]
+            outs[k][m, :, start:] = product[rows, :]
 
 
 def near_kernel(place, own, pair, product):
     panel = own.shape[1]
     thin = panel // 2
+    wrapped = panel + 2 * CLUSTER
     a = halves(own[...])
-    product[:, :panel] = contract(a, a)
+    square = contract(a, a)
+    product[:, :panel] = square
+    product[:, panel:wrapped] = square[:, : 2 * CLUSTER]
 
     @pl.when(place[0] == 0)
     def _():
-        product[:, panel:] = contract(a, halves(pair[:, :thin]))
+        product[:, wrapped:] = contract(a, halves(pair[:, :thin]))
 
     @pl.when(place[0] != 0)
     def _():
         b = [part[:, thin:] for part in a]
-        product[:, panel:] = contract(halves(pair[...]), b)
-
-
-def early_kernel(place, own, pair, value, other, out0, out1, out2, out3, product):
+        product[:, wrapped:] = contract(halves(pair[...]), b)
+
+
+def early_kernel(place, own, pair, value, own_product, out0, out1, out2, out3, product):
     half, width = value.shape
-    panel = own.shape[1]
     rows = pl.ds(pl.multiple_of(place[1] * half, half), half)
     b = halves(value[...])
-    again = panel + 2 * CLUSTER
-    product[:, :panel] = other[:, :panel]
-    product[:, panel:again] = other[:, : 2 * CLUSTER]
-    start = again + other.shape[1] - panel
-    product[:, again:start] = other[:, panel:]
-    product[:, start : start + width] = contract(halves(own[rows, :]), b)
-    product[:, start + width :] = contract(halves(pair[rows, :]), b)
-    write_strips(place, product, (out0, out1, out2, out3), again)
+    product[:, :width] = contract(b, halves(own[rows, :])).T
+    product[:, width:] = contract(b, halves(pair[rows, :])).T
+    write_strips(place, product, (out0, out1, out2, out3), own_product)
 
 
 def prepare_kernel(place, own, pair, first, second):
@@ -351,14 +351,14 @@
     across = [lax.ppermute(value, "lm", OTHER_CHIP) for value in across]
 
     product = kernel_call(
-        near_kernel, [place], shape(panel, panel + thin), [], COSTS[0], own, pair
+        near_kernel, [place], shape(panel, panel + 2 * CLUSTER + thin), [], COSTS[0], own, pair
     )
     widths = [KEPT + thin + 2 * PIECES[0][1], 2 * PIECES[1][1]]
     early = kernel_call(
         early_kernel,
         [place],
         [shape(4, panel // 16, widths[0])] * 4,
-        [(panel, panel + 2 * CLUSTER + thin + 2 * PIECES[0][1])],
+        [(panel, 2 * PIECES[0][1])],
         COSTS[1],
         own,
         pair,

time: 127 us -> 127 us (level)
  no operation moved by 1% of the time
where the time goes in v5:
time: 127 us; the launch traced here: 126 us
  waiting for transfers between devices  49.5 us (39%)
  starting transfers between devices  32.9 us (26%)
  Pallas kernels  25.4 us (20%)
  blocking collectives  12 us (9%)
  local copies, waits for them, and re-layouts  4.89 us (4%)
    pallas_call x10, Pallas kernels, kernel_call(): pl.pallas_call(body, out_shape=out_shape, in_specs=[smem] * len(scalars)...  25.4 us
    ppermute x9, waiting for transfers between devices, sum_along(): lax.ppermute(values[step], ('pts', 'lm'), plane_step(step, swapped))  15.1 us
    ppermute x9, starting transfers between devices, sum_along(): lax.ppermute(values[step], ('pts', 'lm'), plane_step(step, swapped))  12.4 us
    all_to_all x1, blocking collectives, turned(): lax.all_to_all(packed, ('pts', 'lm'), 0, 0, axis_index_groups=groups, til...  12 us
    ppermute x2, waiting for transfers between devices, hop(): got = lax.ppermute(value, 'lm', OTHER_CHIP)  9.39 us
    all_to_all x1, waiting for transfers between devices, turned(): lax.all_to_all(packed, ('pts', 'lm'), 0, 0, axis_index_groups=groups, til...  8.77 us
    ppermute x1, waiting for transfers between devices, per_device(): away = lax.ppermute(value, 'lm', OTHER_CHIP)  5.14 us
    all_to_all x1, starting transfers between devices, turned(): lax.all_to_all(packed, ('pts', 'lm'), 0, 0, axis_index_groups=groups, til...  4.78 us
  transfers between devices with their start and end apart: 26, of which 19 were waited for; matrix products, arithmetic and copies ran while one was open for 3% of the time, Pallas kernels for 16%

profile of v5, /device:TPU:1, one launch (start us, length us, event | category | flops | bytes accessed | tf_op | source)
XLA Modules:
  0.0 126.2 jit_solution(13719451581314269115)
XLA Ops:
  0.0 1.4 %collective-permute-start = (f32[1024,512]{1,0:T(8,128)}, f32[1024,512]{1,0:T(8,128)}, u32[]{:S(2)}, u32[]{:S(2)}) collective-permute-start(f32[1024,512]{1,0:T(8,128)} %refs_1_.7), channel_id=1, source_target_pairs={{0,1},{1,0},{2,3},{3,2},{4,5},{5,4},{6,7},{7,6},{8,9},{9,8},{10,11... | collective-permute-start | bytes 6291464 | tf_op jit(solution)/shard_map/ppermute | solution.py:347
  1.4 1.0 constant_dynamic-slice_fusion.3
  2.4 1.8 %collective-permute-start.1 = (f32[512,128]{1,0:T(8,128)S(1)}, f32[512,128]{1,0:T(8,128)S(1)}, u32[]{:S(2)}, u32[]{:S(2)}) collective-permute-start(f32[512,128]{1,0:T(8,128)S(1)} %constant_dynamic-slice_fusion.3), channel_id=1, source_target_pairs={{0,2},{1,3},{2,0},{3,1},{4,6},{5,7},{6,4},{7,5},{8,10},{9,11},{10,... | collective-permute-start | bytes 786440 | tf_op jit(solution)/shard_map/ppermute | solution.py:351
  4.2 3.1 %slice.11 = f32[1024,512]{1,0:T(8,128)} slice(f32[2048,512]{1,0:T(8,128)} %refs_3_.1), slice={[0:1024], [0:512]} | slice | bytes 4194304 | tf_op jit(solution)/shard_map/slice | solution.py:403
  7.9 4.5 %shard_map.46.refs_4_ = f32[512,1024]{1,0:T(8,128)S(1)} custom-call(s32[8]{0:T(128)S(1)} %stack.53.refs_0_, f32[1024,512]{1,0:T(8,128)S(1)} %copy-done.1, f32[1024,512]{1,0:T(8,128)} %collective-permute-done.refs_2_), custom_call_target="tpu_custom_call" | custom-call | flops 40000000000 | bytes 120000000 | tf_op jit(solution)/shard_map/pallas_call | solution.py:304
  12.3 2.4 %shard_map.47 = (f32[4,32,896]{2,1,0:T(8,128)S(1)}, f32[4,32,896]{2,1,0:T(8,128)S(1)}, f32[4,32,896]{2,1,0:T(8,128)S(1)}, f32[4,32,896]{2,1,0:T(8,128)S(1)}) custom-call(s32[8]{0:T(128)S(1)} %stack.53.refs_0_, f32[1024,512]{1,0:T(8,128)S(1)} %copy-done.1, f32[1024,512]{1,0:T(8,128)} %collective-permute-done.refs_2_, ...), custom_call_target="tpu_custom_call" | custom-call | flops 6000000000 | bytes 18000000 | tf_op jit(solution)/shard_map/pallas_call | solution.py:304
  14.8 1.4 %collective-permute-start.2 = (f32[4,32,896]{2,1,0:T(8,128)S(1)}, f32[4,32,896]{2,1,0:T(8,128)S(1)}, u32[]{:S(2)}, u32[]{:S(2)}) collective-permute-start(f32[4,32,896]{2,1,0:T(8,128)S(1)} %get-tuple-element.36), channel_id=1, source_target_pairs={{0,16},{1,5},{2,18},{3,7},{4,20},{5,9},{6,22},{7,11},{8,24},{9,13}... | collective-permute-start | bytes 1376264 | tf_op jit(solution)/shard_map/ppermute | solution.py:327
  16.2 1.5 %collective-permute-start.3 = (f32[4,32,896]{2,1,0:T(8,128)S(1)}, f32[4,32,896]{2,1,0:T(8,128)S(1)}, u32[]{:S(2)}, u32[]{:S(2)}) collective-permute-start(f32[4,32,896]{2,1,0:T(8,128)S(1)} %get-tuple-element.37), channel_id=1, source_target_pairs={{0,48},{1,13},{2,50},{3,15},{4,52},{5,1},{6,54},{7,3},{8,56},{9,5}... | collective-permute-start | bytes 1376264 | tf_op jit(solution)/shard_map/ppermute | solution.py:327
  17.7 1.6 %collective-permute-start.4 = (f32[4,32,896]{2,1,0:T(8,128)S(1)}, f32[4,32,896]{2,1,0:T(8,128)S(1)}, u32[]{:S(2)}, u32[]{:S(2)}) collective-permute-start(f32[4,32,896]{2,1,0:T(8,128)S(1)} %get-tuple-element.38), channel_id=1, source_target_pairs={{0,32},{1,9},{2,34},{3,11},{4,36},{5,13},{6,38},{7,15},{8,40},{9,1... | collective-permute-start | bytes 1376264 | tf_op jit(solution)/shard_map/ppermute | solution.py:327
  19.2 2.3 %shard_map.48 = (bf16[1024,512]{1,0:T(8,128)(2,1)S(1)}, bf16[1024,512]{1,0:T(8,128)(2,1)S(1)}) custom-call(s32[8]{0:T(128)S(1)} %stack.53.refs_0_, f32[1024,512]{1,0:T(8,128)S(1)} %copy-done.1, f32[1024,512]{1,0:T(8,128)} %collective-permute-done.refs_2_, f32[4,32,896]{2,1,0:T(8,128)S(1)} %get-tuple-element.35.refs_3_.refs_5_), custom_call_target="tpu_custom_call" | custom-call | flops 4000000000 | bytes 12000000 | tf_op jit(solution)/shard_map/pallas_call | solution.py:304
  21.5 2.2 %collective-permute-done.2 = f32[4,32,896]{2,1,0:T(8,128)S(1)} collective-permute-done((f32[4,32,896]{2,1,0:T(8,128)S(1)}, f32[4,32,896]{2,1,0:T(8,128)S(1)}, u32[]{:S(2)}, u32[]{:S(2)}) %collective-permute-start.2) | collective-permute-done | bytes 458784 | tf_op jit(solution)/shard_map/ppermute | solution.py:327
  23.8 4.3 %collective-permute-done.3 = f32[4,32,896]{2,1,0:T(8,128)S(1)} collective-permute-done((f32[4,32,896]{2,1,0:T(8,128)S(1)}, f32[4,32,896]{2,1,0:T(8,128)S(1)}, u32[]{:S(2)}, u32[]{:S(2)}) %collective-permute-start.3) | collective-permute-done | bytes 458784 | tf_op jit(solution)/shard_map/ppermute | solution.py:327
  28.0 1.8 %collective-permute-done.4 = f32[4,32,896]{2,1,0:T(8,128)S(1)} collective-permute-done((f32[4,32,896]{2,1,0:T(8,128)S(1)}, f32[4,32,896]{2,1,0:T(8,128)S(1)}, u32[]{:S(2)}, u32[]{:S(2)}) %collective-permute-start.4) | collective-permute-done | bytes 458784 | tf_op jit(solution)/shard_map/ppermute | solution.py:327
  29.8 1.2 collective-permute-start.6
  31.3 1.7 %collective-permute-done.6.refs_3_ = f32[512,384]{1,0:T(8,128)S(1)} collective-permute-done((f32[512,384]{1,0:T(8,128)S(1)}, f32[512,384]{1,0:T(8,128)S(1)}, u32[]{:S(2)}, u32[]{:S(2)}) %collective-permute-start.6) | collective-permute-done | bytes 786464 | tf_op jit(solution)/shard_map/ppermute | solution.py:381
  33.0 2.4 %shard_map.49 = (f32[4,32,768]{2,1,0:T(8,128)S(1)}, f32[4,32,768]{2,1,0:T(8,128)S(1)}, f32[4,32,768]{2,1,0:T(8,128)S(1)}, f32[4,32,768]{2,1,0:T(8,128)S(1)}) custom-call(s32[8]{0:T(128)S(1)} %stack.53.refs_0_, bf16[1024,512]{1,0:T(8,128)(2,1)S(1)} %get-tuple-element.42.refs_1_, bf16[1024,512]{1,0:T(8,128)(2,1)S(1)} %get-tuple-element.43.refs_2_, ...), custom_call_target="tpu_custom_call" | custom-call | flops 4000000000 | bytes 12000000 | tf_op jit(solution)/shard_map/pallas_call | solution.py:304
  35.4 3.0 %collective-permute-start.9 = (f32[4,32,768]{2,1,0:T(8,128)S(1)}, f32[4,32,768]{2,1,0:T(8,128)S(1)}, u32[]{:S(2)}, u32[]{:S(2)}) collective-permute-start(f32[4,32,768]{2,1,0:T(8,128)S(1)} %get-tuple-element.48), channel_id=1, source_target_pairs={{0,32},{1,9},{2,34},{3,11},{4,36},{5,13},{6,38},{7,15},{8,40},{9,1... | collective-permute-start | bytes 1179656 | tf_op jit(solution)/shard_map/ppermute | solution.py:327
  38.4 0.8 collective-permute-start.8
  39.2 0.7 collective-permute-start.7
  39.9 8.0 %shard_map.50 = (bf16[1024,512]{1,0:T(8,128)(2,1)S(1)}, bf16[1024,512]{1,0:T(8,128)(2,1)S(1)}, bf16[1024,512]{1,0:T(8,128)(2,1)S(1)}, bf16[1024,512]{1,0:T(8,128)(2,1)S(1)}) custom-call(s32[8]{0:T(128)S(1)} %stack.53.refs_0_, f32[512,512]{1,0:T(8,128)S(1)} %bitcast.34, f32[512,512]{1,0:T(8,128)S(1)} %collective-permute-done.10.refs_2_, ...), custom_call_target="tpu_custom_call" | custom-call | flops 4000000000 | bytes 12000000 | tf_op jit(solution)/shard_map/pallas_call | solution.py:304
  49.2 0.8 pad_maximum_fusion.3
  50.5 3.0 %collective-permute-start.13 = (f32[32,1664]{1,0:T(8,128)}, f32[32,1664]{1,0:T(8,128)S(1)}, u32[]{:S(2)}, u32[]{:S(2)}) collective-permute-start(f32[32,1664]{1,0:T(8,128)} %get-tuple-element.52), channel_id=1, source_target_pairs={{0,12},{1,49},{2,14},{3,51},{4,0},{5,53},{6,2},{7,55},{8,4},{9,57}... | collective-permute-start | bytes 638984 | tf_op jit(solution)/shard_map/ppermute | solution.py:327
  53.5 3.2 %collective-permute-done.14 = f32[32,1664]{1,0:T(8,128)S(1)} collective-permute-done((f32[32,1664]{1,0:T(8,128)}, f32[32,1664]{1,0:T(8,128)S(1)}, u32[]{:S(2)}, u32[]{:S(2)}) %collective-permute-start.14) | collective-permute-done | bytes 213024 | tf_op jit(solution)/shard_map/ppermute | solution.py:327
  56.7 1.8 %collective-permute-done.13 = f32[32,1664]{1,0:T(8,128)S(1)} collective-permute-done((f32[32,1664]{1,0:T(8,128)}, f32[32,1664]{1,0:T(8,128)S(1)}, u32[]{:S(2)}, u32[]{:S(2)}) %collective-permute-start.13) | collective-permute-done | bytes 213024 | tf_op jit(solution)/shard_map/ppermute | solution.py:327
  58.5 1.2 collective-permute-done.12
  59.8 3.5 %collective-permute-start.15 = (f32[16,1664]{1,0:T(8,128)S(1)}, f32[16,1664]{1,0:T(8,128)S(1)}, u32[]{:S(2)}, u32[]{:S(2)}) collective-permute-start(f32[16,1664]{1,0:T(8,128)S(1)} %get-tuple-element.55), channel_id=1, source_target_pairs={{0,64},{1,65},{2,66},{3,67},{4,68},{5,69},{6,70},{7,71},{8,72},{9,... | collective-permute-start | bytes 319496 | tf_op jit(solution)/shard_map/ppermute | solution.py:413
  63.9 1.5 %collective-permute-done.15 = f32[16,1664]{1,0:T(8,128)S(1)} collective-permute-done((f32[16,1664]{1,0:T(8,128)S(1)}, f32[16,1664]{1,0:T(8,128)S(1)}, u32[]{:S(2)}, u32[]{:S(2)}) %collective-permute-start.15) | collective-permute-done | bytes 106528 | tf_op jit(solution)/shard_map/ppermute | solution.py:413
  65.4 2.1 %collective-permute-done.16 = f32[16,1664]{1,0:T(8,128)S(1)} collective-permute-done((f32[16,1664]{1,0:T(8,128)S(1)}, f32[16,1664]{1,0:T(8,128)S(1)}, u32[]{:S(2)}, u32[]{:S(2)}) %collective-permute-start.16) | collective-permute-done | bytes 106528 | tf_op jit(solution)/shard_map/ppermute | solution.py:411
  67.4 1.7 %collective-permute-done.17 = f32[16,1664]{1,0:T(8,128)S(1)} collective-permute-done((f32[16,1664]{1,0:T(8,128)S(1)}, f32[16,1664]{1,0:T(8,128)S(1)}, u32[]{:S(2)}, u32[]{:S(2)}) %collective-permute-start.17) | collective-permute-done | bytes 106528 | tf_op jit(solution)/shard_map/ppermute | solution.py:412
  69.2 3.3 %collective-permute-start.18 = (f32[2,16,1664]{2,1,0:T(8,128)S(1)}, f32[2,16,1664]{2,1,0:T(8,128)S(1)}, u32[]{:S(2)}, u32[]{:S(2)}) collective-permute-start(f32[2,16,1664]{2,1,0:T(8,128)S(1)} %pad_maximum_fusion.5), channel_id=1, source_target_pairs={{0,1},{1,0},{2,3},{3,2},{4,5},{5,4},{6,7},{7,6},{8,9},{9,8},{10,11... | collective-permute-start | bytes 638984 | tf_op jit(solution)/shard_map/ppermute | solution.py:417
  72.4 1.1 collective-permute-done.18.refs_4_
  73.5 1.0 shard_map.51.refs_1_
  74.7 4.7 %collective-permute-done.19.refs_2_ = f32[64,512]{1,0:T(8,128)S(1)} collective-permute-done((f32[64,512]{1,0:T(8,128)S(1)}, f32[64,512]{1,0:T(8,128)S(1)}, u32[]{:S(2)}, u32[]{:S(2)}) %collective-permute-start.19) | collective-permute-done | bytes 131104 | tf_op jit(solution)/shard_map/ppermute | solution.py:420
  79.4 1.2 collective-permute-start.20
  80.6 1.0 collective-permute-done.20.refs_3_
  81.6 1.4 %shard_map.52 = (f32[64,512]{1,0:T(8,128)}, f32[16,32,128]{2,1,0:T(8,128)}) custom-call(s32[8]{0:T(128)S(1)} %stack.53.refs_0_, f32[64,512]{1,0:T(8,128)S(1)} %shard_map.51.refs_1_, f32[64,512]{1,0:T(8,128)S(1)} %collective-permute-done.19.refs_2_, f32[64,512]{1,0:T(8,128)S(1)} %collective-permute-done.20.refs_3_, bf16[1024,512]{1,0:T(8,128)(2,1)S(1)} %copy-done.5, ...), custom_call_target="tpu_custom_call" | custom-call | flops 2000000000 | bytes 6000000 | tf_op jit(solution)/shard_map/pallas_call | solution.py:304
  82.9 4.8 %all-to-all-start = ((f32[16,32,128]{2,1,0:T(8,128)}), f32[16,32,128]{2,1,0:T(8,128)S(1)}, u32[]{:S(2)}, u32[]{:S(2)}) async-start(f32[16,32,128]{2,1,0:T(8,128)} %get-tuple-element.60), calls=%async_computation | async-start | bytes 524288 | tf_op jit(solution)/shard_map/all_to_all | solution.py:425
  87.7 8.8 %all-to-all-done = f32[16,32,128]{2,1,0:T(8,128)S(1)} async-done(((f32[16,32,128]{2,1,0:T(8,128)}), f32[16,32,128]{2,1,0:T(8,128)S(1)}, u32[]{:S(2)}, u32[]{:S(2)}) %all-to-all-start) | async-done | bytes 262176 | tf_op jit(solution)/shard_map/all_to_all | solution.py:425
  96.6 5.1 %collective-permute-done.21.refs_3_ = f32[8,32,128]{2,1,0:T(8,128)S(1)} collective-permute-done((f32[8,32,128]{2,1,0:T(8,128)S(1)}, f32[8,32,128]{2,1,0:T(8,128)S(1)}, u32[]{:S(2)}, u32[]{:S(2)}) %collective-permute-start.21) | collective-permute-done | bytes 131104 | tf_op jit(solution)/shard_map/ppermute | solution.py:442
  101.8 0.8 collective-permute-start.22
  102.6 1.2 collective-permute-done.22.refs_4_
  103.8 1.4 %shard_map.53.refs_1_ = f32[64,512]{1,0:T(8,128)S(1)} custom-call(s32[8]{0:T(128)S(1)} %stack.53.refs_0_, s32[16]{0:T(128)S(1)} %copy-done.3, f32[8,32,128]{2,1,0:T(8,128)S(1)} %constant_dynamic-slice_fusion.refs_2_, f32[8,32,128]{2,1,0:T(8,128)S(1)} %collective-permute-done.21.refs_3_, f32[2,8,32,128]{3,2,1,0:T(8,128)S(1)} %collective-permute-done.22.refs_4_, ...), custom_call_target="tpu_custom_call" | custom-call | flops 2000000000 | bytes 6000000 | tf_op jit(solution)/shard_map/pallas_call | solution.py:304
  105.3 4.7 %collective-permute-done.23.refs_2_ = f32[64,512]{1,0:T(8,128)S(1)} collective-permute-done((f32[64,512]{1,0:T(8,128)S(1)}, f32[64,512]{1,0:T(8,128)S(1)}, u32[]{:S(2)}, u32[]{:S(2)}) %collective-permute-start.23) | collective-permute-done | bytes 131104 | tf_op jit(solution)/shard_map/ppermute | solution.py:420
  110.0 1.2 collective-permute-start.24
  111.2 1.0 collective-permute-done.24.refs_3_
  112.2 0.7 shard_map.54
  112.8 12.0 %all_to_all.10.refs_3_ = f32[16,32,128]{2,1,0:T(8,128)S(1)} all-to-all(f32[16,32,128]{2,1,0:T(8,128)S(1)} %get-tuple-element.62), channel_id=1, replica_groups={{1,5,9,13,17,21,25,29,32,36,40,44,48,52,56,60},{2,6,10,14,18,22,26,30,6..., dimensions={0} | all-to-all | bytes 524288 | tf_op jit(solution)/shard_map/all_to_all | solution.py:425
  124.8 1.4 %shard_map.55 = f32[64,512]{1,0:T(8,128)} custom-call(s32[8]{0:T(128)S(1)} %stack.53.refs_0_, f32[1]{0:T(128)} %constant.82.clone.1.refs_1_, f32[64,512]{1,0:T(8,128)S(1)} %get-tuple-element.61.refs_2_, f32[16,32,128]{2,1,0:T(8,128)S(1)} %all_to_all.10.refs_3_), custom_call_target="tpu_custom_call" | custom-call | tf_op jit(solution)/shard_map/pallas_call | solution.py:304
  (53 shorter events, 3.7 us)
Async XLA Ops:
  0.0 7.8 %collective-permute-start = (f32[1024,512]{1,0:T(8,128)}, f32[1024,512]{1,0:T(8,128)}, u32[]{:S(2)}, u32[]{:S(2)}) collective-permute-start(f32[1024,512]{1,0:T(8,128)} %refs_1_.7), channel_id=1, source_target_pairs={{0,1},{1,0},{2,3},{3,2},{4,5},{5,4},{6,7},{7,6},{8,9},{9,8},{10,11... | collective-permute-start | bytes 6291464 | tf_op jit(solution)/shard_map/ppermute | solution.py:347
  2.4 5.2 %copy-start.1 = (f32[1024,512]{1,0:T(8,128)S(1)}, f32[1024,512]{1,0:T(8,128)}, u32[]{:S(2)}) copy-start(f32[1024,512]{1,0:T(8,128)} %refs_1_.7) | copy-start | bytes 6291460
  2.4 9.9 %collective-permute-start.1 = (f32[512,128]{1,0:T(8,128)S(1)}, f32[512,128]{1,0:T(8,128)S(1)}, u32[]{:S(2)}, u32[]{:S(2)}) collective-permute-start(f32[512,128]{1,0:T(8,128)S(1)} %constant_dynamic-slice_fusion.3), channel_id=1, source_target_pairs={{0,2},{1,3},{2,0},{3,1},{4,6},{5,7},{6,4},{7,5},{8,10},{9,11},{10,... | collective-permute-start | bytes 786440 | tf_op jit(solution)/shard_map/ppermute | solution.py:351
  7.3 32.5 %collective-permute-start.11 = (f32[1024,512]{1,0:T(8,128)}, f32[1024,512]{1,0:T(8,128)}, u32[]{:S(2)}, u32[]{:S(2)}) collective-permute-start(f32[1024,512]{1,0:T(8,128)} %slice.11), channel_id=1, source_target_pairs={{0,1},{1,0},{2,3},{3,2},{4,5},{5,4},{6,7},{7,6},{8,9},{9,8},{10,11... | collective-permute-start | bytes 6291464 | tf_op jit(solution)/shard_map/ppermute | solution.py:403
  7.8 22.1 %collective-permute-start.5 = (f32[512,384]{1,0:T(8,128)S(1)}, f32[512,384]{1,0:T(8,128)S(1)}, u32[]{:S(2)}, u32[]{:S(2)}) collective-permute-start(f32[512,384]{1,0:T(8,128)S(1)} %dynamic-slice), channel_id=1, source_target_pairs={{0,2},{1,3},{2,0},{3,1},{4,6},{5,7},{6,4},{7,5},{8,10},{9,11},{10,... | collective-permute-start | bytes 2359304 | tf_op jit(solution)/shard_map/ppermute | solution.py:351
  14.8 9.0 %collective-permute-start.2 = (f32[4,32,896]{2,1,0:T(8,128)S(1)}, f32[4,32,896]{2,1,0:T(8,128)S(1)}, u32[]{:S(2)}, u32[]{:S(2)}) collective-permute-start(f32[4,32,896]{2,1,0:T(8,128)S(1)} %get-tuple-element.36), channel_id=1, source_target_pairs={{0,16},{1,5},{2,18},{3,7},{4,20},{5,9},{6,22},{7,11},{8,24},{9,13}... | collective-permute-start | bytes 1376264 | tf_op jit(solution)/shard_map/ppermute | solution.py:327
  16.2 11.9 %collective-permute-start.3 = (f32[4,32,896]{2,1,0:T(8,128)S(1)}, f32[4,32,896]{2,1,0:T(8,128)S(1)}, u32[]{:S(2)}, u32[]{:S(2)}) collective-permute-start(f32[4,32,896]{2,1,0:T(8,128)S(1)} %get-tuple-element.37), channel_id=1, source_target_pairs={{0,48},{1,13},{2,50},{3,15},{4,52},{5,1},{6,54},{7,3},{8,56},{9,5}... | collective-permute-start | bytes 1376264 | tf_op jit(solution)/shard_map/ppermute | solution.py:327
  17.7 12.2 %collective-permute-start.4 = (f32[4,32,896]{2,1,0:T(8,128)S(1)}, f32[4,32,896]{2,1,0:T(8,128)S(1)}, u32[]{:S(2)}, u32[]{:S(2)}) collective-permute-start(f32[4,32,896]{2,1,0:T(8,128)S(1)} %get-tuple-element.38), channel_id=1, source_target_pairs={{0,32},{1,9},{2,34},{3,11},{4,36},{5,13},{6,38},{7,15},{8,40},{9,1... | collective-permute-start | bytes 1376264 | tf_op jit(solution)/shard_map/ppermute | solution.py:327
  19.2 11.8 %copy-start.2 = (f32[1,512,512]{2,1,0:T(8,128)S(1)}, f32[1,512,512]{2,1,0:T(8,128)}, u32[]{:S(2)}) copy-start(f32[1,512,512]{2,1,0:T(8,128)} %param.6) | copy-start | bytes 3145732
  29.8 3.1 %collective-permute-start.6 = (f32[512,384]{1,0:T(8,128)S(1)}, f32[512,384]{1,0:T(8,128)S(1)}, u32[]{:S(2)}, u32[]{:S(2)}) collective-permute-start(f32[512,384]{1,0:T(8,128)S(1)} %collective-permute-done.5), channel_id=1, source_target_pairs={{0,1},{1,0},{2,3},{3,2},{4,5},{5,4},{6,7},{7,6},{8,9},{9,8},{10,11... | collective-permute-start | bytes 2359304 | tf_op jit(solution)/shard_map/ppermute | solution.py:381
  31.1 8.8 %collective-permute-start.10 = (f32[512,512]{1,0:T(8,128)S(1)}, f32[512,512]{1,0:T(8,128)S(1)}, u32[]{:S(2)}, u32[]{:S(2)}) collective-permute-start(f32[512,512]{1,0:T(8,128)S(1)} %bitcast.33), channel_id=1, source_target_pairs={{0,1},{1,0},{2,3},{3,2},{4,5},{5,4},{6,7},{7,6},{8,9},{9,8},{10,11... | collective-permute-start | bytes 3145736 | tf_op jit(solution)/shard_map/ppermute | solution.py:402
  31.3 8.6 %copy-start = (f32[2048,512]{1,0:T(8,128)S(1)}, f32[2048,512]{1,0:T(8,128)}, u32[]{:S(2)}) copy-start(f32[2048,512]{1,0:T(8,128)} %refs_3_.1) | copy-start | bytes 12582916
  35.4 12.5 %collective-permute-start.9 = (f32[4,32,768]{2,1,0:T(8,128)S(1)}, f32[4,32,768]{2,1,0:T(8,128)S(1)}, u32[]{:S(2)}, u32[]{:S(2)}) collective-permute-start(f32[4,32,768]{2,1,0:T(8,128)S(1)} %get-tuple-element.48), channel_id=1, source_target_pairs={{0,32},{1,9},{2,34},{3,11},{4,36},{5,13},{6,38},{7,15},{8,40},{9,1... | collective-permute-start | bytes 1179656 | tf_op jit(solution)/shard_map/ppermute | solution.py:327
  38.4 10.1 %collective-permute-start.8 = (f32[4,32,768]{2,1,0:T(8,128)S(1)}, f32[4,32,768]{2,1,0:T(8,128)S(1)}, u32[]{:S(2)}, u32[]{:S(2)}) collective-permute-start(f32[4,32,768]{2,1,0:T(8,128)S(1)} %get-tuple-element.47), channel_id=1, source_target_pairs={{0,48},{1,13},{2,50},{3,15},{4,52},{5,1},{6,54},{7,3},{8,56},{9,5}... | collective-permute-start | bytes 1179656 | tf_op jit(solution)/shard_map/ppermute | solution.py:327
  39.2 9.3 %collective-permute-start.7 = (f32[4,32,768]{2,1,0:T(8,128)S(1)}, f32[4,32,768]{2,1,0:T(8,128)S(1)}, u32[]{:S(2)}, u32[]{:S(2)}) collective-permute-start(f32[4,32,768]{2,1,0:T(8,128)S(1)} %get-tuple-element.46), channel_id=1, source_target_pairs={{0,16},{1,5},{2,18},{3,7},{4,20},{5,9},{6,22},{7,11},{8,24},{9,13}... | collective-permute-start | bytes 1179656 | tf_op jit(solution)/shard_map/ppermute | solution.py:327
  47.8 1.0 copy-start.4
  47.8 1.3 %copy-start.7 = (bf16[1024,512]{1,0:T(8,128)(2,1)}, bf16[1024,512]{1,0:T(8,128)(2,1)S(1)}, u32[]{:S(2)}) copy-start(bf16[1024,512]{1,0:T(8,128)(2,1)S(1)} %get-tuple-element.59.refs_5_) | copy-start | bytes 3145732
  48.6 24.9 %copy-start.3 = (s32[16]{0:T(128)S(1)}, s32[16]{0:T(128)}, u32[]{:S(2)}) copy-start(s32[16]{0:T(128)} %refs_1_.9) | copy-start | bytes 196
  50.0 6.7 %collective-permute-start.14 = (f32[32,1664]{1,0:T(8,128)}, f32[32,1664]{1,0:T(8,128)S(1)}, u32[]{:S(2)}, u32[]{:S(2)}) collective-permute-start(f32[32,1664]{1,0:T(8,128)} %get-tuple-element.53), channel_id=1, source_target_pairs={{0,8},{1,33},{2,10},{3,35},{4,12},{5,37},{6,14},{7,39},{8,0},{9,41... | collective-permute-start | bytes 638984 | tf_op jit(solution)/shard_map/ppermute | solution.py:327
  50.5 8.0 %collective-permute-start.13 = (f32[32,1664]{1,0:T(8,128)}, f32[32,1664]{1,0:T(8,128)S(1)}, u32[]{:S(2)}, u32[]{:S(2)}) collective-permute-start(f32[32,1664]{1,0:T(8,128)} %get-tuple-element.52), channel_id=1, source_target_pairs={{0,12},{1,49},{2,14},{3,51},{4,0},{5,53},{6,2},{7,55},{8,4},{9,57}... | collective-permute-start | bytes 638984 | tf_op jit(solution)/shard_map/ppermute | solution.py:327
  53.5 6.2 %collective-permute-start.12 = (f32[32,1664]{1,0:T(8,128)S(1)}, f32[32,1664]{1,0:T(8,128)S(1)}, u32[]{:S(2)}, u32[]{:S(2)}) collective-permute-start(f32[32,1664]{1,0:T(8,128)S(1)} %get-tuple-element.51), channel_id=1, source_target_pairs={{0,4},{1,17},{2,6},{3,19},{4,8},{5,21},{6,10},{7,23},{8,12},{9,25}... | collective-permute-start | bytes 638984 | tf_op jit(solution)/shard_map/ppermute | solution.py:327
  59.8 5.6 %collective-permute-start.15 = (f32[16,1664]{1,0:T(8,128)S(1)}, f32[16,1664]{1,0:T(8,128)S(1)}, u32[]{:S(2)}, u32[]{:S(2)}) collective-permute-start(f32[16,1664]{1,0:T(8,128)S(1)} %get-tuple-element.55), channel_id=1, source_target_pairs={{0,64},{1,65},{2,66},{3,67},{4,68},{5,69},{6,70},{7,71},{8,72},{9,... | collective-permute-start | bytes 319496 | tf_op jit(solution)/shard_map/ppermute | solution.py:413
  63.2 4.2 %collective-permute-start.16 = (f32[16,1664]{1,0:T(8,128)S(1)}, f32[16,1664]{1,0:T(8,128)S(1)}, u32[]{:S(2)}, u32[]{:S(2)}) collective-permute-start(f32[16,1664]{1,0:T(8,128)S(1)} %get-tuple-element.54), channel_id=1, source_target_pairs={{0,2},{1,3},{2,0},{3,1},{4,6},{5,7},{6,4},{7,5},{8,10},{9,11},{10,... | collective-permute-start | bytes 319496 | tf_op jit(solution)/shard_map/ppermute | solution.py:411
  63.9 5.2 %collective-permute-start.17 = (f32[16,1664]{1,0:T(8,128)S(1)}, f32[16,1664]{1,0:T(8,128)S(1)}, u32[]{:S(2)}, u32[]{:S(2)}) collective-permute-start(f32[16,1664]{1,0:T(8,128)S(1)} %get-tuple-element.55), channel_id=1, source_target_pairs={{0,66},{1,67},{2,64},{3,65},{4,70},{5,71},{6,68},{7,69},{8,74},{9,... | collective-permute-start | bytes 319496 | tf_op jit(solution)/shard_map/ppermute | solution.py:412
  69.2 4.3 %collective-permute-start.18 = (f32[2,16,1664]{2,1,0:T(8,128)S(1)}, f32[2,16,1664]{2,1,0:T(8,128)S(1)}, u32[]{:S(2)}, u32[]{:S(2)}) collective-permute-start(f32[2,16,1664]{2,1,0:T(8,128)S(1)} %pad_maximum_fusion.5), channel_id=1, source_target_pairs={{0,1},{1,0},{2,3},{3,2},{4,5},{5,4},{6,7},{7,6},{8,9},{9,8},{10,11... | collective-permute-start | bytes 638984 | tf_op jit(solution)/shard_map/ppermute | solution.py:417
  73.5 8.0 %copy-start.5 = (bf16[1024,512]{1,0:T(8,128)(2,1)S(1)}, bf16[1024,512]{1,0:T(8,128)(2,1)}, u32[]{:S(2)}) copy-start(bf16[1024,512]{1,0:T(8,128)(2,1)} %copy-done.4) | copy-start | bytes 3145732
  73.5 8.0 %copy-start.8 = (bf16[1024,512]{1,0:T(8,128)(2,1)S(1)}, bf16[1024,512]{1,0:T(8,128)(2,1)}, u32[]{:S(2)}) copy-start(bf16[1024,512]{1,0:T(8,128)(2,1)} %copy-done.7) | copy-start | bytes 3145732
  74.6 4.8 %collective-permute-start.19 = (f32[64,512]{1,0:T(8,128)S(1)}, f32[64,512]{1,0:T(8,128)S(1)}, u32[]{:S(2)}, u32[]{:S(2)}) collective-permute-start(f32[64,512]{1,0:T(8,128)S(1)} %shard_map.51.refs_1_), channel_id=1, source_target_pairs={{0,2},{1,3},{2,0},{3,1},{4,6},{5,7},{6,4},{7,5},{8,10},{9,11},{10,... | collective-permute-start | bytes 393224 | tf_op jit(solution)/shard_map/ppermute | solution.py:420
  79.4 2.2 %collective-permute-start.20 = (f32[64,512]{1,0:T(8,128)S(1)}, f32[64,512]{1,0:T(8,128)S(1)}, u32[]{:S(2)}, u32[]{:S(2)}) collective-permute-start(f32[64,512]{1,0:T(8,128)S(1)} %collective-permute-done.19.refs_2_), channel_id=1, source_target_pairs={{0,1},{1,0},{2,3},{3,2},{4,5},{5,4},{6,7},{7,6},{8,9},{9,8},{10,11... | collective-permute-start | bytes 393224 | tf_op jit(solution)/shard_map/ppermute | solution.py:421
  82.9 13.6 %all-to-all-start = ((f32[16,32,128]{2,1,0:T(8,128)}), f32[16,32,128]{2,1,0:T(8,128)S(1)}, u32[]{:S(2)}, u32[]{:S(2)}) async-start(f32[16,32,128]{2,1,0:T(8,128)} %get-tuple-element.60), calls=%async_computation | async-start | bytes 524288 | tf_op jit(solution)/shard_map/all_to_all | solution.py:425
  96.5 5.3 %collective-permute-start.21 = (f32[8,32,128]{2,1,0:T(8,128)S(1)}, f32[8,32,128]{2,1,0:T(8,128)S(1)}, u32[]{:S(2)}, u32[]{:S(2)}) collective-permute-start(f32[8,32,128]{2,1,0:T(8,128)S(1)} %constant_dynamic-slice_fusion.refs_2_), channel_id=1, source_target_pairs={{0,2},{1,3},{2,0},{3,1},{4,6},{5,7},{6,4},{7,5},{8,10},{9,11},{10,... | collective-permute-start | bytes 393224 | tf_op jit(solution)/shard_map/ppermute | solution.py:442
  101.8 10.4 %copy-start.6 = (bf16[1024,512]{1,0:T(8,128)(2,1)S(1)}, bf16[1024,512]{1,0:T(8,128)(2,1)}, u32[]{:S(2)}) copy-start(bf16[1024,512]{1,0:T(8,128)(2,1)} %copy-done.4) | copy-start | bytes 3145732
  101.8 10.4 %copy-start.9 = (bf16[1024,512]{1,0:T(8,128)(2,1)S(1)}, bf16[1024,512]{1,0:T(8,128)(2,1)}, u32[]{:S(2)}) copy-start(bf16[1024,512]{1,0:T(8,128)(2,1)} %copy-done.7) | copy-start | bytes 3145732
  101.8 2.0 %collective-permute-start.22 = (f32[2,8,32,128]{3,2,1,0:T(8,128)S(1)}, f32[2,8,32,128]{3,2,1,0:T(8,128)S(1)}, u32[]{:S(2)}, u32[]{:S(2)}) collective-permute-start(f32[2,8,32,128]{3,2,1,0:T(8,128)S(1)} %pad_maximum_fusion), channel_id=1, source_target_pairs={{0,1},{1,0},{2,3},{3,2},{4,5},{5,4},{6,7},{7,6},{8,9},{9,8},{10,11... | collective-permute-start | bytes 786440 | tf_op jit(solution)/shard_map/ppermute | solution.py:417
  105.2 4.8 %collective-permute-start.23 = (f32[64,512]{1,0:T(8,128)S(1)}, f32[64,512]{1,0:T(8,128)S(1)}, u32[]{:S(2)}, u32[]{:S(2)}) collective-permute-start(f32[64,512]{1,0:T(8,128)S(1)} %shard_map.53.refs_1_), channel_id=1, source_target_pairs={{0,2},{1,3},{2,0},{3,1},{4,6},{5,7},{6,4},{7,5},{8,10},{9,11},{10,... | collective-permute-start | bytes 393224 | tf_op jit(solution)/shard_map/ppermute | solution.py:420
  110.0 2.2 %collective-permute-start.24 = (f32[64,512]{1,0:T(8,128)S(1)}, f32[64,512]{1,0:T(8,128)S(1)}, u32[]{:S(2)}, u32[]{:S(2)}) collective-permute-start(f32[64,512]{1,0:T(8,128)S(1)} %collective-permute-done.23.refs_2_), channel_id=1, source_target_pairs={{0,1},{1,0},{2,3},{3,2},{4,5},{5,4},{6,7},{7,6},{8,9},{9,8},{10,11... | collective-permute-start | bytes 393224 | tf_op jit(solution)/shard_map/ppermute | solution.py:421

commit v6 on v5

--- a/solution.py
+++ b/solution.py
@@ -227,17 +227,15 @@
 
 
 def less_far(place, value, got, got_pair, far, far_low, solved):
-    panel = value.shape[1]
     solved[...] = value[...]
 
     @pl.when(place[1] != 0)
     def _():
-        core = place[0]
-        rows = [pl.ds(pl.multiple_of(c * panel, panel), panel) for c in (core, 1 - core)]
-        total = value[...]
-        for source, r in zip((got, got_pair), rows):
-            total -= multiply(halves(source[...]), (far[r, :], far_low[r, :]))
-        solved[...] = total
+        first = place[0] == 0
+        left = jnp.where(first, got[...], got_pair[...])
+        right = jnp.where(first, got_pair[...], got[...])
+        before = halves(jnp.concatenate([left, right], 1))
+        solved[...] = value[...] - multiply(before, (far[...], far_low[...]))
 
 
 def pack(row, solved, out):

time: 127 us -> 127 us (level)
  no operation moved by 1% of the time
where the time goes in v6:
time: 127 us; the launch traced here: 126 us
  waiting for transfers between devices  49.5 us (39%)
  starting transfers between devices  32.9 us (26%)
  Pallas kernels  25.4 us (20%)
  blocking collectives  11.9 us (9%)
  local copies, waits for them, and re-layouts  4.89 us (4%)
    pallas_call x10, Pallas kernels, kernel_call(): pl.pallas_call(body, out_shape=out_shape, in_specs=[smem] * len(scalars)...  25.4 us
    ppermute x9, waiting for transfers between devices, sum_along(): lax.ppermute(values[step], ('pts', 'lm'), plane_step(step, swapped))  15.1 us
    ppermute x9, starting transfers between devices, sum_along(): lax.ppermute(values[step], ('pts', 'lm'), plane_step(step, swapped))  12.4 us
    all_to_all x1, blocking collectives, turned(): lax.all_to_all(packed, ('pts', 'lm'), 0, 0, axis_index_groups=groups, til...  11.9 us
    ppermute x2, waiting for transfers between devices, hop(): got = lax.ppermute(value, 'lm', OTHER_CHIP)  9.39 us
    all_to_all x1, waiting for transfers between devices, turned(): lax.all_to_all(packed, ('pts', 'lm'), 0, 0, axis_index_groups=groups, til...  8.77 us
    ppermute x1, waiting for transfers between devices, per_device(): away = lax.ppermute(value, 'lm', OTHER_CHIP)  5.14 us
    all_to_all x1, starting transfers between devices, turned(): lax.all_to_all(packed, ('pts', 'lm'), 0, 0, axis_index_groups=groups, til...  4.78 us
  transfers between devices with their start and end apart: 26, of which 19 were waited for; matrix products, arithmetic and copies ran while one was open for 3% of the time, Pallas kernels for 16%

profile of v6, /device:TPU:1, one launch (start us, length us, event | category | flops | bytes accessed | tf_op | source)
XLA Modules:
  0.0 126.2 jit_solution(11398302976671702227)
XLA Ops:
  0.0 1.4 %collective-permute-start = (f32[1024,512]{1,0:T(8,128)}, f32[1024,512]{1,0:T(8,128)}, u32[]{:S(2)}, u32[]{:S(2)}) collective-permute-start(f32[1024,512]{1,0:T(8,128)} %refs_1_.7), channel_id=1, source_target_pairs={{0,1},{1,0},{2,3},{3,2},{4,5},{5,4},{6,7},{7,6},{8,9},{9,8},{10,11... | collective-permute-start | bytes 6291464 | tf_op jit(solution)/shard_map/ppermute | solution.py:345
  1.4 1.0 constant_dynamic-slice_fusion.3
  2.4 1.8 %collective-permute-start.1 = (f32[512,128]{1,0:T(8,128)S(1)}, f32[512,128]{1,0:T(8,128)S(1)}, u32[]{:S(2)}, u32[]{:S(2)}) collective-permute-start(f32[512,128]{1,0:T(8,128)S(1)} %constant_dynamic-slice_fusion.3), channel_id=1, source_target_pairs={{0,2},{1,3},{2,0},{3,1},{4,6},{5,7},{6,4},{7,5},{8,10},{9,11},{10,... | collective-permute-start | bytes 786440 | tf_op jit(solution)/shard_map/ppermute | solution.py:349
  4.2 3.1 %slice.11 = f32[1024,512]{1,0:T(8,128)} slice(f32[2048,512]{1,0:T(8,128)} %refs_3_.1), slice={[0:1024], [0:512]} | slice | bytes 4194304 | tf_op jit(solution)/shard_map/slice | solution.py:401
  7.9 4.5 %shard_map.46.refs_4_ = f32[512,1024]{1,0:T(8,128)S(1)} custom-call(s32[8]{0:T(128)S(1)} %stack.53.refs_0_, f32[1024,512]{1,0:T(8,128)S(1)} %copy-done.1, f32[1024,512]{1,0:T(8,128)} %collective-permute-done.refs_2_), custom_call_target="tpu_custom_call" | custom-call | flops 40000000000 | bytes 120000000 | tf_op jit(solution)/shard_map/pallas_call | solution.py:302
  12.3 2.4 %shard_map.47 = (f32[4,32,896]{2,1,0:T(8,128)S(1)}, f32[4,32,896]{2,1,0:T(8,128)S(1)}, f32[4,32,896]{2,1,0:T(8,128)S(1)}, f32[4,32,896]{2,1,0:T(8,128)S(1)}) custom-call(s32[8]{0:T(128)S(1)} %stack.53.refs_0_, f32[1024,512]{1,0:T(8,128)S(1)} %copy-done.1, f32[1024,512]{1,0:T(8,128)} %collective-permute-done.refs_2_, ...), custom_call_target="tpu_custom_call" | custom-call | flops 6000000000 | bytes 18000000 | tf_op jit(solution)/shard_map/pallas_call | solution.py:302
  14.8 1.4 %collective-permute-start.2 = (f32[4,32,896]{2,1,0:T(8,128)S(1)}, f32[4,32,896]{2,1,0:T(8,128)S(1)}, u32[]{:S(2)}, u32[]{:S(2)}) collective-permute-start(f32[4,32,896]{2,1,0:T(8,128)S(1)} %get-tuple-element.36), channel_id=1, source_target_pairs={{0,16},{1,5},{2,18},{3,7},{4,20},{5,9},{6,22},{7,11},{8,24},{9,13}... | collective-permute-start | bytes 1376264 | tf_op jit(solution)/shard_map/ppermute | solution.py:325
  16.2 1.5 %collective-permute-start.3 = (f32[4,32,896]{2,1,0:T(8,128)S(1)}, f32[4,32,896]{2,1,0:T(8,128)S(1)}, u32[]{:S(2)}, u32[]{:S(2)}) collective-permute-start(f32[4,32,896]{2,1,0:T(8,128)S(1)} %get-tuple-element.37), channel_id=1, source_target_pairs={{0,48},{1,13},{2,50},{3,15},{4,52},{5,1},{6,54},{7,3},{8,56},{9,5}... | collective-permute-start | bytes 1376264 | tf_op jit(solution)/shard_map/ppermute | solution.py:325
  17.7 1.6 %collective-permute-start.4 = (f32[4,32,896]{2,1,0:T(8,128)S(1)}, f32[4,32,896]{2,1,0:T(8,128)S(1)}, u32[]{:S(2)}, u32[]{:S(2)}) collective-permute-start(f32[4,32,896]{2,1,0:T(8,128)S(1)} %get-tuple-element.38), channel_id=1, source_target_pairs={{0,32},{1,9},{2,34},{3,11},{4,36},{5,13},{6,38},{7,15},{8,40},{9,1... | collective-permute-start | bytes 1376264 | tf_op jit(solution)/shard_map/ppermute | solution.py:325
  19.2 2.3 %shard_map.48 = (bf16[1024,512]{1,0:T(8,128)(2,1)S(1)}, bf16[1024,512]{1,0:T(8,128)(2,1)S(1)}) custom-call(s32[8]{0:T(128)S(1)} %stack.53.refs_0_, f32[1024,512]{1,0:T(8,128)S(1)} %copy-done.1, f32[1024,512]{1,0:T(8,128)} %collective-permute-done.refs_2_, f32[4,32,896]{2,1,0:T(8,128)S(1)} %get-tuple-element.35.refs_3_.refs_5_), custom_call_target="tpu_custom_call" | custom-call | flops 4000000000 | bytes 12000000 | tf_op jit(solution)/shard_map/pallas_call | solution.py:302
  21.5 2.2 %collective-permute-done.2 = f32[4,32,896]{2,1,0:T(8,128)S(1)} collective-permute-done((f32[4,32,896]{2,1,0:T(8,128)S(1)}, f32[4,32,896]{2,1,0:T(8,128)S(1)}, u32[]{:S(2)}, u32[]{:S(2)}) %collective-permute-start.2) | collective-permute-done | bytes 458784 | tf_op jit(solution)/shard_map/ppermute | solution.py:325
  23.8 4.3 %collective-permute-done.3 = f32[4,32,896]{2,1,0:T(8,128)S(1)} collective-permute-done((f32[4,32,896]{2,1,0:T(8,128)S(1)}, f32[4,32,896]{2,1,0:T(8,128)S(1)}, u32[]{:S(2)}, u32[]{:S(2)}) %collective-permute-start.3) | collective-permute-done | bytes 458784 | tf_op jit(solution)/shard_map/ppermute | solution.py:325
  28.0 1.8 %collective-permute-done.4 = f32[4,32,896]{2,1,0:T(8,128)S(1)} collective-permute-done((f32[4,32,896]{2,1,0:T(8,128)S(1)}, f32[4,32,896]{2,1,0:T(8,128)S(1)}, u32[]{:S(2)}, u32[]{:S(2)}) %collective-permute-start.4) | collective-permute-done | bytes 458784 | tf_op jit(solution)/shard_map/ppermute | solution.py:325
  29.8 1.2 collective-permute-start.6
  31.3 1.7 %collective-permute-done.6.refs_3_ = f32[512,384]{1,0:T(8,128)S(1)} collective-permute-done((f32[512,384]{1,0:T(8,128)S(1)}, f32[512,384]{1,0:T(8,128)S(1)}, u32[]{:S(2)}, u32[]{:S(2)}) %collective-permute-start.6) | collective-permute-done | bytes 786464 | tf_op jit(solution)/shard_map/ppermute | solution.py:379
  33.0 2.4 %shard_map.49 = (f32[4,32,768]{2,1,0:T(8,128)S(1)}, f32[4,32,768]{2,1,0:T(8,128)S(1)}, f32[4,32,768]{2,1,0:T(8,128)S(1)}, f32[4,32,768]{2,1,0:T(8,128)S(1)}) custom-call(s32[8]{0:T(128)S(1)} %stack.53.refs_0_, bf16[1024,512]{1,0:T(8,128)(2,1)S(1)} %get-tuple-element.42.refs_1_, bf16[1024,512]{1,0:T(8,128)(2,1)S(1)} %get-tuple-element.43.refs_2_, ...), custom_call_target="tpu_custom_call" | custom-call | flops 4000000000 | bytes 12000000 | tf_op jit(solution)/shard_map/pallas_call | solution.py:302
  35.4 3.0 %collective-permute-start.9 = (f32[4,32,768]{2,1,0:T(8,128)S(1)}, f32[4,32,768]{2,1,0:T(8,128)S(1)}, u32[]{:S(2)}, u32[]{:S(2)}) collective-permute-start(f32[4,32,768]{2,1,0:T(8,128)S(1)} %get-tuple-element.48), channel_id=1, source_target_pairs={{0,32},{1,9},{2,34},{3,11},{4,36},{5,13},{6,38},{7,15},{8,40},{9,1... | collective-permute-start | bytes 1179656 | tf_op jit(solution)/shard_map/ppermute | solution.py:325
  38.4 0.8 collective-permute-start.8
  39.2 0.7 collective-permute-start.7
  39.9 8.0 %shard_map.50 = (bf16[1024,512]{1,0:T(8,128)(2,1)S(1)}, bf16[1024,512]{1,0:T(8,128)(2,1)S(1)}, bf16[1024,512]{1,0:T(8,128)(2,1)S(1)}, bf16[1024,512]{1,0:T(8,128)(2,1)S(1)}) custom-call(s32[8]{0:T(128)S(1)} %stack.53.refs_0_, f32[512,512]{1,0:T(8,128)S(1)} %bitcast.34, f32[512,512]{1,0:T(8,128)S(1)} %collective-permute-done.10.refs_2_, ...), custom_call_target="tpu_custom_call" | custom-call | flops 4000000000 | bytes 12000000 | tf_op jit(solution)/shard_map/pallas_call | solution.py:302
  49.2 0.8 pad_maximum_fusion.3
  50.5 3.0 %collective-permute-start.13 = (f32[32,1664]{1,0:T(8,128)}, f32[32,1664]{1,0:T(8,128)S(1)}, u32[]{:S(2)}, u32[]{:S(2)}) collective-permute-start(f32[32,1664]{1,0:T(8,128)} %get-tuple-element.52), channel_id=1, source_target_pairs={{0,12},{1,49},{2,14},{3,51},{4,0},{5,53},{6,2},{7,55},{8,4},{9,57}... | collective-permute-start | bytes 638984 | tf_op jit(solution)/shard_map/ppermute | solution.py:325
  53.5 3.2 %collective-permute-done.14 = f32[32,1664]{1,0:T(8,128)S(1)} collective-permute-done((f32[32,1664]{1,0:T(8,128)}, f32[32,1664]{1,0:T(8,128)S(1)}, u32[]{:S(2)}, u32[]{:S(2)}) %collective-permute-start.14) | collective-permute-done | bytes 213024 | tf_op jit(solution)/shard_map/ppermute | solution.py:325
  56.7 1.8 %collective-permute-done.13 = f32[32,1664]{1,0:T(8,128)S(1)} collective-permute-done((f32[32,1664]{1,0:T(8,128)}, f32[32,1664]{1,0:T(8,128)S(1)}, u32[]{:S(2)}, u32[]{:S(2)}) %collective-permute-start.13) | collective-permute-done | bytes 213024 | tf_op jit(solution)/shard_map/ppermute | solution.py:325
  58.5 1.2 collective-permute-done.12
  59.8 3.5 %collective-permute-start.15 = (f32[16,1664]{1,0:T(8,128)S(1)}, f32[16,1664]{1,0:T(8,128)S(1)}, u32[]{:S(2)}, u32[]{:S(2)}) collective-permute-start(f32[16,1664]{1,0:T(8,128)S(1)} %get-tuple-element.55), channel_id=1, source_target_pairs={{0,64},{1,65},{2,66},{3,67},{4,68},{5,69},{6,70},{7,71},{8,72},{9,... | collective-permute-start | bytes 319496 | tf_op jit(solution)/shard_map/ppermute | solution.py:411
  63.9 1.5 %collective-permute-done.15 = f32[16,1664]{1,0:T(8,128)S(1)} collective-permute-done((f32[16,1664]{1,0:T(8,128)S(1)}, f32[16,1664]{1,0:T(8,128)S(1)}, u32[]{:S(2)}, u32[]{:S(2)}) %collective-permute-start.15) | collective-permute-done | bytes 106528 | tf_op jit(solution)/shard_map/ppermute | solution.py:411
  65.4 2.1 %collective-permute-done.16 = f32[16,1664]{1,0:T(8,128)S(1)} collective-permute-done((f32[16,1664]{1,0:T(8,128)S(1)}, f32[16,1664]{1,0:T(8,128)S(1)}, u32[]{:S(2)}, u32[]{:S(2)}) %collective-permute-start.16) | collective-permute-done | bytes 106528 | tf_op jit(solution)/shard_map/ppermute | solution.py:409
  67.4 1.7 %collective-permute-done.17 = f32[16,1664]{1,0:T(8,128)S(1)} collective-permute-done((f32[16,1664]{1,0:T(8,128)S(1)}, f32[16,1664]{1,0:T(8,128)S(1)}, u32[]{:S(2)}, u32[]{:S(2)}) %collective-permute-start.17) | collective-permute-done | bytes 106528 | tf_op jit(solution)/shard_map/ppermute | solution.py:410
  69.2 3.3 %collective-permute-start.18 = (f32[2,16,1664]{2,1,0:T(8,128)S(1)}, f32[2,16,1664]{2,1,0:T(8,128)S(1)}, u32[]{:S(2)}, u32[]{:S(2)}) collective-permute-start(f32[2,16,1664]{2,1,0:T(8,128)S(1)} %pad_maximum_fusion.5), channel_id=1, source_target_pairs={{0,1},{1,0},{2,3},{3,2},{4,5},{5,4},{6,7},{7,6},{8,9},{9,8},{10,11... | collective-permute-start | bytes 638984 | tf_op jit(solution)/shard_map/ppermute | solution.py:415
  72.4 1.1 collective-permute-done.18.refs_4_
  73.5 1.0 shard_map.51.refs_1_
  74.7 4.7 %collective-permute-done.19.refs_2_ = f32[64,512]{1,0:T(8,128)S(1)} collective-permute-done((f32[64,512]{1,0:T(8,128)S(1)}, f32[64,512]{1,0:T(8,128)S(1)}, u32[]{:S(2)}, u32[]{:S(2)}) %collective-permute-start.19) | collective-permute-done | bytes 131104 | tf_op jit(solution)/shard_map/ppermute | solution.py:418
  79.4 1.2 collective-permute-start.20
  80.6 1.0 collective-permute-done.20.refs_3_
  81.5 1.4 %shard_map.52 = (f32[64,512]{1,0:T(8,128)}, f32[16,32,128]{2,1,0:T(8,128)}) custom-call(s32[8]{0:T(128)S(1)} %stack.53.refs_0_, f32[64,512]{1,0:T(8,128)S(1)} %shard_map.51.refs_1_, f32[64,512]{1,0:T(8,128)S(1)} %collective-permute-done.19.refs_2_, f32[64,512]{1,0:T(8,128)S(1)} %collective-permute-done.20.refs_3_, bf16[1024,512]{1,0:T(8,128)(2,1)S(1)} %copy-done.5, ...), custom_call_target="tpu_custom_call" | custom-call | flops 2000000000 | bytes 6000000 | tf_op jit(solution)/shard_map/pallas_call | solution.py:302
  82.9 4.8 %all-to-all-start = ((f32[16,32,128]{2,1,0:T(8,128)}), f32[16,32,128]{2,1,0:T(8,128)S(1)}, u32[]{:S(2)}, u32[]{:S(2)}) async-start(f32[16,32,128]{2,1,0:T(8,128)} %get-tuple-element.60), calls=%async_computation | async-start | bytes 524288 | tf_op jit(solution)/shard_map/all_to_all | solution.py:423
  87.7 8.8 %all-to-all-done = f32[16,32,128]{2,1,0:T(8,128)S(1)} async-done(((f32[16,32,128]{2,1,0:T(8,128)}), f32[16,32,128]{2,1,0:T(8,128)S(1)}, u32[]{:S(2)}, u32[]{:S(2)}) %all-to-all-start) | async-done | bytes 262176 | tf_op jit(solution)/shard_map/all_to_all | solution.py:423
  96.6 5.1 %collective-permute-done.21.refs_3_ = f32[8,32,128]{2,1,0:T(8,128)S(1)} collective-permute-done((f32[8,32,128]{2,1,0:T(8,128)S(1)}, f32[8,32,128]{2,1,0:T(8,128)S(1)}, u32[]{:S(2)}, u32[]{:S(2)}) %collective-permute-start.21) | collective-permute-done | bytes 131104 | tf_op jit(solution)/shard_map/ppermute | solution.py:440
  101.8 0.8 collective-permute-start.22
  102.6 1.2 collective-permute-done.22.refs_4_
  103.8 1.4 %shard_map.53.refs_1_ = f32[64,512]{1,0:T(8,128)S(1)} custom-call(s32[8]{0:T(128)S(1)} %stack.53.refs_0_, s32[16]{0:T(128)S(1)} %copy-done.3, f32[8,32,128]{2,1,0:T(8,128)S(1)} %constant_dynamic-slice_fusion.refs_2_, f32[8,32,128]{2,1,0:T(8,128)S(1)} %collective-permute-done.21.refs_3_, f32[2,8,32,128]{3,2,1,0:T(8,128)S(1)} %collective-permute-done.22.refs_4_, ...), custom_call_target="tpu_custom_call" | custom-call | flops 2000000000 | bytes 6000000 | tf_op jit(solution)/shard_map/pallas_call | solution.py:302
  105.3 4.7 %collective-permute-done.23.refs_2_ = f32[64,512]{1,0:T(8,128)S(1)} collective-permute-done((f32[64,512]{1,0:T(8,128)S(1)}, f32[64,512]{1,0:T(8,128)S(1)}, u32[]{:S(2)}, u32[]{:S(2)}) %collective-permute-start.23) | collective-permute-done | bytes 131104 | tf_op jit(solution)/shard_map/ppermute | solution.py:418
  110.0 1.2 collective-permute-start.24
  111.2 1.0 collective-permute-done.24.refs_3_
  112.2 0.6 shard_map.54
  112.8 11.9 %all_to_all.10.refs_3_ = f32[16,32,128]{2,1,0:T(8,128)S(1)} all-to-all(f32[16,32,128]{2,1,0:T(8,128)S(1)} %get-tuple-element.62), channel_id=1, replica_groups={{1,5,9,13,17,21,25,29,32,36,40,44,48,52,56,60},{2,6,10,14,18,22,26,30,6..., dimensions={0} | all-to-all | bytes 524288 | tf_op jit(solution)/shard_map/all_to_all | solution.py:423
  124.8 1.4 %shard_map.55 = f32[64,512]{1,0:T(8,128)} custom-call(s32[8]{0:T(128)S(1)} %stack.53.refs_0_, f32[1]{0:T(128)} %constant.82.clone.1.refs_1_, f32[64,512]{1,0:T(8,128)S(1)} %get-tuple-element.61.refs_2_, f32[16,32,128]{2,1,0:T(8,128)S(1)} %all_to_all.10.refs_3_), custom_call_target="tpu_custom_call" | custom-call | tf_op jit(solution)/shard_map/pallas_call | solution.py:302
  (53 shorter events, 3.7 us)
Async XLA Ops:
  0.0 7.8 %collective-permute-start = (f32[1024,512]{1,0:T(8,128)}, f32[1024,512]{1,0:T(8,128)}, u32[]{:S(2)}, u32[]{:S(2)}) collective-permute-start(f32[1024,512]{1,0:T(8,128)} %refs_1_.7), channel_id=1, source_target_pairs={{0,1},{1,0},{2,3},{3,2},{4,5},{5,4},{6,7},{7,6},{8,9},{9,8},{10,11... | collective-permute-start | bytes 6291464 | tf_op jit(solution)/shard_map/ppermute | solution.py:345
  2.4 5.2 %copy-start.1 = (f32[1024,512]{1,0:T(8,128)S(1)}, f32[1024,512]{1,0:T(8,128)}, u32[]{:S(2)}) copy-start(f32[1024,512]{1,0:T(8,128)} %refs_1_.7) | copy-start | bytes 6291460
  2.4 9.9 %collective-permute-start.1 = (f32[512,128]{1,0:T(8,128)S(1)}, f32[512,128]{1,0:T(8,128)S(1)}, u32[]{:S(2)}, u32[]{:S(2)}) collective-permute-start(f32[512,128]{1,0:T(8,128)S(1)} %constant_dynamic-slice_fusion.3), channel_id=1, source_target_pairs={{0,2},{1,3},{2,0},{3,1},{4,6},{5,7},{6,4},{7,5},{8,10},{9,11},{10,... | collective-permute-start | bytes 786440 | tf_op jit(solution)/shard_map/ppermute | solution.py:349
  7.3 32.5 %collective-permute-start.11 = (f32[1024,512]{1,0:T(8,128)}, f32[1024,512]{1,0:T(8,128)}, u32[]{:S(2)}, u32[]{:S(2)}) collective-permute-start(f32[1024,512]{1,0:T(8,128)} %slice.11), channel_id=1, source_target_pairs={{0,1},{1,0},{2,3},{3,2},{4,5},{5,4},{6,7},{7,6},{8,9},{9,8},{10,11... | collective-permute-start | bytes 6291464 | tf_op jit(solution)/shard_map/ppermute | solution.py:401
  7.8 22.1 %collective-permute-start.5 = (f32[512,384]{1,0:T(8,128)S(1)}, f32[512,384]{1,0:T(8,128)S(1)}, u32[]{:S(2)}, u32[]{:S(2)}) collective-permute-start(f32[512,384]{1,0:T(8,128)S(1)} %dynamic-slice), channel_id=1, source_target_pairs={{0,2},{1,3},{2,0},{3,1},{4,6},{5,7},{6,4},{7,5},{8,10},{9,11},{10,... | collective-permute-start | bytes 2359304 | tf_op jit(solution)/shard_map/ppermute | solution.py:349
  14.8 9.0 %collective-permute-start.2 = (f32[4,32,896]{2,1,0:T(8,128)S(1)}, f32[4,32,896]{2,1,0:T(8,128)S(1)}, u32[]{:S(2)}, u32[]{:S(2)}) collective-permute-start(f32[4,32,896]{2,1,0:T(8,128)S(1)} %get-tuple-element.36), channel_id=1, source_target_pairs={{0,16},{1,5},{2,18},{3,7},{4,20},{5,9},{6,22},{7,11},{8,24},{9,13}... | collective-permute-start | bytes 1376264 | tf_op jit(solution)/shard_map/ppermute | solution.py:325
  16.2 11.9 %collective-permute-start.3 = (f32[4,32,896]{2,1,0:T(8,128)S(1)}, f32[4,32,896]{2,1,0:T(8,128)S(1)}, u32[]{:S(2)}, u32[]{:S(2)}) collective-permute-start(f32[4,32,896]{2,1,0:T(8,128)S(1)} %get-tuple-element.37), channel_id=1, source_target_pairs={{0,48},{1,13},{2,50},{3,15},{4,52},{5,1},{6,54},{7,3},{8,56},{9,5}... | collective-permute-start | bytes 1376264 | tf_op jit(solution)/shard_map/ppermute | solution.py:325
  17.7 12.2 %collective-permute-start.4 = (f32[4,32,896]{2,1,0:T(8,128)S(1)}, f32[4,32,896]{2,1,0:T(8,128)S(1)}, u32[]{:S(2)}, u32[]{:S(2)}) collective-permute-start(f32[4,32,896]{2,1,0:T(8,128)S(1)} %get-tuple-element.38), channel_id=1, source_target_pairs={{0,32},{1,9},{2,34},{3,11},{4,36},{5,13},{6,38},{7,15},{8,40},{9,1... | collective-permute-start | bytes 1376264 | tf_op jit(solution)/shard_map/ppermute | solution.py:325
  19.2 11.8 %copy-start.2 = (f32[1,512,512]{2,1,0:T(8,128)S(1)}, f32[1,512,512]{2,1,0:T(8,128)}, u32[]{:S(2)}) copy-start(f32[1,512,512]{2,1,0:T(8,128)} %param.6) | copy-start | bytes 3145732
  29.8 3.1 %collective-permute-start.6 = (f32[512,384]{1,0:T(8,128)S(1)}, f32[512,384]{1,0:T(8,128)S(1)}, u32[]{:S(2)}, u32[]{:S(2)}) collective-permute-start(f32[512,384]{1,0:T(8,128)S(1)} %collective-permute-done.5), channel_id=1, source_target_pairs={{0,1},{1,0},{2,3},{3,2},{4,5},{5,4},{6,7},{7,6},{8,9},{9,8},{10,11... | collective-permute-start | bytes 2359304 | tf_op jit(solution)/shard_map/ppermute | solution.py:379
  31.1 8.8 %collective-permute-start.10 = (f32[512,512]{1,0:T(8,128)S(1)}, f32[512,512]{1,0:T(8,128)S(1)}, u32[]{:S(2)}, u32[]{:S(2)}) collective-permute-start(f32[512,512]{1,0:T(8,128)S(1)} %bitcast.33), channel_id=1, source_target_pairs={{0,1},{1,0},{2,3},{3,2},{4,5},{5,4},{6,7},{7,6},{8,9},{9,8},{10,11... | collective-permute-start | bytes 3145736 | tf_op jit(solution)/shard_map/ppermute | solution.py:400
  31.3 8.6 %copy-start = (f32[2048,512]{1,0:T(8,128)S(1)}, f32[2048,512]{1,0:T(8,128)}, u32[]{:S(2)}) copy-start(f32[2048,512]{1,0:T(8,128)} %refs_3_.1) | copy-start | bytes 12582916
  35.4 12.5 %collective-permute-start.9 = (f32[4,32,768]{2,1,0:T(8,128)S(1)}, f32[4,32,768]{2,1,0:T(8,128)S(1)}, u32[]{:S(2)}, u32[]{:S(2)}) collective-permute-start(f32[4,32,768]{2,1,0:T(8,128)S(1)} %get-tuple-element.48), channel_id=1, source_target_pairs={{0,32},{1,9},{2,34},{3,11},{4,36},{5,13},{6,38},{7,15},{8,40},{9,1... | collective-permute-start | bytes 1179656 | tf_op jit(solution)/shard_map/ppermute | solution.py:325
  38.4 10.1 %collective-permute-start.8 = (f32[4,32,768]{2,1,0:T(8,128)S(1)}, f32[4,32,768]{2,1,0:T(8,128)S(1)}, u32[]{:S(2)}, u32[]{:S(2)}) collective-permute-start(f32[4,32,768]{2,1,0:T(8,128)S(1)} %get-tuple-element.47), channel_id=1, source_target_pairs={{0,48},{1,13},{2,50},{3,15},{4,52},{5,1},{6,54},{7,3},{8,56},{9,5}... | collective-permute-start | bytes 1179656 | tf_op jit(solution)/shard_map/ppermute | solution.py:325
  39.2 9.3 %collective-permute-start.7 = (f32[4,32,768]{2,1,0:T(8,128)S(1)}, f32[4,32,768]{2,1,0:T(8,128)S(1)}, u32[]{:S(2)}, u32[]{:S(2)}) collective-permute-start(f32[4,32,768]{2,1,0:T(8,128)S(1)} %get-tuple-element.46), channel_id=1, source_target_pairs={{0,16},{1,5},{2,18},{3,7},{4,20},{5,9},{6,22},{7,11},{8,24},{9,13}... | collective-permute-start | bytes 1179656 | tf_op jit(solution)/shard_map/ppermute | solution.py:325
  47.8 1.0 copy-start.4
  47.8 1.3 %copy-start.7 = (bf16[1024,512]{1,0:T(8,128)(2,1)}, bf16[1024,512]{1,0:T(8,128)(2,1)S(1)}, u32[]{:S(2)}) copy-start(bf16[1024,512]{1,0:T(8,128)(2,1)S(1)} %get-tuple-element.59.refs_5_) | copy-start | bytes 3145732
  48.6 24.9 %copy-start.3 = (s32[16]{0:T(128)S(1)}, s32[16]{0:T(128)}, u32[]{:S(2)}) copy-start(s32[16]{0:T(128)} %refs_1_.9) | copy-start | bytes 196
  50.0 6.7 %collective-permute-start.14 = (f32[32,1664]{1,0:T(8,128)}, f32[32,1664]{1,0:T(8,128)S(1)}, u32[]{:S(2)}, u32[]{:S(2)}) collective-permute-start(f32[32,1664]{1,0:T(8,128)} %get-tuple-element.53), channel_id=1, source_target_pairs={{0,8},{1,33},{2,10},{3,35},{4,12},{5,37},{6,14},{7,39},{8,0},{9,41... | collective-permute-start | bytes 638984 | tf_op jit(solution)/shard_map/ppermute | solution.py:325
  50.5 8.0 %collective-permute-start.13 = (f32[32,1664]{1,0:T(8,128)}, f32[32,1664]{1,0:T(8,128)S(1)}, u32[]{:S(2)}, u32[]{:S(2)}) collective-permute-start(f32[32,1664]{1,0:T(8,128)} %get-tuple-element.52), channel_id=1, source_target_pairs={{0,12},{1,49},{2,14},{3,51},{4,0},{5,53},{6,2},{7,55},{8,4},{9,57}... | collective-permute-start | bytes 638984 | tf_op jit(solution)/shard_map/ppermute | solution.py:325
  53.5 6.2 %collective-permute-start.12 = (f32[32,1664]{1,0:T(8,128)S(1)}, f32[32,1664]{1,0:T(8,128)S(1)}, u32[]{:S(2)}, u32[]{:S(2)}) collective-permute-start(f32[32,1664]{1,0:T(8,128)S(1)} %get-tuple-element.51), channel_id=1, source_target_pairs={{0,4},{1,17},{2,6},{3,19},{4,8},{5,21},{6,10},{7,23},{8,12},{9,25}... | collective-permute-start | bytes 638984 | tf_op jit(solution)/shard_map/ppermute | solution.py:325
  59.8 5.6 %collective-permute-start.15 = (f32[16,1664]{1,0:T(8,128)S(1)}, f32[16,1664]{1,0:T(8,128)S(1)}, u32[]{:S(2)}, u32[]{:S(2)}) collective-permute-start(f32[16,1664]{1,0:T(8,128)S(1)} %get-tuple-element.55), channel_id=1, source_target_pairs={{0,64},{1,65},{2,66},{3,67},{4,68},{5,69},{6,70},{7,71},{8,72},{9,... | collective-permute-start | bytes 319496 | tf_op jit(solution)/shard_map/ppermute | solution.py:411
  63.2 4.2 %collective-permute-start.16 = (f32[16,1664]{1,0:T(8,128)S(1)}, f32[16,1664]{1,0:T(8,128)S(1)}, u32[]{:S(2)}, u32[]{:S(2)}) collective-permute-start(f32[16,1664]{1,0:T(8,128)S(1)} %get-tuple-element.54), channel_id=1, source_target_pairs={{0,2},{1,3},{2,0},{3,1},{4,6},{5,7},{6,4},{7,5},{8,10},{9,11},{10,... | collective-permute-start | bytes 319496 | tf_op jit(solution)/shard_map/ppermute | solution.py:409
  63.9 5.2 %collective-permute-start.17 = (f32[16,1664]{1,0:T(8,128)S(1)}, f32[16,1664]{1,0:T(8,128)S(1)}, u32[]{:S(2)}, u32[]{:S(2)}) collective-permute-start(f32[16,1664]{1,0:T(8,128)S(1)} %get-tuple-element.55), channel_id=1, source_target_pairs={{0,66},{1,67},{2,64},{3,65},{4,70},{5,71},{6,68},{7,69},{8,74},{9,... | collective-permute-start | bytes 319496 | tf_op jit(solution)/shard_map/ppermute | solution.py:410
  69.2 4.3 %collective-permute-start.18 = (f32[2,16,1664]{2,1,0:T(8,128)S(1)}, f32[2,16,1664]{2,1,0:T(8,128)S(1)}, u32[]{:S(2)}, u32[]{:S(2)}) collective-permute-start(f32[2,16,1664]{2,1,0:T(8,128)S(1)} %pad_maximum_fusion.5), channel_id=1, source_target_pairs={{0,1},{1,0},{2,3},{3,2},{4,5},{5,4},{6,7},{7,6},{8,9},{9,8},{10,11... | collective-permute-start | bytes 638984 | tf_op jit(solution)/shard_map/ppermute | solution.py:415
  73.5 8.0 %copy-start.5 = (bf16[1024,512]{1,0:T(8,128)(2,1)S(1)}, bf16[1024,512]{1,0:T(8,128)(2,1)}, u32[]{:S(2)}) copy-start(bf16[1024,512]{1,0:T(8,128)(2,1)} %copy-done.4) | copy-start | bytes 3145732
  73.5 8.0 %copy-start.8 = (bf16[1024,512]{1,0:T(8,128)(2,1)S(1)}, bf16[1024,512]{1,0:T(8,128)(2,1)}, u32[]{:S(2)}) copy-start(bf16[1024,512]{1,0:T(8,128)(2,1)} %copy-done.7) | copy-start | bytes 3145732
  74.6 4.8 %collective-permute-start.19 = (f32[64,512]{1,0:T(8,128)S(1)}, f32[64,512]{1,0:T(8,128)S(1)}, u32[]{:S(2)}, u32[]{:S(2)}) collective-permute-start(f32[64,512]{1,0:T(8,128)S(1)} %shard_map.51.refs_1_), channel_id=1, source_target_pairs={{0,2},{1,3},{2,0},{3,1},{4,6},{5,7},{6,4},{7,5},{8,10},{9,11},{10,... | collective-permute-start | bytes 393224 | tf_op jit(solution)/shard_map/ppermute | solution.py:418
  79.4 2.2 %collective-permute-start.20 = (f32[64,512]{1,0:T(8,128)S(1)}, f32[64,512]{1,0:T(8,128)S(1)}, u32[]{:S(2)}, u32[]{:S(2)}) collective-permute-start(f32[64,512]{1,0:T(8,128)S(1)} %collective-permute-done.19.refs_2_), channel_id=1, source_target_pairs={{0,1},{1,0},{2,3},{3,2},{4,5},{5,4},{6,7},{7,6},{8,9},{9,8},{10,11... | collective-permute-start | bytes 393224 | tf_op jit(solution)/shard_map/ppermute | solution.py:419
  82.9 13.6 %all-to-all-start = ((f32[16,32,128]{2,1,0:T(8,128)}), f32[16,32,128]{2,1,0:T(8,128)S(1)}, u32[]{:S(2)}, u32[]{:S(2)}) async-start(f32[16,32,128]{2,1,0:T(8,128)} %get-tuple-element.60), calls=%async_computation | async-start | bytes 524288 | tf_op jit(solution)/shard_map/all_to_all | solution.py:423
  96.5 5.3 %collective-permute-start.21 = (f32[8,32,128]{2,1,0:T(8,128)S(1)}, f32[8,32,128]{2,1,0:T(8,128)S(1)}, u32[]{:S(2)}, u32[]{:S(2)}) collective-permute-start(f32[8,32,128]{2,1,0:T(8,128)S(1)} %constant_dynamic-slice_fusion.refs_2_), channel_id=1, source_target_pairs={{0,2},{1,3},{2,0},{3,1},{4,6},{5,7},{6,4},{7,5},{8,10},{9,11},{10,... | collective-permute-start | bytes 393224 | tf_op jit(solution)/shard_map/ppermute | solution.py:440
  101.8 10.4 %copy-start.6 = (bf16[1024,512]{1,0:T(8,128)(2,1)S(1)}, bf16[1024,512]{1,0:T(8,128)(2,1)}, u32[]{:S(2)}) copy-start(bf16[1024,512]{1,0:T(8,128)(2,1)} %copy-done.4) | copy-start | bytes 3145732
  101.8 10.4 %copy-start.9 = (bf16[1024,512]{1,0:T(8,128)(2,1)S(1)}, bf16[1024,512]{1,0:T(8,128)(2,1)}, u32[]{:S(2)}) copy-start(bf16[1024,512]{1,0:T(8,128)(2,1)} %copy-done.7) | copy-start | bytes 3145732
  101.8 2.0 %collective-permute-start.22 = (f32[2,8,32,128]{3,2,1,0:T(8,128)S(1)}, f32[2,8,32,128]{3,2,1,0:T(8,128)S(1)}, u32[]{:S(2)}, u32[]{:S(2)}) collective-permute-start(f32[2,8,32,128]{3,2,1,0:T(8,128)S(1)} %pad_maximum_fusion), channel_id=1, source_target_pairs={{0,1},{1,0},{2,3},{3,2},{4,5},{5,4},{6,7},{7,6},{8,9},{9,8},{10,11... | collective-permute-start | bytes 786440 | tf_op jit(solution)/shard_map/ppermute | solution.py:415
  105.2 4.8 %collective-permute-start.23 = (f32[64,512]{1,0:T(8,128)S(1)}, f32[64,512]{1,0:T(8,128)S(1)}, u32[]{:S(2)}, u32[]{:S(2)}) collective-permute-start(f32[64,512]{1,0:T(8,128)S(1)} %shard_map.53.refs_1_), channel_id=1, source_target_pairs={{0,2},{1,3},{2,0},{3,1},{4,6},{5,7},{6,4},{7,5},{8,10},{9,11},{10,... | collective-permute-start | bytes 393224 | tf_op jit(solution)/shard_map/ppermute | solution.py:418
  110.0 2.2 %collective-permute-start.24 = (f32[64,512]{1,0:T(8,128)S(1)}, f32[64,512]{1,0:T(8,128)S(1)}, u32[]{:S(2)}, u32[]{:S(2)}) collective-permute-start(f32[64,512]{1,0:T(8,128)S(1)} %collective-permute-done.23.refs_2_), channel_id=1, source_target_pairs={{0,1},{1,0},{2,3},{3,2},{4,5},{5,4},{6,7},{7,6},{8,9},{9,8},{10,11... | collective-permute-start | bytes 393224 | tf_op jit(solution)/shard_map/ppermute | solution.py:419

commit v7 on v6

--- a/solution.py
+++ b/solution.py
@@ -385,7 +385,7 @@
         COSTS[3],
         *prepared,
         across[1],
-        after=(early_sum,),
+        after=tuple(arrived),
     )
     late_sum, _ = sum_along(late, False)
     parts = [jnp.concatenate([a, b], -1) for a, b in zip(early_sum, late_sum)]

time: 127 us -> 136 us (1.071)
  starting transfers between devices: 32.9 us -> 37.2 us
  waiting for transfers between devices: 49.5 us -> 53.7 us
    ppermute x9, waiting for transfers between devices: 15.1 us -> 22.3 us  [sum_along(): lax.ppermute(values[step], ('pts', 'lm'), plane_step(step, swapped))]
    ppermute x2, starting transfers between devices: 4.07 us -> 1.43 us  [spread(): lax.ppermute(jnp.stack([value, away]), 'lm', OTHER_CORE)]
    ppermute x2, starting transfers between devices: 0.17 us -> 2.33 us  [hop(): got = lax.ppermute(value, 'lm', OTHER_CHIP)]
    ppermute x2, waiting for transfers between devices: 9.39 us -> 7.25 us  [hop(): got = lax.ppermute(value, 'lm', OTHER_CHIP)]
    ppermute x2, waiting for transfers between devices: 0.01 us -> 2.01 us  [per_device(): across = [lax.ppermute(value, 'lm', OTHER_CHIP) for value in across]]
    ppermute x1, starting transfers between devices: 0.09 us -> 2 us  [per_device(): away = lax.ppermute(value, 'lm', OTHER_CHIP)]
    ppermute x1, waiting for transfers between devices: 1.69 us -> 0.01 us  [per_device(): across[1] = lax.ppermute(across[1], 'lm', OTHER_CORE)]
    ppermute x9, starting transfers between devices: 12.4 us -> 14.1 us  [sum_along(): lax.ppermute(values[step], ('pts', 'lm'), plane_step(step, swapped))]
  transfers between devices with their start and end apart: 26 -> 26, of which waited for: 19 -> 20; matrix products, arithmetic and copies ran while one was open for 3% -> 3% of each run, Pallas kernels for 16% -> 13%
where the time goes in v7:
time: 136 us; the launch traced here: 135 us
  waiting for transfers between devices  53.7 us (39%)
  starting transfers between devices  37.2 us (27%)
  Pallas kernels  25.6 us (19%)
  blocking collectives  11.9 us (9%)
  local copies, waits for them, and re-layouts  5.38 us (4%)
    pallas_call x10, Pallas kernels, kernel_call(): pl.pallas_call(body, out_shape=out_shape, in_specs=[smem] * len(scalars)...  25.6 us
    ppermute x9, waiting for transfers between devices, sum_along(): lax.ppermute(values[step], ('pts', 'lm'), plane_step(step, swapped))  22.3 us
    ppermute x9, starting transfers between devices, sum_along(): lax.ppermute(values[step], ('pts', 'lm'), plane_step(step, swapped))  14.1 us
    all_to_all x1, blocking collectives, turned(): lax.all_to_all(packed, ('pts', 'lm'), 0, 0, axis_index_groups=groups, til...  11.9 us
    all_to_all x1, waiting for transfers between devices, turned(): lax.all_to_all(packed, ('pts', 'lm'), 0, 0, axis_index_groups=groups, til...  8.77 us
    ppermute x2, waiting for transfers between devices, hop(): got = lax.ppermute(value, 'lm', OTHER_CHIP)  7.25 us
    all_to_all x1, starting transfers between devices, turned(): lax.all_to_all(packed, ('pts', 'lm'), 0, 0, axis_index_groups=groups, til...  5.4 us
    ppermute x1, waiting for transfers between devices, per_device(): away = lax.ppermute(value, 'lm', OTHER_CHIP)  3.79 us
  transfers between devices with their start and end apart: 26, of which 20 were waited for; matrix products, arithmetic and copies ran while one was open for 3% of the time, Pallas kernels for 13%

profile of v7, /device:TPU:1, one launch (start us, length us, event | category | flops | bytes accessed | tf_op | source)
XLA Modules:
  0.0 135.2 jit_solution(1488936646461611078)
XLA Ops:
  0.0 1.4 %collective-permute-start = (f32[1024,512]{1,0:T(8,128)}, f32[1024,512]{1,0:T(8,128)}, u32[]{:S(2)}, u32[]{:S(2)}) collective-permute-start(f32[1024,512]{1,0:T(8,128)} %refs_1_.7), channel_id=1, source_target_pairs={{0,1},{1,0},{2,3},{3,2},{4,5},{5,4},{6,7},{7,6},{8,9},{9,8},{10,11... | collective-permute-start | bytes 6291464 | tf_op jit(solution)/shard_map/ppermute | solution.py:345
  1.4 1.0 constant_dynamic-slice_fusion.3
  2.4 1.8 %collective-permute-start.1 = (f32[512,128]{1,0:T(8,128)S(1)}, f32[512,128]{1,0:T(8,128)S(1)}, u32[]{:S(2)}, u32[]{:S(2)}) collective-permute-start(f32[512,128]{1,0:T(8,128)S(1)} %constant_dynamic-slice_fusion.3), channel_id=1, source_target_pairs={{0,2},{1,3},{2,0},{3,1},{4,6},{5,7},{6,4},{7,5},{8,10},{9,11},{10,... | collective-permute-start | bytes 786440 | tf_op jit(solution)/shard_map/ppermute | solution.py:349
  4.2 3.1 %slice.11 = f32[1024,512]{1,0:T(8,128)} slice(f32[2048,512]{1,0:T(8,128)} %refs_3_.1), slice={[0:1024], [0:512]} | slice | bytes 4194304 | tf_op jit(solution)/shard_map/slice | solution.py:401
  7.8 4.5 %shard_map.46.refs_4_ = f32[512,1024]{1,0:T(8,128)S(1)} custom-call(s32[8]{0:T(128)S(1)} %stack.53.refs_0_, f32[1024,512]{1,0:T(8,128)S(1)} %copy-done.1, f32[1024,512]{1,0:T(8,128)} %collective-permute-done.refs_2_), custom_call_target="tpu_custom_call" | custom-call | flops 40000000000 | bytes 120000000 | tf_op jit(solution)/shard_map/pallas_call | solution.py:302
  12.3 2.5 %shard_map.47 = (f32[4,32,896]{2,1,0:T(8,128)S(1)}, f32[4,32,896]{2,1,0:T(8,128)S(1)}, f32[4,32,896]{2,1,0:T(8,128)S(1)}, f32[4,32,896]{2,1,0:T(8,128)S(1)}) custom-call(s32[8]{0:T(128)S(1)} %stack.53.refs_0_, f32[1024,512]{1,0:T(8,128)S(1)} %copy-done.1, f32[1024,512]{1,0:T(8,128)} %collective-permute-done.refs_2_, ...), custom_call_target="tpu_custom_call" | custom-call | flops 6000000000 | bytes 18000000 | tf_op jit(solution)/shard_map/pallas_call | solution.py:302
  14.8 1.4 %collective-permute-start.2 = (f32[4,32,896]{2,1,0:T(8,128)S(1)}, f32[4,32,896]{2,1,0:T(8,128)S(1)}, u32[]{:S(2)}, u32[]{:S(2)}) collective-permute-start(f32[4,32,896]{2,1,0:T(8,128)S(1)} %get-tuple-element.36), channel_id=1, source_target_pairs={{0,16},{1,5},{2,18},{3,7},{4,20},{5,9},{6,22},{7,11},{8,24},{9,13}... | collective-permute-start | bytes 1376264 | tf_op jit(solution)/shard_map/ppermute | solution.py:325
  16.2 1.0 collective-permute-start.10
  17.2 2.7 %collective-permute-start.3 = (f32[4,32,896]{2,1,0:T(8,128)S(1)}, f32[4,32,896]{2,1,0:T(8,128)S(1)}, u32[]{:S(2)}, u32[]{:S(2)}) collective-permute-start(f32[4,32,896]{2,1,0:T(8,128)S(1)} %get-tuple-element.37), channel_id=1, source_target_pairs={{0,48},{1,13},{2,50},{3,15},{4,52},{5,1},{6,54},{7,3},{8,56},{9,5}... | collective-permute-start | bytes 1376264 | tf_op jit(solution)/shard_map/ppermute | solution.py:325
  19.9 3.8 %collective-permute-done.2.refs_4_ = f32[4,32,896]{2,1,0:T(8,128)S(1)} collective-permute-done((f32[4,32,896]{2,1,0:T(8,128)S(1)}, f32[4,32,896]{2,1,0:T(8,128)S(1)}, u32[]{:S(2)}, u32[]{:S(2)}) %collective-permute-start.2) | collective-permute-done | bytes 458784 | tf_op jit(solution)/shard_map/ppermute | solution.py:325
  23.8 1.6 %collective-permute-start.4 = (f32[4,32,896]{2,1,0:T(8,128)S(1)}, f32[4,32,896]{2,1,0:T(8,128)S(1)}, u32[]{:S(2)}, u32[]{:S(2)}) collective-permute-start(f32[4,32,896]{2,1,0:T(8,128)S(1)} %get-tuple-element.38), channel_id=1, source_target_pairs={{0,32},{1,9},{2,34},{3,11},{4,36},{5,13},{6,38},{7,15},{8,40},{9,1... | collective-permute-start | bytes 1376264 | tf_op jit(solution)/shard_map/ppermute | solution.py:325
  25.4 2.4 %shard_map.48 = (bf16[1024,512]{1,0:T(8,128)(2,1)S(1)}, bf16[1024,512]{1,0:T(8,128)(2,1)S(1)}) custom-call(s32[8]{0:T(128)S(1)} %stack.53.refs_0_, f32[1024,512]{1,0:T(8,128)S(1)} %copy-done.1, f32[1024,512]{1,0:T(8,128)} %collective-permute-done.refs_2_, f32[4,32,896]{2,1,0:T(8,128)S(1)} %get-tuple-element.35.refs_3_.refs_5_), custom_call_target="tpu_custom_call" | custom-call | flops 4000000000 | bytes 12000000 | tf_op jit(solution)/shard_map/pallas_call | solution.py:302
  27.8 5.1 %collective-permute-done.4.refs_6_ = f32[4,32,896]{2,1,0:T(8,128)S(1)} collective-permute-done((f32[4,32,896]{2,1,0:T(8,128)S(1)}, f32[4,32,896]{2,1,0:T(8,128)S(1)}, u32[]{:S(2)}, u32[]{:S(2)}) %collective-permute-start.4) | collective-permute-done | bytes 458784 | tf_op jit(solution)/shard_map/ppermute | solution.py:325
  32.9 2.0 %collective-permute-done.5 = f32[512,384]{1,0:T(8,128)S(1)} collective-permute-done((f32[512,384]{1,0:T(8,128)S(1)}, f32[512,384]{1,0:T(8,128)S(1)}, u32[]{:S(2)}, u32[]{:S(2)}) %collective-permute-start.5) | collective-permute-done | bytes 786464 | tf_op jit(solution)/shard_map/ppermute | solution.py:349
  34.9 1.2 collective-permute-start.6
  36.1 7.9 %shard_map.50 = (bf16[1024,512]{1,0:T(8,128)(2,1)S(1)}, bf16[1024,512]{1,0:T(8,128)(2,1)S(1)}, bf16[1024,512]{1,0:T(8,128)(2,1)S(1)}, bf16[1024,512]{1,0:T(8,128)(2,1)S(1)}) custom-call(s32[8]{0:T(128)S(1)} %stack.53.refs_0_, f32[512,512]{1,0:T(8,128)S(1)} %bitcast.34, f32[512,512]{1,0:T(8,128)S(1)} %collective-permute-done.10.refs_2_, ...), custom_call_target="tpu_custom_call" | custom-call | flops 4000000000 | bytes 12000000 | tf_op jit(solution)/shard_map/pallas_call | solution.py:302
  44.1 1.0 copy-done.4
  45.1 2.4 %shard_map.49 = (f32[4,32,768]{2,1,0:T(8,128)S(1)}, f32[4,32,768]{2,1,0:T(8,128)S(1)}, f32[4,32,768]{2,1,0:T(8,128)S(1)}, f32[4,32,768]{2,1,0:T(8,128)S(1)}) custom-call(s32[8]{0:T(128)S(1)} %stack.53.refs_0_, bf16[1024,512]{1,0:T(8,128)(2,1)S(1)} %get-tuple-element.42.refs_1_, bf16[1024,512]{1,0:T(8,128)(2,1)S(1)} %get-tuple-element.43.refs_2_, ...), custom_call_target="tpu_custom_call" | custom-call | flops 4000000000 | bytes 12000000 | tf_op jit(solution)/shard_map/pallas_call | solution.py:302
  47.6 2.7 %collective-permute-start.9 = (f32[4,32,768]{2,1,0:T(8,128)S(1)}, f32[4,32,768]{2,1,0:T(8,128)S(1)}, u32[]{:S(2)}, u32[]{:S(2)}) collective-permute-start(f32[4,32,768]{2,1,0:T(8,128)S(1)} %get-tuple-element.48), channel_id=1, source_target_pairs={{0,32},{1,9},{2,34},{3,11},{4,36},{5,13},{6,38},{7,15},{8,40},{9,1... | collective-permute-start | bytes 1179656 | tf_op jit(solution)/shard_map/ppermute | solution.py:325
  50.2 1.1 collective-permute-start.8
  51.9 4.0 %collective-permute-done.9 = f32[4,32,768]{2,1,0:T(8,128)S(1)} collective-permute-done((f32[4,32,768]{2,1,0:T(8,128)S(1)}, f32[4,32,768]{2,1,0:T(8,128)S(1)}, u32[]{:S(2)}, u32[]{:S(2)}) %collective-permute-start.9) | collective-permute-done | bytes 393248 | tf_op jit(solution)/shard_map/ppermute | solution.py:325
  55.9 3.3 %collective-permute-done.8 = f32[4,32,768]{2,1,0:T(8,128)S(1)} collective-permute-done((f32[4,32,768]{2,1,0:T(8,128)S(1)}, f32[4,32,768]{2,1,0:T(8,128)S(1)}, u32[]{:S(2)}, u32[]{:S(2)}) %collective-permute-start.8) | collective-permute-done | bytes 393248 | tf_op jit(solution)/shard_map/ppermute | solution.py:325
  61.0 2.7 %collective-permute-start.14 = (f32[32,1664]{1,0:T(8,128)}, f32[32,1664]{1,0:T(8,128)S(1)}, u32[]{:S(2)}, u32[]{:S(2)}) collective-permute-start(f32[32,1664]{1,0:T(8,128)} %get-tuple-element.53), channel_id=1, source_target_pairs={{0,8},{1,33},{2,10},{3,35},{4,12},{5,37},{6,14},{7,39},{8,0},{9,41... | collective-permute-start | bytes 638984 | tf_op jit(solution)/shard_map/ppermute | solution.py:325
  65.2 2.2 %collective-permute-done.14 = f32[32,1664]{1,0:T(8,128)S(1)} collective-permute-done((f32[32,1664]{1,0:T(8,128)}, f32[32,1664]{1,0:T(8,128)S(1)}, u32[]{:S(2)}, u32[]{:S(2)}) %collective-permute-start.14) | collective-permute-done | bytes 213024 | tf_op jit(solution)/shard_map/ppermute | solution.py:325
  67.4 2.3 %collective-permute-done.13 = f32[32,1664]{1,0:T(8,128)S(1)} collective-permute-done((f32[32,1664]{1,0:T(8,128)}, f32[32,1664]{1,0:T(8,128)S(1)}, u32[]{:S(2)}, u32[]{:S(2)}) %collective-permute-start.13) | collective-permute-done | bytes 213024 | tf_op jit(solution)/shard_map/ppermute | solution.py:325
  70.5 3.4 %collective-permute-start.15 = (f32[16,1664]{1,0:T(8,128)S(1)}, f32[16,1664]{1,0:T(8,128)S(1)}, u32[]{:S(2)}, u32[]{:S(2)}) collective-permute-start(f32[16,1664]{1,0:T(8,128)S(1)} %get-tuple-element.55), channel_id=1, source_target_pairs={{0,64},{1,65},{2,66},{3,67},{4,68},{5,69},{6,70},{7,71},{8,72},{9,... | collective-permute-start | bytes 319496 | tf_op jit(solution)/shard_map/ppermute | solution.py:411
  74.3 2.9 %collective-permute-done.15 = f32[16,1664]{1,0:T(8,128)S(1)} collective-permute-done((f32[16,1664]{1,0:T(8,128)S(1)}, f32[16,1664]{1,0:T(8,128)S(1)}, u32[]{:S(2)}, u32[]{:S(2)}) %collective-permute-start.15) | collective-permute-done | bytes 106528 | tf_op jit(solution)/shard_map/ppermute | solution.py:411
  77.2 1.9 %collective-permute-done.16 = f32[16,1664]{1,0:T(8,128)S(1)} collective-permute-done((f32[16,1664]{1,0:T(8,128)S(1)}, f32[16,1664]{1,0:T(8,128)S(1)}, u32[]{:S(2)}, u32[]{:S(2)}) %collective-permute-start.16) | collective-permute-done | bytes 106528 | tf_op jit(solution)/shard_map/ppermute | solution.py:409
  79.7 1.0 collective-permute-start.18
  80.7 1.1 collective-permute-done.18.refs_4_
  81.8 1.0 shard_map.51.refs_1_
  82.8 1.2 collective-permute-start.19
  84.0 3.6 %collective-permute-done.19.refs_2_ = f32[64,512]{1,0:T(8,128)S(1)} collective-permute-done((f32[64,512]{1,0:T(8,128)S(1)}, f32[64,512]{1,0:T(8,128)S(1)}, u32[]{:S(2)}, u32[]{:S(2)}) %collective-permute-start.19) | collective-permute-done | bytes 131104 | tf_op jit(solution)/shard_map/ppermute | solution.py:418
  87.6 1.2 collective-permute-start.20
  88.8 1.0 collective-permute-done.20.refs_3_
  89.8 1.4 %shard_map.52 = (f32[64,512]{1,0:T(8,128)}, f32[16,32,128]{2,1,0:T(8,128)}) custom-call(s32[8]{0:T(128)S(1)} %stack.53.refs_0_, f32[64,512]{1,0:T(8,128)S(1)} %shard_map.51.refs_1_, f32[64,512]{1,0:T(8,128)S(1)} %collective-permute-done.19.refs_2_, f32[64,512]{1,0:T(8,128)S(1)} %collective-permute-done.20.refs_3_, bf16[1024,512]{1,0:T(8,128)(2,1)S(1)} %copy-done.5, ...), custom_call_target="tpu_custom_call" | custom-call | flops 2000000000 | bytes 6000000 | tf_op jit(solution)/shard_map/pallas_call | solution.py:302
  91.2 5.4 %all-to-all-start = ((f32[16,32,128]{2,1,0:T(8,128)}), f32[16,32,128]{2,1,0:T(8,128)S(1)}, u32[]{:S(2)}, u32[]{:S(2)}) async-start(f32[16,32,128]{2,1,0:T(8,128)} %get-tuple-element.60), calls=%async_computation | async-start | bytes 524288 | tf_op jit(solution)/shard_map/all_to_all | solution.py:423
  96.6 8.8 %all-to-all-done = f32[16,32,128]{2,1,0:T(8,128)S(1)} async-done(((f32[16,32,128]{2,1,0:T(8,128)}), f32[16,32,128]{2,1,0:T(8,128)S(1)}, u32[]{:S(2)}, u32[]{:S(2)}) %all-to-all-start) | async-done | bytes 262176 | tf_op jit(solution)/shard_map/all_to_all | solution.py:423
  105.4 2.0 %collective-permute-start.21 = (f32[8,32,128]{2,1,0:T(8,128)S(1)}, f32[8,32,128]{2,1,0:T(8,128)S(1)}, u32[]{:S(2)}, u32[]{:S(2)}) collective-permute-start(f32[8,32,128]{2,1,0:T(8,128)S(1)} %constant_dynamic-slice_fusion.refs_2_), channel_id=1, source_target_pairs={{0,2},{1,3},{2,0},{3,1},{4,6},{5,7},{6,4},{7,5},{8,10},{9,11},{10,... | collective-permute-start | bytes 393224 | tf_op jit(solution)/shard_map/ppermute | solution.py:440
  107.4 3.8 %collective-permute-done.21.refs_3_ = f32[8,32,128]{2,1,0:T(8,128)S(1)} collective-permute-done((f32[8,32,128]{2,1,0:T(8,128)S(1)}, f32[8,32,128]{2,1,0:T(8,128)S(1)}, u32[]{:S(2)}, u32[]{:S(2)}) %collective-permute-start.21) | collective-permute-done | bytes 131104 | tf_op jit(solution)/shard_map/ppermute | solution.py:440
  111.7 1.2 collective-permute-done.22.refs_4_
  112.9 1.4 %shard_map.53.refs_1_ = f32[64,512]{1,0:T(8,128)S(1)} custom-call(s32[8]{0:T(128)S(1)} %stack.53.refs_0_, s32[16]{0:T(128)S(1)} %copy-done.3, f32[8,32,128]{2,1,0:T(8,128)S(1)} %constant_dynamic-slice_fusion.refs_2_, f32[8,32,128]{2,1,0:T(8,128)S(1)} %collective-permute-done.21.refs_3_, f32[2,8,32,128]{3,2,1,0:T(8,128)S(1)} %collective-permute-done.22.refs_4_, ...), custom_call_target="tpu_custom_call" | custom-call | flops 2000000000 | bytes 6000000 | tf_op jit(solution)/shard_map/pallas_call | solution.py:302
  114.3 1.1 collective-permute-start.23
  115.4 3.7 %collective-permute-done.23.refs_2_ = f32[64,512]{1,0:T(8,128)S(1)} collective-permute-done((f32[64,512]{1,0:T(8,128)S(1)}, f32[64,512]{1,0:T(8,128)S(1)}, u32[]{:S(2)}, u32[]{:S(2)}) %collective-permute-start.23) | collective-permute-done | bytes 131104 | tf_op jit(solution)/shard_map/ppermute | solution.py:418
  119.1 1.2 collective-permute-start.24
  120.3 1.0 collective-permute-done.24.refs_3_
  121.9 11.9 %all_to_all.10.refs_3_ = f32[16,32,128]{2,1,0:T(8,128)S(1)} all-to-all(f32[16,32,128]{2,1,0:T(8,128)S(1)} %get-tuple-element.62), channel_id=1, replica_groups={{1,5,9,13,17,21,25,29,32,36,40,44,48,52,56,60},{2,6,10,14,18,22,26,30,6..., dimensions={0} | all-to-all | bytes 524288 | tf_op jit(solution)/shard_map/all_to_all | solution.py:423
  133.9 1.4 %shard_map.55 = f32[64,512]{1,0:T(8,128)} custom-call(s32[8]{0:T(128)S(1)} %stack.53.refs_0_, f32[1]{0:T(128)} %constant.82.clone.1.refs_1_, f32[64,512]{1,0:T(8,128)S(1)} %get-tuple-element.61.refs_2_, f32[16,32,128]{2,1,0:T(8,128)S(1)} %all_to_all.10.refs_3_), custom_call_target="tpu_custom_call" | custom-call | tf_op jit(solution)/shard_map/pallas_call | solution.py:302
  (53 shorter events, 7.3 us)
Async XLA Ops:
  0.0 7.8 %collective-permute-start = (f32[1024,512]{1,0:T(8,128)}, f32[1024,512]{1,0:T(8,128)}, u32[]{:S(2)}, u32[]{:S(2)}) collective-permute-start(f32[1024,512]{1,0:T(8,128)} %refs_1_.7), channel_id=1, source_target_pairs={{0,1},{1,0},{2,3},{3,2},{4,5},{5,4},{6,7},{7,6},{8,9},{9,8},{10,11... | collective-permute-start | bytes 6291464 | tf_op jit(solution)/shard_map/ppermute | solution.py:345
  2.4 5.2 %copy-start.1 = (f32[1024,512]{1,0:T(8,128)S(1)}, f32[1024,512]{1,0:T(8,128)}, u32[]{:S(2)}) copy-start(f32[1024,512]{1,0:T(8,128)} %refs_1_.7) | copy-start | bytes 6291460
  2.4 9.9 %collective-permute-start.1 = (f32[512,128]{1,0:T(8,128)S(1)}, f32[512,128]{1,0:T(8,128)S(1)}, u32[]{:S(2)}, u32[]{:S(2)}) collective-permute-start(f32[512,128]{1,0:T(8,128)S(1)} %constant_dynamic-slice_fusion.3), channel_id=1, source_target_pairs={{0,2},{1,3},{2,0},{3,1},{4,6},{5,7},{6,4},{7,5},{8,10},{9,11},{10,... | collective-permute-start | bytes 786440 | tf_op jit(solution)/shard_map/ppermute | solution.py:349
  7.3 28.8 %collective-permute-start.11 = (f32[1024,512]{1,0:T(8,128)}, f32[1024,512]{1,0:T(8,128)}, u32[]{:S(2)}, u32[]{:S(2)}) collective-permute-start(f32[1024,512]{1,0:T(8,128)} %slice.11), channel_id=1, source_target_pairs={{0,1},{1,0},{2,3},{3,2},{4,5},{5,4},{6,7},{7,6},{8,9},{9,8},{10,11... | collective-permute-start | bytes 6291464 | tf_op jit(solution)/shard_map/ppermute | solution.py:401
  12.2 3.9 %copy-start.2 = (f32[1,512,512]{2,1,0:T(8,128)S(1)}, f32[1,512,512]{2,1,0:T(8,128)}, u32[]{:S(2)}) copy-start(f32[1,512,512]{2,1,0:T(8,128)} %param.6) | copy-start | bytes 3145732
  14.8 9.0 %collective-permute-start.2 = (f32[4,32,896]{2,1,0:T(8,128)S(1)}, f32[4,32,896]{2,1,0:T(8,128)S(1)}, u32[]{:S(2)}, u32[]{:S(2)}) collective-permute-start(f32[4,32,896]{2,1,0:T(8,128)S(1)} %get-tuple-element.36), channel_id=1, source_target_pairs={{0,16},{1,5},{2,18},{3,7},{4,20},{5,9},{6,22},{7,11},{8,24},{9,13}... | collective-permute-start | bytes 1376264 | tf_op jit(solution)/shard_map/ppermute | solution.py:325
  16.2 18.7 %collective-permute-start.5 = (f32[512,384]{1,0:T(8,128)S(1)}, f32[512,384]{1,0:T(8,128)S(1)}, u32[]{:S(2)}, u32[]{:S(2)}) collective-permute-start(f32[512,384]{1,0:T(8,128)S(1)} %dynamic-slice), channel_id=1, source_target_pairs={{0,2},{1,3},{2,0},{3,1},{4,6},{5,7},{6,4},{7,5},{8,10},{9,11},{10,... | collective-permute-start | bytes 2359304 | tf_op jit(solution)/shard_map/ppermute | solution.py:349
  16.2 20.0 %collective-permute-start.10 = (f32[512,512]{1,0:T(8,128)S(1)}, f32[512,512]{1,0:T(8,128)S(1)}, u32[]{:S(2)}, u32[]{:S(2)}) collective-permute-start(f32[512,512]{1,0:T(8,128)S(1)} %bitcast.33), channel_id=1, source_target_pairs={{0,1},{1,0},{2,3},{3,2},{4,5},{5,4},{6,7},{7,6},{8,9},{9,8},{10,11... | collective-permute-start | bytes 3145736 | tf_op jit(solution)/shard_map/ppermute | solution.py:400
  17.2 10.6 %collective-permute-start.3 = (f32[4,32,896]{2,1,0:T(8,128)S(1)}, f32[4,32,896]{2,1,0:T(8,128)S(1)}, u32[]{:S(2)}, u32[]{:S(2)}) collective-permute-start(f32[4,32,896]{2,1,0:T(8,128)S(1)} %get-tuple-element.37), channel_id=1, source_target_pairs={{0,48},{1,13},{2,50},{3,15},{4,52},{5,1},{6,54},{7,3},{8,56},{9,5}... | collective-permute-start | bytes 1376264 | tf_op jit(solution)/shard_map/ppermute | solution.py:325
  23.8 9.1 %collective-permute-start.4 = (f32[4,32,896]{2,1,0:T(8,128)S(1)}, f32[4,32,896]{2,1,0:T(8,128)S(1)}, u32[]{:S(2)}, u32[]{:S(2)}) collective-permute-start(f32[4,32,896]{2,1,0:T(8,128)S(1)} %get-tuple-element.38), channel_id=1, source_target_pairs={{0,32},{1,9},{2,34},{3,11},{4,36},{5,13},{6,38},{7,15},{8,40},{9,1... | collective-permute-start | bytes 1376264 | tf_op jit(solution)/shard_map/ppermute | solution.py:325
  25.4 10.7 %copy-start = (f32[2048,512]{1,0:T(8,128)S(1)}, f32[2048,512]{1,0:T(8,128)}, u32[]{:S(2)}) copy-start(f32[2048,512]{1,0:T(8,128)} %refs_3_.1) | copy-start | bytes 12582916
  34.9 10.2 %collective-permute-start.6 = (f32[512,384]{1,0:T(8,128)S(1)}, f32[512,384]{1,0:T(8,128)S(1)}, u32[]{:S(2)}, u32[]{:S(2)}) collective-permute-start(f32[512,384]{1,0:T(8,128)S(1)} %collective-permute-done.5), channel_id=1, source_target_pairs={{0,1},{1,0},{2,3},{3,2},{4,5},{5,4},{6,7},{7,6},{8,9},{9,8},{10,11... | collective-permute-start | bytes 2359304 | tf_op jit(solution)/shard_map/ppermute | solution.py:379
  44.1 1.0 copy-start.4
  45.1 2.5 %copy-start.7 = (bf16[1024,512]{1,0:T(8,128)(2,1)}, bf16[1024,512]{1,0:T(8,128)(2,1)S(1)}, u32[]{:S(2)}) copy-start(bf16[1024,512]{1,0:T(8,128)(2,1)S(1)} %get-tuple-element.59.refs_5_) | copy-start | bytes 3145732
  47.6 8.3 %collective-permute-start.9 = (f32[4,32,768]{2,1,0:T(8,128)S(1)}, f32[4,32,768]{2,1,0:T(8,128)S(1)}, u32[]{:S(2)}, u32[]{:S(2)}) collective-permute-start(f32[4,32,768]{2,1,0:T(8,128)S(1)} %get-tuple-element.48), channel_id=1, source_target_pairs={{0,32},{1,9},{2,34},{3,11},{4,36},{5,13},{6,38},{7,15},{8,40},{9,1... | collective-permute-start | bytes 1179656 | tf_op jit(solution)/shard_map/ppermute | solution.py:325
  50.2 8.9 %collective-permute-start.8 = (f32[4,32,768]{2,1,0:T(8,128)S(1)}, f32[4,32,768]{2,1,0:T(8,128)S(1)}, u32[]{:S(2)}, u32[]{:S(2)}) collective-permute-start(f32[4,32,768]{2,1,0:T(8,128)S(1)} %get-tuple-element.47), channel_id=1, source_target_pairs={{0,48},{1,13},{2,50},{3,15},{4,52},{5,1},{6,54},{7,3},{8,56},{9,5}... | collective-permute-start | bytes 1179656 | tf_op jit(solution)/shard_map/ppermute | solution.py:325
  51.3 8.7 %collective-permute-start.7 = (f32[4,32,768]{2,1,0:T(8,128)S(1)}, f32[4,32,768]{2,1,0:T(8,128)S(1)}, u32[]{:S(2)}, u32[]{:S(2)}) collective-permute-start(f32[4,32,768]{2,1,0:T(8,128)S(1)} %get-tuple-element.46), channel_id=1, source_target_pairs={{0,16},{1,5},{2,18},{3,7},{4,20},{5,9},{6,22},{7,11},{8,24},{9,13}... | collective-permute-start | bytes 1179656 | tf_op jit(solution)/shard_map/ppermute | solution.py:325
  60.1 21.7 %copy-start.3 = (s32[16]{0:T(128)S(1)}, s32[16]{0:T(128)}, u32[]{:S(2)}) copy-start(s32[16]{0:T(128)} %refs_1_.9) | copy-start | bytes 196
  61.0 6.4 %collective-permute-start.14 = (f32[32,1664]{1,0:T(8,128)}, f32[32,1664]{1,0:T(8,128)S(1)}, u32[]{:S(2)}, u32[]{:S(2)}) collective-permute-start(f32[32,1664]{1,0:T(8,128)} %get-tuple-element.53), channel_id=1, source_target_pairs={{0,8},{1,33},{2,10},{3,35},{4,12},{5,37},{6,14},{7,39},{8,0},{9,41... | collective-permute-start | bytes 638984 | tf_op jit(solution)/shard_map/ppermute | solution.py:325
  63.7 6.0 %collective-permute-start.13 = (f32[32,1664]{1,0:T(8,128)}, f32[32,1664]{1,0:T(8,128)S(1)}, u32[]{:S(2)}, u32[]{:S(2)}) collective-permute-start(f32[32,1664]{1,0:T(8,128)} %get-tuple-element.52), channel_id=1, source_target_pairs={{0,12},{1,49},{2,14},{3,51},{4,0},{5,53},{6,2},{7,55},{8,4},{9,57}... | collective-permute-start | bytes 638984 | tf_op jit(solution)/shard_map/ppermute | solution.py:325
  64.6 5.9 %collective-permute-start.12 = (f32[32,1664]{1,0:T(8,128)S(1)}, f32[32,1664]{1,0:T(8,128)S(1)}, u32[]{:S(2)}, u32[]{:S(2)}) collective-permute-start(f32[32,1664]{1,0:T(8,128)S(1)} %get-tuple-element.51), channel_id=1, source_target_pairs={{0,4},{1,17},{2,6},{3,19},{4,8},{5,21},{6,10},{7,23},{8,12},{9,25}... | collective-permute-start | bytes 638984 | tf_op jit(solution)/shard_map/ppermute | solution.py:325
  70.5 6.6 %collective-permute-start.15 = (f32[16,1664]{1,0:T(8,128)S(1)}, f32[16,1664]{1,0:T(8,128)S(1)}, u32[]{:S(2)}, u32[]{:S(2)}) collective-permute-start(f32[16,1664]{1,0:T(8,128)S(1)} %get-tuple-element.55), channel_id=1, source_target_pairs={{0,64},{1,65},{2,66},{3,67},{4,68},{5,69},{6,70},{7,71},{8,72},{9,... | collective-permute-start | bytes 319496 | tf_op jit(solution)/shard_map/ppermute | solution.py:411
  73.9 5.2 %collective-permute-start.16 = (f32[16,1664]{1,0:T(8,128)S(1)}, f32[16,1664]{1,0:T(8,128)S(1)}, u32[]{:S(2)}, u32[]{:S(2)}) collective-permute-start(f32[16,1664]{1,0:T(8,128)S(1)} %get-tuple-element.54), channel_id=1, source_target_pairs={{0,2},{1,3},{2,0},{3,1},{4,6},{5,7},{6,4},{7,5},{8,10},{9,11},{10,... | collective-permute-start | bytes 319496 | tf_op jit(solution)/shard_map/ppermute | solution.py:409
  74.0 5.7 %collective-permute-start.17 = (f32[16,1664]{1,0:T(8,128)S(1)}, f32[16,1664]{1,0:T(8,128)S(1)}, u32[]{:S(2)}, u32[]{:S(2)}) collective-permute-start(f32[16,1664]{1,0:T(8,128)S(1)} %get-tuple-element.55), channel_id=1, source_target_pairs={{0,66},{1,67},{2,64},{3,65},{4,70},{5,71},{6,68},{7,69},{8,74},{9,... | collective-permute-start | bytes 319496 | tf_op jit(solution)/shard_map/ppermute | solution.py:410
  79.7 2.0 %collective-permute-start.18 = (f32[2,16,1664]{2,1,0:T(8,128)S(1)}, f32[2,16,1664]{2,1,0:T(8,128)S(1)}, u32[]{:S(2)}, u32[]{:S(2)}) collective-permute-start(f32[2,16,1664]{2,1,0:T(8,128)S(1)} %pad_maximum_fusion.5), channel_id=1, source_target_pairs={{0,1},{1,0},{2,3},{3,2},{4,5},{5,4},{6,7},{7,6},{8,9},{9,8},{10,11... | collective-permute-start | bytes 638984 | tf_op jit(solution)/shard_map/ppermute | solution.py:415
  81.8 8.0 %copy-start.5 = (bf16[1024,512]{1,0:T(8,128)(2,1)S(1)}, bf16[1024,512]{1,0:T(8,128)(2,1)}, u32[]{:S(2)}) copy-start(bf16[1024,512]{1,0:T(8,128)(2,1)} %copy-done.4) | copy-start | bytes 3145732
  81.8 8.0 %copy-start.8 = (bf16[1024,512]{1,0:T(8,128)(2,1)S(1)}, bf16[1024,512]{1,0:T(8,128)(2,1)}, u32[]{:S(2)}) copy-start(bf16[1024,512]{1,0:T(8,128)(2,1)} %copy-done.7) | copy-start | bytes 3145732
  82.8 4.8 %collective-permute-start.19 = (f32[64,512]{1,0:T(8,128)S(1)}, f32[64,512]{1,0:T(8,128)S(1)}, u32[]{:S(2)}, u32[]{:S(2)}) collective-permute-start(f32[64,512]{1,0:T(8,128)S(1)} %shard_map.51.refs_1_), channel_id=1, source_target_pairs={{0,2},{1,3},{2,0},{3,1},{4,6},{5,7},{6,4},{7,5},{8,10},{9,11},{10,... | collective-permute-start | bytes 393224 | tf_op jit(solution)/shard_map/ppermute | solution.py:418
  87.6 2.2 %collective-permute-start.20 = (f32[64,512]{1,0:T(8,128)S(1)}, f32[64,512]{1,0:T(8,128)S(1)}, u32[]{:S(2)}, u32[]{:S(2)}) collective-permute-start(f32[64,512]{1,0:T(8,128)S(1)} %collective-permute-done.19.refs_2_), channel_id=1, source_target_pairs={{0,1},{1,0},{2,3},{3,2},{4,5},{5,4},{6,7},{7,6},{8,9},{9,8},{10,11... | collective-permute-start | bytes 393224 | tf_op jit(solution)/shard_map/ppermute | solution.py:419
  91.2 14.2 %all-to-all-start = ((f32[16,32,128]{2,1,0:T(8,128)}), f32[16,32,128]{2,1,0:T(8,128)S(1)}, u32[]{:S(2)}, u32[]{:S(2)}) async-start(f32[16,32,128]{2,1,0:T(8,128)} %get-tuple-element.60), calls=%async_computation | async-start | bytes 524288 | tf_op jit(solution)/shard_map/all_to_all | solution.py:423
  105.4 5.8 %collective-permute-start.21 = (f32[8,32,128]{2,1,0:T(8,128)S(1)}, f32[8,32,128]{2,1,0:T(8,128)S(1)}, u32[]{:S(2)}, u32[]{:S(2)}) collective-permute-start(f32[8,32,128]{2,1,0:T(8,128)S(1)} %constant_dynamic-slice_fusion.refs_2_), channel_id=1, source_target_pairs={{0,2},{1,3},{2,0},{3,1},{4,6},{5,7},{6,4},{7,5},{8,10},{9,11},{10,... | collective-permute-start | bytes 393224 | tf_op jit(solution)/shard_map/ppermute | solution.py:440
  111.2 10.1 %copy-start.6 = (bf16[1024,512]{1,0:T(8,128)(2,1)S(1)}, bf16[1024,512]{1,0:T(8,128)(2,1)}, u32[]{:S(2)}) copy-start(bf16[1024,512]{1,0:T(8,128)(2,1)} %copy-done.4) | copy-start | bytes 3145732
  111.2 10.1 %copy-start.9 = (bf16[1024,512]{1,0:T(8,128)(2,1)S(1)}, bf16[1024,512]{1,0:T(8,128)(2,1)}, u32[]{:S(2)}) copy-start(bf16[1024,512]{1,0:T(8,128)(2,1)} %copy-done.7) | copy-start | bytes 3145732
  111.2 1.6 %collective-permute-start.22 = (f32[2,8,32,128]{3,2,1,0:T(8,128)S(1)}, f32[2,8,32,128]{3,2,1,0:T(8,128)S(1)}, u32[]{:S(2)}, u32[]{:S(2)}) collective-permute-start(f32[2,8,32,128]{3,2,1,0:T(8,128)S(1)} %pad_maximum_fusion), channel_id=1, source_target_pairs={{0,1},{1,0},{2,3},{3,2},{4,5},{5,4},{6,7},{7,6},{8,9},{9,8},{10,11... | collective-permute-start | bytes 786440 | tf_op jit(solution)/shard_map/ppermute | solution.py:415
  114.3 4.8 %collective-permute-start.23 = (f32[64,512]{1,0:T(8,128)S(1)}, f32[64,512]{1,0:T(8,128)S(1)}, u32[]{:S(2)}, u32[]{:S(2)}) collective-permute-start(f32[64,512]{1,0:T(8,128)S(1)} %shard_map.53.refs_1_), channel_id=1, source_target_pairs={{0,2},{1,3},{2,0},{3,1},{4,6},{5,7},{6,4},{7,5},{8,10},{9,11},{10,... | collective-permute-start | bytes 393224 | tf_op jit(solution)/shard_map/ppermute | solution.py:418
  119.1 2.2 %collective-permute-start.24 = (f32[64,512]{1,0:T(8,128)S(1)}, f32[64,512]{1,0:T(8,128)S(1)}, u32[]{:S(2)}, u32[]{:S(2)}) collective-permute-start(f32[64,512]{1,0:T(8,128)S(1)} %collective-permute-done.23.refs_2_), channel_id=1, source_target_pairs={{0,1},{1,0},{2,3},{3,2},{4,5},{5,4},{6,7},{7,6},{8,9},{9,8},{10,11... | collective-permute-start | bytes 393224 | tf_op jit(solution)/shard_map/ppermute | solution.py:419
